TPU v7x, 32 devices: a whole 2x2x4 slice. The times are simulated.
32 devices in a mesh: lon: 2 (over x), lat: 4 (over y, core), lev: 4 (over z).
Axes of the slice: x: 2, y: 2, z: 4, core: 2. Of those that a mesh axis runs over, the one named last changes fastest.
Arguments:
- adjoint_field: float32 [12, 12, 128, 256], P(None, 'lev', 'lat', 'lon'), may hold values from -6 to 6
- east_courant: float32 [12, 128, 256], P('lev', 'lat', 'lon'), may hold values from -0.2 to 0.2
- north_courant: float32 [12, 128, 256], P('lev', 'lat', 'lon'), may hold values from -0.2 to 0.2
- pole_courant: float32 [12, 256], P('lev', 'lon'), may hold values from -0.2 to 0.2
- mix_fraction: float32 [12, 128, 256], P('lev', 'lat', 'lon'), may hold values from 0.05 to 0.6
- detrain_share: float32 [12, 128, 256], P('lev', 'lat', 'lon'), may hold values from 0.1 to 3
- sounding_owner: int32 [2, 2048, 1], P(None, ('lon', 'lat')), may hold values from 0 to 7; in each aligned block of 256 rows (0 to 255, 256 to 511, ..., all dimensions but the last counted through in order) at most 64 rows name the same one
- sounding_cell: int32 [2, 2048], P(None, ('lon', 'lat')), may hold values from 0 to 4095
- sounding_count: int32 [2, 8], P(None, ('lon', 'lat')), may hold values from 1 to 256, 1280 in all within a row
- sounding_forcing: float32 [2, 12, 2048], P(None, 'lev', ('lon', 'lat')), may hold values from -6 to 6
Outputs:
- earlier_adjoint: float32 [12, 12, 128, 256], P(None, 'lev', 'lat', 'lon')
Inputs may be any that keep to these rules, and one draw needn't show every extreme that they name: `sounding_owner`: in each aligned block of 256 slots of one step (the slots of one device) no owner is named more than 64 times, a bound that some block reaches. `sounding_count`: each step's counts sum to 1280; at each step some device has exactly 256.
All inputs are finite; a program needn't handle non-finite values.
Results may differ from a plain program's by a relative error of at most 0.0001.
Values sent between devices are 32-bit elements; how exact they have to be, the bound alone decides.
No kernel may reach another device: no remote copies, remote signals or barrier semaphores. Data moves between devices by JAX's collectives and lax.ppermute only.
A program may use at most 128 MiB of HBM per device.

v0:
```python
import jax
import jax.numpy as jnp
from jax import lax
from jax.sharding import PartitionSpec as P


def from_behind(value, axis, steps):
    count = lax.axis_size(axis)
    pairs = [(source, (source + steps) % count) for source in range(count)]
    return lax.ppermute(value, axis, pairs)


def from_behind_2(block, axis, distance):
    devices = range(lax.axis_size(axis))
    route = [(i - distance, i) for i in devices if i - distance in devices]
    return lax.ppermute(block, axis, route)


def extended(x, sides, width, wrap):
    for axis, dim in sides:
        size, length = (lax.axis_size(axis), x.shape[dim])
        up = [(i, (i + 1) % size) for i in range(size if wrap else size - 1)]
        down = [(j, i) for i, j in up]
        last = lax.slice_in_dim(x, length - width, length, axis=dim)
        initial = lax.slice_in_dim(x, 0, width, axis=dim)
        before = lax.ppermute(last, axis, up)
        after = lax.ppermute(initial, axis, down)
        x = jnp.concatenate([before, x, after], axis=dim)
    return x


def mix_sum(partial_sum):
    return lax.psum(partial_sum, "lev")


def on_device(
    adjoint_field,
    east_courant,
    north_courant,
    pole_courant,
    mix_fraction,
    detrain_share,
    sounding_owner,
    sounding_cell,
    sounding_count,
    sounding_forcing,
):
    lon_count = lax.axis_size("lon")
    lat_count = lax.axis_size("lat")
    lat_place = lax.axis_index("lat")
    owner_self = lax.axis_index("lon") * lat_count + lat_place
    tracers, lev_dev, lat_rows, lon_cols = adjoint_field.shape
    step_count = sounding_forcing.shape[0]
    slot_count = sounding_forcing.shape[2]
    grid_cells = lat_rows * lon_cols
    live_slots = jnp.arange(slot_count, dtype=jnp.int32)[None, :] < sounding_count
    values = jnp.where(live_slots[:, None, :], sounding_forcing, 0.0)
    owner_ids = sounding_owner[:, :, 0]
    step_ids = jnp.arange(step_count, dtype=jnp.int32)[:, None]
    index_pair = jnp.stack([owner_ids, sounding_cell], axis=1)
    all_values, all_pairs = (
        lax.all_gather(values, ("lon", "lat"), axis=2, tiled=True),
        lax.all_gather(index_pair, ("lon", "lat"), axis=2, tiled=True),
    )
    kept_values = jnp.where((all_pairs[:, 0, :] == owner_self)[:, None, :], all_values, 0.0)
    target_cells = all_pairs[:, 1, :]
    forcing_grid = (
        jnp.zeros((step_count, lev_dev, grid_cells), jnp.float32)
        .at[step_ids, :, target_cells]
        .add(jnp.swapaxes(kept_values, 1, 2))
    )
    forcing_grid = forcing_grid.reshape(step_count, lev_dev, lat_rows, lon_cols)
    west_column = from_behind(east_courant[:, :, -1:], "lon", 1)
    west_wind = jnp.concatenate([west_column, east_courant[:, :, :-1]], axis=2)
    south_row = from_behind_2(north_courant[:, -1:, :], "lat", 1)
    south_wind = jnp.concatenate([south_row, north_courant[:, :-1, :]], axis=1)
    pole_pair = jnp.stack([north_courant[:, -1, :], pole_courant], axis=0)
    partner_winds = from_behind(pole_pair, "lon", lon_count // 2)
    row_index = jnp.arange(lat_rows, dtype=jnp.int32)[None, :, None]
    at_top = jnp.logical_and(lat_place == lat_count - 1, row_index == lat_rows - 1)
    at_bottom = jnp.logical_and(lat_place == 0, row_index == 0)
    upwind_east = jnp.maximum(east_courant, 0.0)
    upwind_west = -jnp.minimum(west_wind, 0.0)
    upwind_north = jnp.maximum(north_courant, 0.0) + jnp.where(
        at_top, -jnp.minimum(partner_winds[0], 0.0)[:, None, :], 0.0
    )
    upwind_south = jnp.where(
        at_bottom,
        (jnp.maximum(pole_courant, 0.0) - jnp.minimum(partner_winds[1], 0.0))[:, None, :],
        -jnp.minimum(south_wind, 0.0),
    )
    total_detrain = lax.psum(jnp.sum(detrain_share, axis=0), "lev")
    adjoint = adjoint_field
    for position in range(step_count):
        step_now = step_count - 1 - position
        adjoint = adjoint + forcing_grid[step_now][None]
        partial_sum = jnp.sum(detrain_share[None] * adjoint, axis=1)
        column_sum = mix_sum(partial_sum)
        adjoint = (1.0 - mix_fraction)[None] * adjoint + mix_fraction[None] * (
            column_sum / total_detrain
        )[:, None]
        across = extended(adjoint, (("lon", 3),), 1, True)
        east_side = across[:, :, :, 2:]
        west_side = across[:, :, :, :-2]
        upright = extended(adjoint, (("lat", 2),), 1, False)
        north_side = upright[:, :, 2:, :]
        south_side = upright[:, :, :-2, :]
        edge_row = jnp.where(lat_place == 0, adjoint[:, :, :1, :], adjoint[:, :, -1:, :])
        partner_row = from_behind(edge_row, "lon", lon_count // 2)
        north_side = jnp.where(at_top, partner_row, north_side)
        south_side = jnp.where(at_bottom, partner_row, south_side)
        adjoint = (
            adjoint
            + upwind_east * (east_side - adjoint)
            + upwind_west * (west_side - adjoint)
            + upwind_north * (north_side - adjoint)
            + upwind_south * (south_side - adjoint)
        )
    return adjoint


def solution(mesh):
    return jax.shard_map(
        on_device,
        mesh=mesh,
        in_specs=(
            P(None, "lev", "lat", "lon"),
            P("lev", "lat", "lon"),
            P("lev", "lat", "lon"),
            P("lev", "lon"),
            P("lev", "lat", "lon"),
            P("lev", "lat", "lon"),
            P(None, ("lon", "lat"), None),
            P(None, ("lon", "lat")),
            P(None, ("lon", "lat")),
            P(None, "lev", ("lon", "lat")),
        ),
        out_specs=P(None, "lev", "lat", "lon"),
        check_vma=False,
    )
```

profile of v0, /device:TPU:0, one launch (start us, length us, event | category | flops | bytes accessed | tf_op | source)
XLA Modules:
  0.0 172.1 jit_solution(16442646671950266922)
XLA Ops:
  6.5 0.7 copy.54
  7.2 0.7 pad_add_fusion.1
  7.9 10.3 %all_gather.6 = s32[2,2,2048]{2,0,1:T(2,128)S(1)} all-gather(s32[2,2,256]{2,0,1:T(2,128)S(1)} %pad_add_fusion.1), channel_id=1, replica_groups=mesh['lon'=2,'lat'=4,'lev'=4] {'lon','lat'}, dimensions={2}, use_global_device_ids=true | all-gather | bytes 36864 | tf_op jit(solution)/shard_map/all_gather | solution.py:63
  18.2 0.8 multiply_reduce_fusion.1
  19.0 0.8 and_reduce_fusion
  19.8 0.7 iota_compare_fusion
  20.6 0.7 broadcast_select_fusion.2
  21.3 8.9 %all_gather.7 = f32[2,3,2048]{2,0,1:T(2,128)S(1)} all-gather(f32[2,3,256]{2,0,1:T(2,128)S(1)} %broadcast_select_fusion.2), channel_id=1, replica_groups=mesh['lon'=2,'lat'=4,'lev'=4] {'lon','lat'}, dimensions={2}, use_global_device_ids=true | all-gather | bytes 55296 | tf_op jit(solution)/shard_map/all_gather | solution.py:62
  30.2 0.6 copy.38
  30.8 24.5 %scatter_custom_fusion = f32[3,8192]{0,1:T(8,128)} fusion(s32[4096]{0:T(1024)S(1)} %bitcast.44, f32[4096,3]{1,0:T(8,128)S(1)} %bitcast.39, f32[]{:T(128)} %constant.12.clone.1), kind=kCustom, calls=%fused_computation.1 | custom fusion | flops 12288 | bytes 98308
  55.3 3.8 %fusion.43 = (f32[1,3,4096]{1,2,0:T(8,128)}, f32[1,3,4096]{1,2,0:T(8,128)S(1)}) fusion(f32[2,3,4096]{1,2,0:T(8,128)} %bitcast.36), kind=kLoop, calls=%fused_computation.81 | loop fusion | bytes 196608 | tf_op jit(solution)/shard_map/slice | solution.py:96
  59.2 2.3 %copy.24 = f32[3,32,128]{2,1,0:T(8,128)S(1)} copy(f32[3,32,128]{0,2,1:T(8,128)} %bitcast.38) | data formatting | bytes 98304 | tf_op jit(solution)/shard_map/add | solution.py:96
  61.5 1.1 fusion.34
  62.7 2.3 %collective-permute-start.6 = (f32[3,1,128]{2,0,1:T(4,128)S(1)}, f32[3,1,128]{2,0,1:T(4,128)S(1)}, u32[]{:S(2)}, u32[]{:S(2)}) collective-permute-start(f32[3,1,128]{2,0,1:T(4,128)S(1)} %copy.55), channel_id=1, source_target_pairs={{0,4},{4,8},{8,12},{1,5},{5,9},{9,13},{2,6},{6,10},{10,14},{3,7},{... | collective-permute-start | bytes 4616 | tf_op jit(solution)/shard_map/ppermute | solution.py:16
  65.0 0.6 collective-permute-start.3
  65.6 1.5 collective-permute-start.1
  67.2 19.0 %psum.22 = f32[32,128]{1,0:T(8,128)S(1)} all-reduce(f32[32,128]{1,0:T(8,128)S(1)} %reduce_sum.28), channel_id=1, replica_groups=mesh['lon'=2,'lat'=4,'lev'=4] {'lev'}, use_global_device_ids=true, to_apply=%region_4.5 | all-reduce | flops 4096 | bytes 32768 | tf_op jit(solution)/shard_map/psum | solution.py:92
  86.2 0.6 copy.32
  87.1 11.4 %all-reduce.3.cloned.1.call-done = f32[12,32,128]{2,0,1:T(8,128)} async-done(((f32[12,32,128]{2,0,1:T(8,128)}), f32[12,32,128]{2,0,1:T(8,128)}) %all-reduce.3.cloned.1.call-update) | async-done | bytes 196624 | tf_op jit(solution)/shard_map/psum | solution.py:33
  98.5 1.0 broadcast_divide_fusion.1
  99.4 0.5 fusion.33
  100.2 1.5 collective-permute-start.4
  101.7 1.3 collective-permute-start.5
  103.0 3.0 %collective-permute-start.7 = (f32[12,3,1,128]{3,0,2,1:T(8,128)S(1)}, f32[12,3,1,128]{3,0,2,1:T(8,128)S(1)}, u32[]{:S(2)}, u32[]{:S(2)}) collective-permute-start(f32[12,3,1,128]{3,0,2,1:T(8,128)S(1)} %get-tuple-element.17), channel_id=1, source_target_pairs={{0,4},{4,8},{8,12},{1,5},{5,9},{9,13},{2,6},{6,10},{10,14},{3,7},{... | collective-permute-start | bytes 55304 | tf_op jit(solution)/shard_map/ppermute | solution.py:26
  106.1 0.3 copy.26
  106.4 0.6 collective-permute-start
  107.3 1.5 collective-permute-start.2
  108.9 1.3 collective-permute-done
  110.3 0.4 copy.27
  110.7 0.5 collective-permute-done.2
  111.2 0.4 copy.29
  111.7 0.6 copy-done.5
  112.3 0.6 copy-done.7
  112.9 2.3 %multiply_reduce_fusion = (f32[12,32,128]{2,0,1:T(8,128)}, f32[12,3,32,128]{3,0,2,1:T(8,128)S(1)}) fusion(f32[3,32,128]{2,1,0:T(8,128)S(1)} %copy-done.1, f32[3,32,128]{2,1,0:T(8,128)S(1)} %copy.32, f32[12,3,32,128]{3,0,2,1:T(8,128)S(1)} %fusion.33, f32[12,3,1,128]{3,0,2,1:T(8,128)} %copy-done.7, pred[32]{0:T(512)(128)(4,1)} %copy-done.8, ...), kind=kLoop, calls=%fused_computation.46 | loop fusion | flops 3047424 | bytes 1735744 | tf_op jit(solution)/shard_map/reduce_sum | solution.py:97
  115.2 35.2 %all-reduce.5.cloned.1.call-done = f32[12,32,128]{2,0,1:T(8,128)} async-done(((f32[12,32,128]{2,0,1:T(8,128)}), f32[12,32,128]{2,0,1:T(8,128)}) %all-reduce.5.cloned.1.call-update) | async-done | bytes 196624 | tf_op jit(solution)/shard_map/psum | solution.py:33
  150.4 1.0 broadcast_divide_fusion
  151.5 1.5 collective-permute-start.10
  153.1 1.3 collective-permute-start.11
  154.4 3.2 %collective-permute-start.12 = (f32[12,3,1,128]{3,0,2,1:T(8,128)S(1)}, f32[12,3,1,128]{3,0,2,1:T(8,128)S(1)}, u32[]{:S(2)}, u32[]{:S(2)}) collective-permute-start(f32[12,3,1,128]{3,0,2,1:T(8,128)S(1)} %get-tuple-element.10), channel_id=1, source_target_pairs={{0,4},{4,8},{8,12},{1,5},{5,9},{9,13},{2,6},{6,10},{10,14},{3,7},{... | collective-permute-start | bytes 55304 | tf_op jit(solution)/shard_map/ppermute | solution.py:26
  157.9 0.3 copy.33
  158.2 0.6 collective-permute-start.8
  159.2 1.5 collective-permute-start.9
  160.7 1.4 collective-permute-done.8
  162.1 0.4 copy.34
  162.5 0.5 collective-permute-done.9
  163.0 0.4 copy.36
  163.5 0.8 fusion.5
  164.2 1.0 copy.37
  (64 shorter events, 2.0 us)
Async XLA Ops:
  6.5 91.9 %all-reduce.3.cloned.1.call-start = ((), (), s32[]{:S(2)}) async-start(), calls=%async_computation | async-start | bytes 524288 | tf_op jit(solution)/shard_map/psum | solution.py:33
  59.1 2.3 %copy-start = (f32[12,3,32,128]{3,2,1,0:T(8,128)S(1)}, f32[12,3,32,128]{3,2,1,0:T(8,128)}, u32[]{:S(2)}) copy-start(f32[12,3,32,128]{3,2,1,0:T(8,128)} %param.10) | copy-start | bytes 1769476
  59.1 2.3 %copy-start.1 = (f32[3,32,128]{2,1,0:T(8,128)S(1)}, f32[3,32,128]{2,1,0:T(8,128)}, u32[]{:S(2)}) copy-start(f32[3,32,128]{2,1,0:T(8,128)} %param.15) | copy-start | bytes 147460
  59.1 3.5 %copy-start.4 = (f32[3,32,128]{2,1,0:T(8,128)S(1)}, f32[3,32,128]{2,1,0:T(8,128)}, u32[]{:S(2)}) copy-start(f32[3,32,128]{2,1,0:T(8,128)} %param.12) | copy-start | bytes 147460
  59.1 5.8 %copy-start.12 = (f32[3,128]{1,0:T(4,128)S(1)}, f32[3,128]{1,0:T(4,128)}, u32[]{:S(2)}) copy-start(f32[3,128]{1,0:T(4,128)} %param.13) | copy-start | bytes 4612
  59.2 6.4 %copy-start.2 = (f32[3,32,128]{2,1,0:T(8,128)S(1)}, f32[3,32,128]{2,1,0:T(8,128)}, u32[]{:S(2)}) copy-start(f32[3,32,128]{2,1,0:T(8,128)} %param.11) | copy-start | bytes 147460
  59.2 8.0 %copy-start.3 = (f32[3,32,128]{2,1,0:T(8,128)S(1)}, f32[3,32,128]{2,1,0:T(8,128)}, u32[]{:S(2)}) copy-start(f32[3,32,128]{2,1,0:T(8,128)} %param.14) | copy-start | bytes 147460
  62.6 87.8 %all-reduce.5.cloned.1.call-start = ((), (), s32[]{:S(2)}) async-start(), calls=%async_computation.1 | async-start | bytes 524288 | tf_op jit(solution)/shard_map/psum | solution.py:33
  62.7 24.3 %collective-permute-start.6 = (f32[3,1,128]{2,0,1:T(4,128)S(1)}, f32[3,1,128]{2,0,1:T(4,128)S(1)}, u32[]{:S(2)}, u32[]{:S(2)}) collective-permute-start(f32[3,1,128]{2,0,1:T(4,128)S(1)} %copy.55), channel_id=1, source_target_pairs={{0,4},{4,8},{8,12},{1,5},{5,9},{9,13},{2,6},{6,10},{10,14},{3,7},{... | collective-permute-start | bytes 4616 | tf_op jit(solution)/shard_map/ppermute | solution.py:16
  65.0 22.0 %collective-permute-start.3 = (f32[2,3,128]{2,1,0:T(4,128)S(1)}, f32[2,3,128]{2,1,0:T(4,128)S(1)}, u32[]{:S(2)}, u32[]{:S(2)}) collective-permute-start(f32[2,3,128]{2,1,0:T(4,128)S(1)} %pad_maximum_fusion.8), channel_id=1, source_target_pairs={{0,16},{16,0},{1,17},{17,1},{2,18},{18,2},{3,19},{19,3},{4,20},{20... | collective-permute-start | bytes 9224 | tf_op jit(solution)/shard_map/ppermute | solution.py:10
  65.6 21.2 %collective-permute-start.1 = (f32[3,32,1]{2,1,0:T(8,128)S(1)}, f32[3,32,1]{2,1,0:T(8,128)S(1)}, u32[]{:S(2)}, u32[]{:S(2)}) collective-permute-start(f32[3,32,1]{2,1,0:T(8,128)S(1)} %slice.98), channel_id=1, source_target_pairs={{0,16},{16,0},{1,17},{17,1},{2,18},{18,2},{3,19},{19,3},{4,20},{20... | collective-permute-start | bytes 1160 | tf_op jit(solution)/shard_map/ppermute | solution.py:10
  67.2 32.7 %copy-start.10 = (pred[32]{0:T(512)(128)(4,1)}, pred[32]{0:T(512)(128)(4,1)S(1)}, u32[]{:S(2)}) copy-start(pred[32]{0:T(512)(128)(4,1)S(1)} %get-tuple-element.22) | copy-start | bytes 100
  67.2 41.6 %copy-start.8 = (pred[32]{0:T(512)(128)(4,1)}, pred[32]{0:T(512)(128)(4,1)S(1)}, u32[]{:S(2)}) copy-start(pred[32]{0:T(512)(128)(4,1)S(1)} %get-tuple-element.21) | copy-start | bytes 100
  100.2 11.4 %collective-permute-start.4 = (f32[12,3,1,128]{3,0,2,1:T(8,128)S(1)}, f32[12,3,1,128]{3,0,2,1:T(8,128)S(1)}, u32[]{:S(2)}, u32[]{:S(2)}) collective-permute-start(f32[12,3,1,128]{3,0,2,1:T(8,128)S(1)} %get-tuple-element.16), channel_id=1, source_target_pairs={{0,16},{16,0},{1,17},{17,1},{2,18},{18,2},{3,19},{19,3},{4,20},{20... | collective-permute-start | bytes 55304 | tf_op jit(solution)/shard_map/ppermute | solution.py:10
  101.7 9.9 %collective-permute-start.5 = (f32[12,3,1,128]{3,0,2,1:T(8,128)S(1)}, f32[12,3,1,128]{3,0,2,1:T(8,128)S(1)}, u32[]{:S(2)}, u32[]{:S(2)}) collective-permute-start(f32[12,3,1,128]{3,0,2,1:T(8,128)S(1)} %get-tuple-element.18), channel_id=1, source_target_pairs={{4,0},{8,4},{12,8},{5,1},{9,5},{13,9},{6,2},{10,6},{14,10},{7,3},{... | collective-permute-start | bytes 55304 | tf_op jit(solution)/shard_map/ppermute | solution.py:27
  103.0 8.6 %collective-permute-start.7 = (f32[12,3,1,128]{3,0,2,1:T(8,128)S(1)}, f32[12,3,1,128]{3,0,2,1:T(8,128)S(1)}, u32[]{:S(2)}, u32[]{:S(2)}) collective-permute-start(f32[12,3,1,128]{3,0,2,1:T(8,128)S(1)} %get-tuple-element.17), channel_id=1, source_target_pairs={{0,4},{4,8},{8,12},{1,5},{5,9},{9,13},{2,6},{6,10},{10,14},{3,7},{... | collective-permute-start | bytes 55304 | tf_op jit(solution)/shard_map/ppermute | solution.py:26
  106.4 3.9 %collective-permute-start = (f32[12,3,32,1]{2,3,1,0:T(1,128)S(1)}, f32[12,3,32,1]{2,3,1,0:T(1,128)S(1)}, u32[]{:S(2)}, u32[]{:S(2)}) collective-permute-start(f32[12,3,32,1]{2,3,1,0:T(1,128)S(1)} %copy.26), channel_id=1, source_target_pairs={{16,0},{0,16},{17,1},{1,17},{18,2},{2,18},{19,3},{3,19},{20,4},{4,... | collective-permute-start | bytes 13832 | tf_op jit(solution)/shard_map/ppermute | solution.py:27
  107.3 3.8 %collective-permute-start.2 = (f32[12,3,32,1]{2,3,1,0:T(1,128)S(1)}, f32[12,3,32,1]{2,3,1,0:T(1,128)S(1)}, u32[]{:S(2)}, u32[]{:S(2)}) collective-permute-start(f32[12,3,32,1]{2,3,1,0:T(1,128)S(1)} %copy.28), channel_id=1, source_target_pairs={{0,16},{16,0},{1,17},{17,1},{2,18},{18,2},{3,19},{19,3},{4,20},{20... | collective-permute-start | bytes 13832 | tf_op jit(solution)/shard_map/ppermute | solution.py:26
  111.6 0.6 copy-start.5
  111.6 0.6 copy-start.6
  112.3 0.6 copy-start.7
  151.5 11.9 %collective-permute-start.10 = (f32[12,3,1,128]{3,0,2,1:T(8,128)S(1)}, f32[12,3,1,128]{3,0,2,1:T(8,128)S(1)}, u32[]{:S(2)}, u32[]{:S(2)}) collective-permute-start(f32[12,3,1,128]{3,0,2,1:T(8,128)S(1)} %get-tuple-element.9), channel_id=1, source_target_pairs={{0,16},{16,0},{1,17},{17,1},{2,18},{18,2},{3,19},{19,3},{4,20},{20... | collective-permute-start | bytes 55304 | tf_op jit(solution)/shard_map/ppermute | solution.py:10
  153.1 10.4 %collective-permute-start.11 = (f32[12,3,1,128]{3,0,2,1:T(8,128)S(1)}, f32[12,3,1,128]{3,0,2,1:T(8,128)S(1)}, u32[]{:S(2)}, u32[]{:S(2)}) collective-permute-start(f32[12,3,1,128]{3,0,2,1:T(8,128)S(1)} %get-tuple-element.11), channel_id=1, source_target_pairs={{4,0},{8,4},{12,8},{5,1},{9,5},{13,9},{6,2},{10,6},{14,10},{7,3},{... | collective-permute-start | bytes 55304 | tf_op jit(solution)/shard_map/ppermute | solution.py:27
  154.4 9.1 %collective-permute-start.12 = (f32[12,3,1,128]{3,0,2,1:T(8,128)S(1)}, f32[12,3,1,128]{3,0,2,1:T(8,128)S(1)}, u32[]{:S(2)}, u32[]{:S(2)}) collective-permute-start(f32[12,3,1,128]{3,0,2,1:T(8,128)S(1)} %get-tuple-element.10), channel_id=1, source_target_pairs={{0,4},{4,8},{8,12},{1,5},{5,9},{9,13},{2,6},{6,10},{10,14},{3,7},{... | collective-permute-start | bytes 55304 | tf_op jit(solution)/shard_map/ppermute | solution.py:26
  157.9 5.6 %copy-start.9 = (pred[32]{0:T(512)(128)(4,1)S(1)}, pred[32]{0:T(512)(128)(4,1)}, u32[]{:S(2)}) copy-start(pred[32]{0:T(512)(128)(4,1)} %copy-done.8) | copy-start | bytes 100
  157.9 5.6 %copy-start.11 = (pred[32]{0:T(512)(128)(4,1)S(1)}, pred[32]{0:T(512)(128)(4,1)}, u32[]{:S(2)}) copy-start(pred[32]{0:T(512)(128)(4,1)} %copy-done.10) | copy-start | bytes 100
  158.2 3.9 %collective-permute-start.8 = (f32[12,3,32,1]{2,3,1,0:T(1,128)S(1)}, f32[12,3,32,1]{2,3,1,0:T(1,128)S(1)}, u32[]{:S(2)}, u32[]{:S(2)}) collective-permute-start(f32[12,3,32,1]{2,3,1,0:T(1,128)S(1)} %copy.33), channel_id=1, source_target_pairs={{16,0},{0,16},{17,1},{1,17},{18,2},{2,18},{19,3},{3,19},{20,4},{4,... | collective-permute-start | bytes 13832 | tf_op jit(solution)/shard_map/ppermute | solution.py:27
  159.2 3.8 %collective-permute-start.9 = (f32[12,3,32,1]{2,3,1,0:T(1,128)S(1)}, f32[12,3,32,1]{2,3,1,0:T(1,128)S(1)}, u32[]{:S(2)}, u32[]{:S(2)}) collective-permute-start(f32[12,3,32,1]{2,3,1,0:T(1,128)S(1)} %copy.35), channel_id=1, source_target_pairs={{0,16},{16,0},{1,17},{17,1},{2,18},{18,2},{3,19},{19,3},{4,20},{20... | collective-permute-start | bytes 13832 | tf_op jit(solution)/shard_map/ppermute | solution.py:26
Sparse Core Ops, SparseCore 0:
  62.7 35.6 all-reduce.2
  115.3 35.0 all-reduce.4
where the time goes:
time: 173 us; the launch traced here: 172 us
  waiting for transfers between devices  50.4 us (29%)
  blocking collectives  38.2 us (22%)
  other arithmetic  35.3 us (20%)
  starting transfers between devices  20.5 us (12%)
  local copies, waits for them, and re-layouts  13.9 us (8%)
  between operations  13.9 us (8%)
    psum x2, waiting for transfers between devices, mix_sum(): return lax.psum(partial_sum, 'lev')  46.6 us
    unnamed x4, other arithmetic  26.1 us
    psum x1, blocking collectives, on_device(): total_detrain = lax.psum(jnp.sum(detrain_share, axis=0), 'lev')  19 us
    all_gather x1, blocking collectives, on_device(): lax.all_gather(index_pair, ('lon', 'lat'), axis=2, tiled=True)  10.3 us
    ppermute x4, starting transfers between devices, extended(): before = lax.ppermute(last, axis, up)  9.26 us
    all_gather x1, blocking collectives, on_device(): lax.all_gather(values, ('lon', 'lat'), axis=2, tiled=True)  8.87 us
    ppermute x4, starting transfers between devices, from_behind(): return lax.ppermute(value, axis, pairs)  5.17 us
    slice x1, local copies, waits for them, and re-layouts, on_device(): adjoint = adjoint + forcing_grid[step_now][None]  3.81 us
  transfers between devices with their start and end apart: 15, of which 6 were waited for; matrix products, arithmetic and copies ran while one was open for 2% of the time, Pallas kernels for 0%

commit v1 on v0

v1 whole, which is shorter than its diff:
```python
import functools

import jax
import jax.numpy as jnp
from jax import lax
from jax.experimental import pallas as pl
from jax.experimental.pallas import tpu as pltpu
from jax.sharding import PartitionSpec as P

F32 = jnp.float32
LANES = 128
TOP, BOTTOM, ASCENDING, PARITY, SELF, NORTH, SOUTH, EAST, WEST, NORTH_ROW, SOUTH_ROW = range(11)


def swap_over(value, axis, bit):
    return lax.ppermute(value, axis, [(i, i ^ bit) for i in range(lax.axis_size(axis))])


def shift_over(value, axis, steps):
    count = lax.axis_size(axis)
    return lax.ppermute(value, axis, [(i, (i + steps) % count) for i in range(count)])


def meridian_rings(lon_count, lat_count, steps):
    pairs = []
    for lon in range(lon_count // 2):
        ring = [lon * lat_count + lat for lat in range(lat_count)]
        ring += [(lon + lon_count // 2) * lat_count + lat for lat in reversed(range(lat_count))]
        pairs += [(ring[i], ring[(i + steps) % len(ring)]) for i in range(len(ring))]
    return pairs


def exchange_rows(forward, back):
    lon_count, lat_count = lax.axis_size("lon"), lax.axis_size("lat")
    return (
        lax.ppermute(forward, ("lon", "lat"), meridian_rings(lon_count, lat_count, 1)),
        lax.ppermute(back, ("lon", "lat"), meridian_rings(lon_count, lat_count, -1)),
    )


def exchange_columns(columns):
    if lax.axis_size("lon") == 2:
        other = swap_over(columns, "lon", 1)
        return other, other
    return shift_over(columns, "lon", -1), shift_over(columns, "lon", 1)


def gather_blocks(block):
    blocks = block[None]
    for axis in ("lat", "lon"):
        count = lax.axis_size(axis)
        if count & (count - 1) == 0 and count <= 4:
            bit = 1
            while bit < count:
                blocks = jnp.concatenate([blocks, swap_over(blocks, axis, bit)], axis=0)
                bit *= 2
        else:
            blocks = lax.all_gather(blocks, axis, axis=0, tiled=True)
    return blocks


def lane_and_row(rows):
    return (
        lax.broadcasted_iota(jnp.int32, (rows, LANES), 1),
        lax.broadcasted_iota(jnp.int32, (rows, LANES), 0),
    )


def shifted(x, side, north, south):
    rows = x.shape[0]
    lane, row = lane_and_row(rows)
    east = jnp.where(lane == LANES - 1, side, pltpu.roll(x, LANES - 1, 1))
    west = jnp.where(lane == 0, side, pltpu.roll(x, 1, 1))
    above = jnp.where(row == rows - 1, north, pltpu.roll(x, rows - 1, 0))
    below = jnp.where(row == 0, south, pltpu.roll(x, 1, 0))
    return east, west, above, below


def stencil(coefs, x, side, north, south):
    east, west, above, below = shifted(x, side, north, south)
    own, to_east, to_west, to_north, to_south = coefs
    return own * x + to_east * east + to_west * west + to_north * above + to_south * below


class Columns:
    def __init__(self, rows):
        self.rows = rows
        self.per = LANES // rows
        self.blocks = [jnp.zeros((rows, LANES), F32)] * self.per
        self.lane = lane_and_row(rows)[0]

    def put(self, index, slab):
        group, place = divmod(index, self.per)
        turned = pltpu.roll(slab, 2 * group + 1, 1)
        self.blocks[place] = jnp.where(self.lane // 2 == group, turned, self.blocks[place])

    def get(self, rows):
        return jnp.transpose(jnp.concatenate(self.blocks, axis=0))[:rows]


def sides_of(eastern, western):
    rows = eastern.shape[0]
    row = lane_and_row(rows)[1]
    return jnp.where(row % 2 == 0, pltpu.roll(eastern, rows - 1, 0), pltpu.roll(western, 1, 0))


def turn(rows):
    pad = jnp.zeros((LANES - rows.shape[0], LANES), F32)
    return jnp.transpose(jnp.concatenate([rows, pad], axis=0))


def side_of(turned, index, rows):
    group, place = divmod(index, LANES // rows)
    return pltpu.roll(turned[place * rows : (place + 1) * rows], (LANES - 2 * group - 1) % LANES, 1)


def first_kernel(
    tracers, levels, rows, flags, field, detrain, mix, east, north, pole, keep, send, forward, back, columns, halves, ring
):
    half = tracers // 2
    slabs = tracers * levels
    weights = [detrain[k] for k in range(levels)]
    stay = [1.0 - mix[k] for k in range(levels)]
    cols = Columns(rows)
    ring[...] = jnp.zeros(ring.shape, F32)

    def edge_rows(place, slab):
        ring[0, place : place + 1, :] = slab[rows - 1 : rows]
        ring[1, place : place + 1, :] = slab[:1]

    for t in range(tracers):
        partial = None
        for k in range(levels):
            slab = field[t, k]
            term = weights[k] * slab
            partial = term if partial is None else partial + term
            slab = stay[k] * slab
            cols.put(t * levels + k, slab)
            edge_rows(t * levels + k, slab)
        halves[t // half, (t % half) * rows : (t % half + 1) * rows, :] = partial
        cols.put(slabs + t, partial)
        edge_rows(slabs + t, partial)
    total = functools.reduce(lambda a, b: a + b, weights)
    for h in range(2):
        halves[h, half * rows :, :] = total[h * rows // 2 : (h + 1) * rows // 2]
    cols.put(slabs + tracers, total)
    edge_rows(slabs + tracers, total)
    base = slabs + tracers + 1
    per = LANES // rows
    group = -(-base // per)
    for k in range(levels):
        edge_rows(base + k, mix[k])
        edge_rows(base + levels + k, detrain[k])
        ring[0, base + 2 * levels + k : base + 2 * levels + k + 1, :] = north[k, rows - 1 : rows, :]
        ring[1, base + 2 * levels + k : base + 2 * levels + k + 1, :] = pole[k : k + 1, :]
        cols.put(group * per + k, mix[k])
        cols.put((group + 1) * per + k, detrain[k])
        cols.put((group + 2) * per + k, east[k])
    parity = flags[PARITY]
    keep[...] = halves[parity]
    send[...] = halves[1 - parity]
    ascending = flags[ASCENDING]
    forward[...] = ring[1 - ascending]
    back[...] = ring[ascending]
    columns[...] = cols.get(columns.shape[0])


def second_kernel(
    tracers, levels, rows, flags, field, detrain, mix, east, north, pole, forward, back, eastern, western,
    keep, send, coefs, edges, turned, halves,
):
    half = tracers // 2
    slabs = tracers * levels
    base = slabs + tracers + 1
    per = LANES // rows
    group = -(-base // per)
    ascending = flags[ASCENDING] == 1
    from_north = jnp.where(ascending, back[...], forward[...])
    from_south = jnp.where(ascending, forward[...], back[...])
    edges[0] = from_north
    edges[1] = from_south
    sides = sides_of(eastern[...], western[...])
    around = turn(sides)
    turned[...] = around
    lane, row = lane_and_row(rows)
    top = jnp.logical_and(row == rows - 1, flags[TOP] == 1)
    bottom = jnp.logical_and(row == 0, flags[BOTTOM] == 1)
    weighted, stay = [], []
    mixed = None
    for k in range(levels):
        place = base + 2 * levels + k
        wind = east[k]
        behind = jnp.where(lane == 0, side_of(around, (group + 2) * per + k, rows), pltpu.roll(wind, 1, 1))
        to_east = jnp.maximum(wind, 0.0)
        to_west = jnp.maximum(-behind, 0.0)
        wind = north[k]
        across_north = jnp.maximum(-from_north[place : place + 1], 0.0)
        to_north = jnp.maximum(wind, 0.0) + jnp.where(top, across_north, 0.0)
        below = from_south[place : place + 1]
        across_south = jnp.maximum(pole[k : k + 1, :], 0.0) + jnp.maximum(-below, 0.0)
        behind = jnp.where(row == 0, below, pltpu.roll(wind, 1, 0))
        to_south = jnp.where(bottom, across_south, jnp.maximum(-behind, 0.0))
        own = 1.0 - to_east - to_west - to_north - to_south
        five = [own, to_east, to_west, to_north, to_south]
        for i in range(5):
            coefs[i, k] = five[i]
        weighted.append([detrain[k] * c for c in five])
        stay.append(1.0 - mix[k])
        share = mix[k]
        around_share = shifted(
            share,
            side_of(around, group * per + k, rows),
            from_north[base + k : base + k + 1],
            from_south[base + k : base + k + 1],
        )
        terms = [c * s for c, s in zip(weighted[k], (share,) + around_share)]
        mixed = terms if mixed is None else [a + b for a, b in zip(mixed, terms)]
    for t in range(tracers):
        partial = None
        for k in range(levels):
            place = t * levels + k
            term = stencil(
                weighted[k],
                stay[k] * field[t, k],
                side_of(around, place, rows),
                from_north[place : place + 1],
                from_south[place : place + 1],
            )
            partial = term if partial is None else partial + term
        halves[t // half, (t % half) * rows : (t % half + 1) * rows, :] = partial
    start = half * rows
    for i in range(5):
        for h in range(2):
            at = start + i * (rows // 2)
            halves[h, at : at + rows // 2, :] = mixed[i][h * rows // 2 : (h + 1) * rows // 2]
    start += 5 * (rows // 2)
    halves[:, start:, :] = jnp.zeros((2, halves.shape[1] - start, LANES), F32)
    lon_rows = 2 * (group - slabs // per)
    halves[0, start : start + lon_rows, :] = sides[2 * (slabs // per) : 2 * group]
    start += lon_rows
    halves[0, start : start + tracers + 1, :] = from_north[slabs : slabs + tracers + 1]
    halves[1, start : start + tracers + 1, :] = from_south[slabs : slabs + tracers + 1]
    parity = flags[PARITY]
    keep[...] = halves[parity]
    send[...] = halves[1 - parity]


def pieces(x):
    high = x.astype(jnp.bfloat16)
    rest = x - high.astype(F32)
    middle = rest.astype(jnp.bfloat16)
    low = (rest - middle.astype(F32)).astype(jnp.bfloat16)
    return [high, middle, low]


def product(a, b):
    return lax.dot_general(a, b, (((1,), (1,)), ((), ())), preferred_element_type=F32)


def forcing_kernel(levels, rows, steps, flags, slots, detrain, mix, coefs, edges, turned, base, grids, edge_rows, sums):
    count = slots.shape[2]
    per = LANES // rows
    row_ids = lax.broadcasted_iota(jnp.int32, (rows, count), 0)
    lane_ids = lax.broadcasted_iota(jnp.int32, (LANES, count), 0)
    group = -(-base // per)

    def add_block(index, carry):
        late, early, ring_sides = carry
        block = slots[index]
        results = []
        for step in range(steps):
            first = step * (levels + 2)
            values = [block[first + k : first + k + 1] for k in range(levels)]
            owner = block[first + levels : first + levels + 1].astype(jnp.int32)
            cell = block[first + levels + 1 : first + levels + 2].astype(jnp.int32)
            slot_row, slot_lane = cell // LANES, cell % LANES
            lanes = (lane_ids == slot_lane).astype(F32).astype(jnp.bfloat16)
            here = jnp.logical_and(row_ids == slot_row, owner == flags[SELF])
            left = [jnp.where(here, value, 0.0) for value in values]
            if step == steps - 1:
                in_north = jnp.logical_and(owner == flags[NORTH], slot_row == flags[NORTH_ROW])
                in_south = jnp.logical_and(owner == flags[SOUTH], slot_row == flags[SOUTH_ROW])
                left += [jnp.where(in_north, value, 0.0) for value in values]
                left += [jnp.where(in_south, value, 0.0) for value in values]
                left += [jnp.zeros((8 - 2 * levels, count), F32)]
            left = jnp.concatenate(left, axis=0)
            results.append(sum(product(piece, lanes) for piece in pieces(left)))
            if step == steps - 1:
                in_east = jnp.logical_and(owner == flags[EAST], slot_lane == 0)
                in_west = jnp.logical_and(owner == flags[WEST], slot_lane == LANES - 1)
                right = [jnp.where(in_east, value, 0.0) for value in values]
                right += [jnp.where(in_west, value, 0.0) for value in values]
                right += [jnp.zeros((8 - 2 * levels, count), F32)]
                right = jnp.concatenate(right, axis=0)
                at_row = (row_ids == slot_row).astype(F32).astype(jnp.bfloat16)
                ring_sides = ring_sides + sum(product(at_row, piece) for piece in pieces(right))
        return late + results[1], early + results[0], ring_sides

    late, early, ring_sides = lax.fori_loop(
        0,
        slots.shape[0],
        add_block,
        (
            jnp.zeros((levels * rows + 8, LANES), F32),
            jnp.zeros((levels * rows, LANES), F32),
            jnp.zeros((rows, 8), F32),
        ),
    )
    lane, _ = lane_and_row(rows)
    north_rows = late[levels * rows : levels * rows + levels]
    south_rows = late[levels * rows + levels : levels * rows + 2 * levels]
    edge_rows[...] = late[levels * rows :]
    around = turned[...]
    at_end = at_first = None
    ring = jnp.zeros((rows, LANES), F32)
    ring_north = jnp.zeros((1, LANES), F32)
    ring_south = jnp.zeros((1, LANES), F32)
    for k in range(levels):
        own = late[k * rows : (k + 1) * rows]
        now = early[k * rows : (k + 1) * rows]
        east_side = jnp.broadcast_to(ring_sides[:, k : k + 1], (rows, LANES))
        west_side = jnp.broadcast_to(ring_sides[:, levels + k : levels + k + 1], (rows, LANES))
        side = jnp.where(lane == LANES - 1, east_side, jnp.where(lane == 0, west_side, 0.0))
        grids[k] = own
        grids[levels + k] = now
        grids[2 * levels + k] = side
        mix_side = side_of(around, group * per + k, rows)
        detrain_side = side_of(around, (group + 1) * per + k, rows)
        north, south = north_rows[k : k + 1], south_rows[k : k + 1]
        moved = stencil(
            [coefs[i, k] for i in range(5)],
            (1.0 - mix[k]) * own,
            (1.0 - mix_side) * side,
            (1.0 - edges[0, base + k : base + k + 1, :]) * north,
            (1.0 - edges[1, base + k : base + k + 1, :]) * south,
        )
        first = detrain[k] * own
        second = detrain[k] * (moved + now)
        at_first = first if at_first is None else at_first + first
        at_end = second if at_end is None else at_end + second
        ring = ring + detrain_side * side
        place = base + levels + k
        ring_north = ring_north + edges[0, place : place + 1, :] * north
        ring_south = ring_south + edges[1, place : place + 1, :] * south
    sums[:rows] = at_first
    sums[rows : 2 * rows] = at_end
    flat = jnp.transpose(jnp.concatenate([ring] + [jnp.zeros((rows, LANES), F32)] * (per - 1), axis=0))
    sums[2 * rows :] = jnp.concatenate(
        [ring_north, ring_south, flat[LANES - 1 :], flat[:1], jnp.zeros((4, LANES), F32)], axis=0
    )


def third_kernel(
    tracers, levels, rows, flags, field, mix, coefs, edges, turned, grids, edge_rows,
    mine_first, other_first, mine_second, other_second,
    mixed_out, forward, back, columns, first, second, ring,
):
    half = tracers // 2
    slabs = tracers * levels
    base = slabs + tracers + 1
    per = LANES // rows
    group = -(-base // per)
    parity = flags[PARITY]
    second_rows = second.shape[1]
    first[parity] = mine_first[...]
    first[1 - parity] = other_first[...]
    second[parity] = mine_second[:second_rows]
    second[1 - parity] = other_second[:second_rows]
    forced = mine_second[second_rows:] + other_second[second_rows:]
    forced_first, forced_second = forced[:rows], forced[rows : 2 * rows]
    forced_ring = forced[2 * rows :]

    start = half * rows
    total = jnp.concatenate([first[0, start:, :], first[1, start:, :]], axis=0)
    inverse = 1.0 / total
    spread = []
    for i in range(5):
        at = start + i * (rows // 2)
        spread.append(jnp.concatenate([second[h, at : at + rows // 2, :] for h in range(2)], axis=0))
    start += 5 * (rows // 2)
    groups = tracers // per
    lon_sums = second[0, start : start + 2 * (group - slabs // per), :]
    start += 2 * (group - slabs // per)
    north_sums = second[0, start : start + tracers, :] + forced_ring[0:1]
    north_column = north_sums / second[0, start + tracers : start + tracers + 1, :]
    south_sums = second[1, start : start + tracers, :] + forced_ring[1:2]
    south_column = south_sums / second[1, start + tracers : start + tracers + 1, :]

    def tiled(x):
        lane = lax.broadcasted_iota(jnp.int32, x.shape, 1)
        x = jnp.where(lane < rows, x, 0.0)
        width = rows
        while width < LANES:
            x = x + pltpu.roll(x, width, 1)
            width *= 2
        return x

    side_total = tiled(lon_sums[2 * groups : 2 * groups + 2])
    side_forced = tiled(forced_ring[2:4])
    side_rows = [(lon_sums[2 * g : 2 * g + 2] + side_forced) / side_total for g in range(groups)]
    around_column = turn(jnp.concatenate(side_rows + [jnp.zeros((8 - 2 * groups, LANES), F32)], axis=0))
    around = turned[...]

    stay = [1.0 - mix[k] for k in range(levels)]
    mix_side = [side_of(around, group * per + k, rows) for k in range(levels)]
    forced_side = [(1.0 - mix_side[k]) * grids[2 * levels + k] for k in range(levels)]
    mix_edge = [[edges[e, base + k : base + k + 1, :] for k in range(levels)] for e in range(2)]
    forced_edge = [
        [(1.0 - mix_edge[e][k]) * edge_rows[e * levels + k : e * levels + k + 1, :] for k in range(levels)]
        for e in range(2)
    ]
    five = [[coefs[i, k] for i in range(5)] for k in range(levels)]
    cols = Columns(rows)
    ring[...] = jnp.zeros(ring.shape, F32)
    for t in range(tracers):
        h, at = t // half, (t % half) * rows
        column = (first[h, at : at + rows, :] + forced_first) * inverse
        column_side = side_of(around_column, t, rows)
        column_north, column_south = north_column[t : t + 1], south_column[t : t + 1]
        later = second[h, at : at + rows, :] + forced_second
        later = (later + stencil(spread, column, column_side, column_north, column_south)) * inverse
        for k in range(levels):
            place = t * levels + k
            now = stay[k] * (field[t, k] + grids[k]) + mix[k] * column
            side = side_of(around, place, rows) + forced_side[k] + mix_side[k] * column_side
            north = edges[0, place : place + 1, :] + forced_edge[0][k] + mix_edge[0][k] * column_north
            south = edges[1, place : place + 1, :] + forced_edge[1][k] + mix_edge[1][k] * column_south
            moved = stencil(five[k], now, side, north, south)
            moved = stay[k] * (moved + grids[levels + k]) + mix[k] * later
            mixed_out[t, k] = moved
            cols.put(place, moved)
            ring[0, place : place + 1, :] = moved[rows - 1 : rows]
            ring[1, place : place + 1, :] = moved[:1]
    ascending = flags[ASCENDING]
    forward[...] = ring[1 - ascending]
    back[...] = ring[ascending]
    columns[...] = cols.get(columns.shape[0])


def last_kernel(tracers, levels, rows, flags, mixed, coefs, forward, back, eastern, western, out):
    ascending = flags[ASCENDING] == 1
    from_north = jnp.where(ascending, back[...], forward[...])
    from_south = jnp.where(ascending, forward[...], back[...])
    around = turn(sides_of(eastern[...], western[...]))
    five = [[coefs[i, k] for i in range(5)] for k in range(levels)]
    for t in range(tracers):
        for k in range(levels):
            place = t * levels + k
            out[t, k] = stencil(
                five[k],
                mixed[t, k],
                side_of(around, place, rows),
                from_north[place : place + 1],
                from_south[place : place + 1],
            )


def up8(count):
    return -(-count // 8) * 8


def call(kernel, flags, args, outs, scratch=()):
    vmem = pl.BlockSpec(memory_space=pltpu.VMEM)
    shapes = [jax.ShapeDtypeStruct(shape, F32) for shape in outs]
    return pl.pallas_call(
        kernel,
        out_shape=shapes,
        in_specs=[pl.BlockSpec(memory_space=pltpu.SMEM)] + [vmem] * len(args),
        out_specs=[vmem] * len(shapes),
        scratch_shapes=[pltpu.VMEM(shape, F32) for shape in scratch],
        compiler_params=pltpu.CompilerParams(vmem_limit_bytes=32 * 1024 * 1024),
    )(flags, *args)


def on_device(
    adjoint_field,
    east_courant,
    north_courant,
    pole_courant,
    mix_fraction,
    detrain_share,
    sounding_owner,
    sounding_cell,
    sounding_count,
    sounding_forcing,
):
    lon_count, lat_count = lax.axis_size("lon"), lax.axis_size("lat")
    lon, lat, lev = lax.axis_index("lon"), lax.axis_index("lat"), lax.axis_index("lev")
    tracers, levels, rows, lanes = adjoint_field.shape
    steps, slot_count = sounding_cell.shape
    slabs = tracers * levels
    base = slabs + tracers + 1
    per = lanes // rows
    size = (tracers, levels, rows)

    top, bottom = lat == lat_count - 1, lat == 0
    partner = (lon + lon_count // 2) % lon_count
    flags = [
        top,
        bottom,
        lon < lon_count // 2,
        lev % 2,
        lon * lat_count + lat,
        jnp.where(top, partner * lat_count + lat, lon * lat_count + lat + 1),
        jnp.where(bottom, partner * lat_count + lat, lon * lat_count + lat - 1),
        (lon + 1) % lon_count * lat_count + lat,
        (lon + lon_count - 1) % lon_count * lat_count + lat,
        jnp.where(top, rows - 1, 0),
        jnp.where(bottom, 0, rows - 1),
    ]
    flags = jnp.stack([jnp.asarray(flag, jnp.int32) for flag in flags])

    live = jnp.arange(slot_count, dtype=jnp.int32)[None, :] < sounding_count
    values = jnp.where(live[:, None, :], sounding_forcing, 0.0)
    places = jnp.stack([sounding_owner[:, :, 0], sounding_cell], axis=1).astype(F32)
    slots = jnp.concatenate([values, places], axis=1).reshape(steps * (levels + 2), slot_count)
    slots = jnp.pad(slots, ((0, up8(slots.shape[0]) - slots.shape[0]), (0, 0)))

    ring_rows = up8(base + 3 * levels)
    column_rows = up8(2 * (-(-base // per) + 3))
    first_rows = tracers // 2 * rows + rows // 2
    keep, send, forward, back, columns = call(
        functools.partial(first_kernel, *size),
        flags,
        [adjoint_field, detrain_share, mix_fraction, east_courant, north_courant, pole_courant],
        [(first_rows, lanes)] * 2 + [(ring_rows, lanes)] * 2 + [(column_rows, lanes)],
        [(2, first_rows, lanes), (2, ring_rows, lanes)],
    )
    forward, back = exchange_rows(forward, back)
    eastern, western = exchange_columns(columns)
    first = keep + swap_over(send, "lev", 1)
    slots = gather_blocks(slots)

    lon_rows = 2 * (-(-base // per) - slabs // per)
    second_rows = tracers // 2 * rows + 5 * (rows // 2) + up8(lon_rows + tracers + 1)
    keep, send, coefs, edges, turned = call(
        functools.partial(second_kernel, *size),
        flags,
        [
            adjoint_field, detrain_share, mix_fraction, east_courant, north_courant, pole_courant,
            forward, back, eastern, western,
        ],
        [(second_rows, lanes)] * 2 + [(5, levels, rows, lanes), (2, ring_rows, lanes), (lanes, lanes)],
        [(2, second_rows, lanes)],
    )
    second = keep + swap_over(send, "lev", 1)
    first = first + swap_over(first, "lev", 2)

    grids, edge_rows, sums = call(
        lambda *refs: forcing_kernel(levels, rows, steps, *refs[:7], base, *refs[7:]),
        flags,
        [slots, detrain_share, mix_fraction, coefs, edges, turned],
        [(3 * levels, rows, lanes), (8, lanes), (2 * rows + 8, lanes)],
    )
    second = jnp.concatenate([second, sums], axis=0)
    second = second + swap_over(second, "lev", 2)
    other_first = swap_over(first, "lev", 1)
    other_second = swap_over(second, "lev", 1)

    slab_rows = up8(slabs)
    mixed, forward, back, columns = call(
        functools.partial(third_kernel, *size),
        flags,
        [
            adjoint_field, mix_fraction, coefs, edges, turned, grids, edge_rows,
            first, other_first, second, other_second,
        ],
        [adjoint_field.shape] + [(slab_rows, lanes)] * 2 + [(up8(2 * (slabs // per)), lanes)],
        [(2, first_rows, lanes), (2, second_rows, lanes), (2, slab_rows, lanes)],
    )
    forward, back = exchange_rows(forward, back)
    eastern, western = exchange_columns(columns)
    (out,) = call(
        functools.partial(last_kernel, *size),
        flags,
        [mixed, coefs, forward, back, eastern, western],
        [adjoint_field.shape],
    )
    return out


def solution(mesh):
    return jax.shard_map(
        on_device,
        mesh=mesh,
        in_specs=(
            P(None, "lev", "lat", "lon"),
            P("lev", "lat", "lon"),
            P("lev", "lat", "lon"),
            P("lev", "lon"),
            P("lev", "lat", "lon"),
            P("lev", "lat", "lon"),
            P(None, ("lon", "lat"), None),
            P(None, ("lon", "lat")),
            P(None, ("lon", "lat")),
            P(None, "lev", ("lon", "lat")),
        ),
        out_specs=P(None, "lev", "lat", "lon"),
        check_vma=False,
    )
```

time: 173 us -> 53.6 us (0.31)
  blocking collectives: 38.2 us -> 0 us
  other arithmetic: 35.3 us -> 0.19 us
  waiting for transfers between devices: 50.4 us -> 17.5 us
  between operations: 13.9 us -> 0.15 us
  local copies, waits for them, and re-layouts: 13.9 us -> 3.26 us
  Pallas kernels: 0 us -> 10.5 us
    psum x2 -> x0, waiting for transfers between devices: 46.6 us -> none  [mix_sum(): return lax.psum(partial_sum, 'lev')]
    unnamed x4 -> x0, other arithmetic: 26.1 us -> none
    all_gather x2 -> x0, blocking collectives: 19.2 us -> none  [the longest x1 10.3 us: on_device(): lax.all_gather(index_pair, ('lon', 'lat'), axis=2, tiled=True)]
    psum x1 -> x0, blocking collectives: 19 us -> none  [on_device(): total_detrain = lax.psum(jnp.sum(detrain_share, axis=0), 'lev')]
    ppermute x13 -> x15, waiting for transfers between devices: 3.78 us -> 17.5 us  [the longest x11 17.5 us: swap_over(): lax.ppermute(value, axis, [(i, i ^ bit) for i in range(lax.axis_size(axis...]
    pallas_call x0 -> x5, Pallas kernels: none -> 10.5 us  [call(): pl.pallas_call(kernel, out_shape=shapes, in_specs=[pl.BlockSpec(memory_sp...]
    slice x9 -> x0, local copies, waits for them, and re-layouts: 5.8 us -> none  [the longest x1 3.81 us: on_device(): adjoint = adjoint + forcing_grid[step_now][None]]
    add x3 -> x0, local copies, waits for them, and re-layouts: 3.88 us -> none  [the longest x2 2.89 us: on_device(): adjoint = adjoint + forcing_grid[step_now][None]]
  transfers between devices with their start and end apart: 15 -> 15, of which waited for: 6 -> 8; matrix products, arithmetic and copies ran while one was open for 2% -> 0% of each run, Pallas kernels for 0% -> 10%
where the time goes in v1:
time: 53.6 us; the launch traced here: 53.3 us
  starting transfers between devices  21.7 us (40%)
  waiting for transfers between devices  17.5 us (33%)
  Pallas kernels  10.5 us (20%)
  local copies, waits for them, and re-layouts  3.26 us (6%)
    ppermute x11, starting transfers between devices, swap_over(): lax.ppermute(value, axis, [(i, i ^ bit) for i in range(lax.axis_size(axis...  17.6 us
    ppermute x11, waiting for transfers between devices, swap_over(): lax.ppermute(value, axis, [(i, i ^ bit) for i in range(lax.axis_size(axis...  17.5 us
    pallas_call x5, Pallas kernels, call(): pl.pallas_call(kernel, out_shape=shapes, in_specs=[pl.BlockSpec(memory_sp...  10.5 us
    ppermute x2, starting transfers between devices, exchange_rows(): lax.ppermute(back, ('lon', 'lat'), meridian_rings(lon_count, lat_count, -1))  4.03 us
    unnamed x23, local copies, waits for them, and re-layouts  3.16 us
  transfers between devices with their start and end apart: 15, of which 8 were waited for; matrix products, arithmetic and copies ran while one was open for 0% of the time, Pallas kernels for 10%

profile of v1, /device:TPU:0, one launch (start us, length us, event | category | flops | bytes accessed | tf_op | source)
XLA Modules:
  0.0 53.3 jit_solution(14156247213386140084)
XLA Ops:
  0.0 0.7 %copy-done.10 = s32[2,1]{0,1:T(1,128)S(1)} copy-done((s32[2,1]{0,1:T(1,128)S(1)}, s32[2,1]{0,1:T(1,128)}, u32[]{:S(2)}) %copy-start.10) | copy-done | bytes 32
  0.7 0.1 iota_compare_fusion
  0.7 0.0 copy-done.8
  0.7 0.0 copy-start.7
  0.8 0.7 %copy-done.9 = s32[2,256]{1,0:T(2,128)S(1)} copy-done((s32[2,256]{1,0:T(2,128)S(1)}, s32[2,256]{1,0:T(2,128)}, u32[]{:S(2)}) %copy-start.9) | copy-done | bytes 2072
  1.4 0.0 copy-done.7
  1.5 0.0 copy-start.5
  1.5 0.5 collective-permute-start.3
  2.0 0.8 %collective-permute-done.3 = f32[1,16,256]{2,1,0:T(8,128)S(1)} collective-permute-done((f32[1,16,256]{2,1,0:T(8,128)S(1)}, f32[1,16,256]{2,1,0:T(8,128)S(1)}, u32[]{:S(2)}, u32[]{:S(2)}) %collective-permute-start.3) | collective-permute-done | bytes 16416 | tf_op jit(solution)/shard_map/ppermute | solution.py:16
  2.9 2.9 %collective-permute-start.4 = (f32[2,16,256]{2,1,0:T(8,128)S(1)}, f32[2,16,256]{2,1,0:T(8,128)S(1)}, u32[]{:S(2)}, u32[]{:S(2)}) collective-permute-start(f32[2,16,256]{2,1,0:T(8,128)S(1)} %pad_maximum_fusion.3), channel_id=1, source_target_pairs={{0,8},{4,12},{8,0},{12,4},{1,9},{5,13},{9,1},{13,5},{2,10},{6,14},... | collective-permute-start | bytes 98312 | tf_op jit(solution)/shard_map/ppermute | solution.py:16
  5.7 0.1 stack.62.flags.refs_0_
  5.8 0.0 copy-done.5
  5.8 0.6 %copy-done.6 = f32[3,128]{1,0:T(4,128)S(1)} copy-done((f32[3,128]{1,0:T(4,128)S(1)}, f32[3,128]{1,0:T(4,128)}, u32[]{:S(2)}) %copy-start.6) | copy-done | bytes 1560
  6.4 0.1 copy-done.3
  6.5 0.0 copy-done.2
  6.6 1.1 %copy-done = f32[12,3,32,128]{3,2,1,0:T(8,128)S(1)} copy-done((f32[12,3,32,128]{3,2,1,0:T(8,128)S(1)}, f32[12,3,32,128]{3,2,1,0:T(8,128)}, u32[]{:S(2)}) %copy-start) | copy-done | bytes 589848
  7.6 0.9 %shard_map.100 = (f32[208,128]{1,0:T(8,128)S(1)}, f32[208,128]{1,0:T(8,128)S(1)}, f32[64,128]{1,0:T(8,128)S(1)}, f32[64,128]{1,0:T(8,128)S(1)}, f32[32,128]{1,0:T(8,128)S(1)}) custom-call(s32[11]{0:T(128)S(1)} %stack.62.flags.refs_0_, f32[12,3,32,128]{3,2,1,0:T(8,128)S(1)} %copy-done, f32[3,32,128]{2,1,0:T(8,128)S(1)} %copy-done.3, ...), custom_call_target="tpu_custom_call" | custom-call | tf_op jit(solution)/shard_map/pallas_call | solution.py:465
  8.6 0.0 collective-permute-start
  8.6 2.0 %collective-permute-start.1 = (f32[64,128]{1,0:T(8,128)S(1)}, f32[64,128]{1,0:T(8,128)S(1)}, u32[]{:S(2)}, u32[]{:S(2)}) collective-permute-start(f32[64,128]{1,0:T(8,128)S(1)} %get-tuple-element.23), channel_id=1, source_target_pairs={{0,16},{4,0},{8,4},{12,8},{28,12},{24,28},{20,24},{16,20},{1,17},{... | collective-permute-start | bytes 98312 | tf_op jit(solution)/shard_map/ppermute | solution.py:37
  10.6 0.0 collective-permute-done.4
  10.6 0.1 collective-permute-start.5
  10.7 2.0 %collective-permute-start.2 = (f32[32,128]{1,0:T(8,128)S(1)}, f32[32,128]{1,0:T(8,128)S(1)}, u32[]{:S(2)}, u32[]{:S(2)}) collective-permute-start(f32[32,128]{1,0:T(8,128)S(1)} %get-tuple-element.24), channel_id=1, source_target_pairs={{0,16},{16,0},{1,17},{17,1},{2,18},{18,2},{3,19},{19,3},{4,20},{20... | collective-permute-start | bytes 49160 | tf_op jit(solution)/shard_map/ppermute | solution.py:16
  12.7 2.4 %collective-permute-done.2.eastern.western = f32[32,128]{1,0:T(8,128)S(1)} collective-permute-done((f32[32,128]{1,0:T(8,128)S(1)}, f32[32,128]{1,0:T(8,128)S(1)}, u32[]{:S(2)}, u32[]{:S(2)}) %collective-permute-start.2) | collective-permute-done | bytes 16416 | tf_op jit(solution)/shard_map/ppermute | solution.py:16
  15.1 0.0 collective-permute-done.forward
  15.1 0.0 collective-permute-done.1.back
  15.2 1.2 %shard_map.101 = (f32[296,128]{1,0:T(8,128)S(1)}, f32[296,128]{1,0:T(8,128)S(1)}, f32[5,3,32,128]{3,2,1,0:T(8,128)S(1)}, f32[2,64,128]{2,1,0:T(8,128)S(1)}, f32[128,128]{1,0:T(8,128)S(1)}) custom-call(s32[11]{0:T(128)S(1)} %stack.62.flags.refs_0_, f32[12,3,32,128]{3,2,1,0:T(8,128)S(1)} %copy-done, f32[3,32,128]{2,1,0:T(8,128)S(1)} %copy-done.3, ...), custom_call_target="tpu_custom_call" | custom-call | tf_op jit(solution)/shard_map/pallas_call | solution.py:465
  16.4 1.6 %collective-permute-start.9 = (f32[296,128]{1,0:T(8,128)S(1)}, f32[296,128]{1,0:T(8,128)S(1)}, u32[]{:S(2)}, u32[]{:S(2)}) collective-permute-start(f32[296,128]{1,0:T(8,128)S(1)} %get-tuple-element.33), channel_id=1, source_target_pairs={{0,1},{1,0},{2,3},{3,2},{4,5},{5,4},{6,7},{7,6},{8,9},{9,8},{10,11... | collective-permute-start | bytes 454664 | tf_op jit(solution)/shard_map/ppermute | solution.py:16
  18.1 0.0 collective-permute-done.5
  18.1 3.2 %shard_map.102 = (f32[9,32,128]{2,1,0:T(8,128)S(1)}, f32[8,128]{1,0:T(8,128)S(1)}, f32[72,128]{1,0:T(8,128)S(1)}) custom-call(s32[11]{0:T(128)S(1)} %stack.62.flags.refs_0_, f32[8,16,256]{2,1,0:T(8,128)S(1)} %pad_maximum_fusion.1.refs_1_, f32[3,32,128]{2,1,0:T(8,128)S(1)} %copy-done.3, f32[3,32,128]{2,1,0:T(8,128)S(1)} %copy-done.2, ...), custom_call_target="tpu_custom_call" | custom-call | tf_op jit(solution)/shard_map/pallas_call | solution.py:465
  21.3 0.4 collective-permute-done.9
  21.7 2.7 %collective-permute-start.10 = (f32[368,128]{1,0:T(8,128)S(1)}, f32[368,128]{1,0:T(8,128)S(1)}, u32[]{:S(2)}, u32[]{:S(2)}) collective-permute-start(f32[368,128]{1,0:T(8,128)S(1)} %pad_maximum_fusion), channel_id=1, source_target_pairs={{0,2},{1,3},{2,0},{3,1},{4,6},{5,7},{6,4},{7,5},{8,10},{9,11},{10,... | collective-permute-start | bytes 565256 | tf_op jit(solution)/shard_map/ppermute | solution.py:16
  24.4 1.6 %collective-permute-start.6 = (f32[208,128]{1,0:T(8,128)S(1)}, f32[208,128]{1,0:T(8,128)S(1)}, u32[]{:S(2)}, u32[]{:S(2)}) collective-permute-start(f32[208,128]{1,0:T(8,128)S(1)} %get-tuple-element.31), channel_id=1, source_target_pairs={{0,1},{1,0},{2,3},{3,2},{4,5},{5,4},{6,7},{7,6},{8,9},{9,8},{10,11... | collective-permute-start | bytes 319496 | tf_op jit(solution)/shard_map/ppermute | solution.py:16
  25.9 4.4 %collective-permute-done.6 = f32[208,128]{1,0:T(8,128)S(1)} collective-permute-done((f32[208,128]{1,0:T(8,128)S(1)}, f32[208,128]{1,0:T(8,128)S(1)}, u32[]{:S(2)}, u32[]{:S(2)}) %collective-permute-start.6) | collective-permute-done | bytes 106528 | tf_op jit(solution)/shard_map/ppermute | solution.py:16
  30.4 1.1 %collective-permute-start.7 = (f32[208,128]{1,0:T(8,128)S(1)}, f32[208,128]{1,0:T(8,128)S(1)}, u32[]{:S(2)}, u32[]{:S(2)}) collective-permute-start(f32[208,128]{1,0:T(8,128)S(1)} %add.52), channel_id=1, source_target_pairs={{0,2},{1,3},{2,0},{3,1},{4,6},{5,7},{6,4},{7,5},{8,10},{9,11},{10,... | collective-permute-start | bytes 319496 | tf_op jit(solution)/shard_map/ppermute | solution.py:16
  31.4 1.2 %collective-permute-done.10 = f32[368,128]{1,0:T(8,128)S(1)} collective-permute-done((f32[368,128]{1,0:T(8,128)S(1)}, f32[368,128]{1,0:T(8,128)S(1)}, u32[]{:S(2)}, u32[]{:S(2)}) %collective-permute-start.10) | collective-permute-done | bytes 188448 | tf_op jit(solution)/shard_map/ppermute | solution.py:16
  32.6 1.6 %collective-permute-start.11 = (f32[368,128]{1,0:T(8,128)S(1)}, f32[368,128]{1,0:T(8,128)S(1)}, u32[]{:S(2)}, u32[]{:S(2)}) collective-permute-start(f32[368,128]{1,0:T(8,128)S(1)} %fusion.mine_second), channel_id=1, source_target_pairs={{0,1},{1,0},{2,3},{3,2},{4,5},{5,4},{6,7},{7,6},{8,9},{9,8},{10,11... | collective-permute-start | bytes 565256 | tf_op jit(solution)/shard_map/ppermute | solution.py:16
  34.3 1.9 %collective-permute-done.7 = f32[208,128]{1,0:T(8,128)S(1)} collective-permute-done((f32[208,128]{1,0:T(8,128)S(1)}, f32[208,128]{1,0:T(8,128)S(1)}, u32[]{:S(2)}, u32[]{:S(2)}) %collective-permute-start.7) | collective-permute-done | bytes 106528 | tf_op jit(solution)/shard_map/ppermute | solution.py:16
  36.2 3.5 %collective-permute-start.8 = (f32[208,128]{1,0:T(8,128)S(1)}, f32[208,128]{1,0:T(8,128)S(1)}, u32[]{:S(2)}, u32[]{:S(2)}) collective-permute-start(f32[208,128]{1,0:T(8,128)S(1)} %add.53.mine_first), channel_id=1, source_target_pairs={{0,1},{1,0},{2,3},{3,2},{4,5},{5,4},{6,7},{7,6},{8,9},{9,8},{10,11... | collective-permute-start | bytes 319496 | tf_op jit(solution)/shard_map/ppermute | solution.py:16
  39.7 2.7 %collective-permute-done.8.other_first = f32[208,128]{1,0:T(8,128)S(1)} collective-permute-done((f32[208,128]{1,0:T(8,128)S(1)}, f32[208,128]{1,0:T(8,128)S(1)}, u32[]{:S(2)}, u32[]{:S(2)}) %collective-permute-start.8) | collective-permute-done | bytes 106528 | tf_op jit(solution)/shard_map/ppermute | solution.py:16
  42.4 0.0 collective-permute-done.11.other_second
  42.4 3.2 %shard_map.103 = (f32[12,3,32,128]{3,2,1,0:T(8,128)S(1)}, f32[40,128]{1,0:T(8,128)S(1)}, f32[40,128]{1,0:T(8,128)S(1)}, f32[24,128]{1,0:T(8,128)S(1)}) custom-call(s32[11]{0:T(128)S(1)} %stack.62.flags.refs_0_, f32[12,3,32,128]{3,2,1,0:T(8,128)S(1)} %copy-done.1, f32[3,32,128]{2,1,0:T(8,128)S(1)} %copy-done.2, ...), custom_call_target="tpu_custom_call" | custom-call | tf_op jit(solution)/shard_map/pallas_call | solution.py:465
  45.5 0.0 collective-permute-start.12
  45.6 2.0 %collective-permute-start.13 = (f32[40,128]{1,0:T(8,128)S(1)}, f32[40,128]{1,0:T(8,128)S(1)}, u32[]{:S(2)}, u32[]{:S(2)}) collective-permute-start(f32[40,128]{1,0:T(8,128)S(1)} %get-tuple-element.37), channel_id=1, source_target_pairs={{0,16},{4,0},{8,4},{12,8},{28,12},{24,28},{20,24},{16,20},{1,17},{... | collective-permute-start | bytes 61448 | tf_op jit(solution)/shard_map/ppermute | solution.py:37
  47.6 0.0 collective-permute-start.14
  47.6 3.7 %collective-permute-done.14.eastern.western = f32[24,128]{1,0:T(8,128)S(1)} collective-permute-done((f32[24,128]{1,0:T(8,128)S(1)}, f32[24,128]{1,0:T(8,128)S(1)}, u32[]{:S(2)}, u32[]{:S(2)}) %collective-permute-start.14) | collective-permute-done | bytes 12320 | tf_op jit(solution)/shard_map/ppermute | solution.py:16
  51.3 0.0 collective-permute-done.12.forward
  51.3 0.0 collective-permute-done.13.back
  51.3 2.0 %shard_map.104 = f32[12,3,32,128]{3,2,1,0:T(8,128)} custom-call(s32[11]{0:T(128)S(1)} %stack.62.flags.refs_0_, f32[12,3,32,128]{3,2,1,0:T(8,128)S(1)} %get-tuple-element.35.mixed, f32[5,3,32,128]{3,2,1,0:T(8,128)S(1)} %get-tuple-element.25.refs_4_.coefs, f32[40,128]{1,0:T(8,128)S(1)} %collective-permute-done.12.forward, ...), custom_call_target="tpu_custom_call" | custom-call | tf_op jit(solution)/shard_map/pallas_call | solution.py:465
  (26 shorter events, 0.2 us)
Async XLA Ops:
  0.0 0.7 %copy-start.10 = (s32[2,1]{0,1:T(1,128)S(1)}, s32[2,1]{0,1:T(1,128)}, u32[]{:S(2)}) copy-start(s32[2,1]{0,1:T(1,128)} %param.18) | copy-start | bytes 28
  0.0 0.7 %copy-start.8 = (s32[2,256,1]{1,2,0:T(1,128)S(1)}, s32[2,256,1]{1,2,0:T(1,128)}, u32[]{:S(2)}) copy-start(s32[2,256,1]{1,2,0:T(1,128)} %param.16) | copy-start | bytes 6148
  0.7 0.7 %copy-start.9 = (s32[2,256]{1,0:T(2,128)S(1)}, s32[2,256]{1,0:T(2,128)}, u32[]{:S(2)}) copy-start(s32[2,256]{1,0:T(2,128)} %param.17) | copy-start | bytes 6148
  0.7 0.7 %copy-start.7 = (f32[2,3,256]{2,0,1:T(2,128)S(1)}, f32[2,3,256]{2,0,1:T(2,128)}, u32[]{:S(2)}) copy-start(f32[2,3,256]{2,0,1:T(2,128)} %param.19) | copy-start | bytes 18436
  1.5 4.3 %copy-start.5 = (f32[3,32,128]{2,1,0:T(8,128)S(1)}, f32[3,32,128]{2,1,0:T(8,128)}, u32[]{:S(2)}) copy-start(f32[3,32,128]{2,1,0:T(8,128)} %north.3) | copy-start | bytes 147460
  1.5 1.4 %collective-permute-start.3 = (f32[1,16,256]{2,1,0:T(8,128)S(1)}, f32[1,16,256]{2,1,0:T(8,128)S(1)}, u32[]{:S(2)}, u32[]{:S(2)}) collective-permute-start(f32[1,16,256]{2,1,0:T(8,128)S(1)} %pad_bitcast_fusion), channel_id=1, source_target_pairs={{0,4},{4,0},{8,12},{12,8},{1,5},{5,1},{9,13},{13,9},{2,6},{6,2},{1... | collective-permute-start | bytes 49160 | tf_op jit(solution)/shard_map/ppermute | solution.py:16
  2.9 3.0 %copy-start.4 = (f32[3,32,128]{2,1,0:T(8,128)S(1)}, f32[3,32,128]{2,1,0:T(8,128)}, u32[]{:S(2)}) copy-start(f32[3,32,128]{2,1,0:T(8,128)} %east.3) | copy-start | bytes 147460
  2.9 7.7 %collective-permute-start.4 = (f32[2,16,256]{2,1,0:T(8,128)S(1)}, f32[2,16,256]{2,1,0:T(8,128)S(1)}, u32[]{:S(2)}, u32[]{:S(2)}) collective-permute-start(f32[2,16,256]{2,1,0:T(8,128)S(1)} %pad_maximum_fusion.3), channel_id=1, source_target_pairs={{0,8},{4,12},{8,0},{12,4},{1,9},{5,13},{9,1},{13,5},{2,10},{6,14},... | collective-permute-start | bytes 98312 | tf_op jit(solution)/shard_map/ppermute | solution.py:16
  5.7 0.7 %copy-start.6 = (f32[3,128]{1,0:T(4,128)S(1)}, f32[3,128]{1,0:T(4,128)}, u32[]{:S(2)}) copy-start(f32[3,128]{1,0:T(4,128)} %pole.3) | copy-start | bytes 4612
  5.7 0.8 %copy-start.3 = (f32[3,32,128]{2,1,0:T(8,128)S(1)}, f32[3,32,128]{2,1,0:T(8,128)}, u32[]{:S(2)}) copy-start(f32[3,32,128]{2,1,0:T(8,128)} %refs_2_.1) | copy-start | bytes 147460
  5.7 0.8 %copy-start.2 = (f32[3,32,128]{2,1,0:T(8,128)S(1)}, f32[3,32,128]{2,1,0:T(8,128)}, u32[]{:S(2)}) copy-start(f32[3,32,128]{2,1,0:T(8,128)} %mix.5) | copy-start | bytes 147460
  6.6 1.1 %copy-start = (f32[12,3,32,128]{3,2,1,0:T(8,128)S(1)}, f32[12,3,32,128]{3,2,1,0:T(8,128)}, u32[]{:S(2)}) copy-start(f32[12,3,32,128]{3,2,1,0:T(8,128)} %field.5) | copy-start | bytes 1769476
  8.6 6.6 %collective-permute-start = (f32[64,128]{1,0:T(8,128)S(1)}, f32[64,128]{1,0:T(8,128)S(1)}, u32[]{:S(2)}, u32[]{:S(2)}) collective-permute-start(f32[64,128]{1,0:T(8,128)S(1)} %get-tuple-element.22), channel_id=1, source_target_pairs={{0,4},{4,8},{8,12},{12,28},{28,24},{24,20},{20,16},{16,0},{1,5},{5... | collective-permute-start | bytes 98312 | tf_op jit(solution)/shard_map/ppermute | solution.py:36
  8.6 6.6 %collective-permute-start.1 = (f32[64,128]{1,0:T(8,128)S(1)}, f32[64,128]{1,0:T(8,128)S(1)}, u32[]{:S(2)}, u32[]{:S(2)}) collective-permute-start(f32[64,128]{1,0:T(8,128)S(1)} %get-tuple-element.23), channel_id=1, source_target_pairs={{0,16},{4,0},{8,4},{12,8},{28,12},{24,28},{20,24},{16,20},{1,17},{... | collective-permute-start | bytes 98312 | tf_op jit(solution)/shard_map/ppermute | solution.py:37
  10.6 7.4 %collective-permute-start.5 = (f32[4,16,256]{2,1,0:T(8,128)S(1)}, f32[4,16,256]{2,1,0:T(8,128)S(1)}, u32[]{:S(2)}, u32[]{:S(2)}) collective-permute-start(f32[4,16,256]{2,1,0:T(8,128)S(1)} %pad_maximum_fusion.2), channel_id=1, source_target_pairs={{0,16},{16,0},{1,17},{17,1},{2,18},{18,2},{3,19},{19,3},{4,20},{20... | collective-permute-start | bytes 196616 | tf_op jit(solution)/shard_map/ppermute | solution.py:16
  10.7 4.4 %collective-permute-start.2 = (f32[32,128]{1,0:T(8,128)S(1)}, f32[32,128]{1,0:T(8,128)S(1)}, u32[]{:S(2)}, u32[]{:S(2)}) collective-permute-start(f32[32,128]{1,0:T(8,128)S(1)} %get-tuple-element.24), channel_id=1, source_target_pairs={{0,16},{16,0},{1,17},{17,1},{2,18},{18,2},{3,19},{19,3},{4,20},{20... | collective-permute-start | bytes 49160 | tf_op jit(solution)/shard_map/ppermute | solution.py:16
  16.4 5.3 %collective-permute-start.9 = (f32[296,128]{1,0:T(8,128)S(1)}, f32[296,128]{1,0:T(8,128)S(1)}, u32[]{:S(2)}, u32[]{:S(2)}) collective-permute-start(f32[296,128]{1,0:T(8,128)S(1)} %get-tuple-element.33), channel_id=1, source_target_pairs={{0,1},{1,0},{2,3},{3,2},{4,5},{5,4},{6,7},{7,6},{8,9},{9,8},{10,11... | collective-permute-start | bytes 454664 | tf_op jit(solution)/shard_map/ppermute | solution.py:16
  21.7 10.9 %collective-permute-start.10 = (f32[368,128]{1,0:T(8,128)S(1)}, f32[368,128]{1,0:T(8,128)S(1)}, u32[]{:S(2)}, u32[]{:S(2)}) collective-permute-start(f32[368,128]{1,0:T(8,128)S(1)} %pad_maximum_fusion), channel_id=1, source_target_pairs={{0,2},{1,3},{2,0},{3,1},{4,6},{5,7},{6,4},{7,5},{8,10},{9,11},{10,... | collective-permute-start | bytes 565256 | tf_op jit(solution)/shard_map/ppermute | solution.py:16
  24.4 6.0 %collective-permute-start.6 = (f32[208,128]{1,0:T(8,128)S(1)}, f32[208,128]{1,0:T(8,128)S(1)}, u32[]{:S(2)}, u32[]{:S(2)}) collective-permute-start(f32[208,128]{1,0:T(8,128)S(1)} %get-tuple-element.31), channel_id=1, source_target_pairs={{0,1},{1,0},{2,3},{3,2},{4,5},{5,4},{6,7},{7,6},{8,9},{9,8},{10,11... | collective-permute-start | bytes 319496 | tf_op jit(solution)/shard_map/ppermute | solution.py:16
  30.4 12.0 %copy-start.1 = (f32[12,3,32,128]{3,2,1,0:T(8,128)S(1)}, f32[12,3,32,128]{3,2,1,0:T(8,128)}, u32[]{:S(2)}) copy-start(f32[12,3,32,128]{3,2,1,0:T(8,128)} %field.5) | copy-start | bytes 1769476
  30.4 5.8 %collective-permute-start.7 = (f32[208,128]{1,0:T(8,128)S(1)}, f32[208,128]{1,0:T(8,128)S(1)}, u32[]{:S(2)}, u32[]{:S(2)}) collective-permute-start(f32[208,128]{1,0:T(8,128)S(1)} %add.52), channel_id=1, source_target_pairs={{0,2},{1,3},{2,0},{3,1},{4,6},{5,7},{6,4},{7,5},{8,10},{9,11},{10,... | collective-permute-start | bytes 319496 | tf_op jit(solution)/shard_map/ppermute | solution.py:16
  32.6 9.7 %collective-permute-start.11 = (f32[368,128]{1,0:T(8,128)S(1)}, f32[368,128]{1,0:T(8,128)S(1)}, u32[]{:S(2)}, u32[]{:S(2)}) collective-permute-start(f32[368,128]{1,0:T(8,128)S(1)} %fusion.mine_second), channel_id=1, source_target_pairs={{0,1},{1,0},{2,3},{3,2},{4,5},{5,4},{6,7},{7,6},{8,9},{9,8},{10,11... | collective-permute-start | bytes 565256 | tf_op jit(solution)/shard_map/ppermute | solution.py:16
  36.2 6.2 %collective-permute-start.8 = (f32[208,128]{1,0:T(8,128)S(1)}, f32[208,128]{1,0:T(8,128)S(1)}, u32[]{:S(2)}, u32[]{:S(2)}) collective-permute-start(f32[208,128]{1,0:T(8,128)S(1)} %add.53.mine_first), channel_id=1, source_target_pairs={{0,1},{1,0},{2,3},{3,2},{4,5},{5,4},{6,7},{7,6},{8,9},{9,8},{10,11... | collective-permute-start | bytes 319496 | tf_op jit(solution)/shard_map/ppermute | solution.py:16
  45.5 5.8 %collective-permute-start.12 = (f32[40,128]{1,0:T(8,128)S(1)}, f32[40,128]{1,0:T(8,128)S(1)}, u32[]{:S(2)}, u32[]{:S(2)}) collective-permute-start(f32[40,128]{1,0:T(8,128)S(1)} %get-tuple-element.36), channel_id=1, source_target_pairs={{0,4},{4,8},{8,12},{12,28},{28,24},{24,20},{20,16},{16,0},{1,5},{5... | collective-permute-start | bytes 61448 | tf_op jit(solution)/shard_map/ppermute | solution.py:36
  45.6 5.7 %collective-permute-start.13 = (f32[40,128]{1,0:T(8,128)S(1)}, f32[40,128]{1,0:T(8,128)S(1)}, u32[]{:S(2)}, u32[]{:S(2)}) collective-permute-start(f32[40,128]{1,0:T(8,128)S(1)} %get-tuple-element.37), channel_id=1, source_target_pairs={{0,16},{4,0},{8,4},{12,8},{28,12},{24,28},{20,24},{16,20},{1,17},{... | collective-permute-start | bytes 61448 | tf_op jit(solution)/shard_map/ppermute | solution.py:37
  47.6 3.7 %collective-permute-start.14 = (f32[24,128]{1,0:T(8,128)S(1)}, f32[24,128]{1,0:T(8,128)S(1)}, u32[]{:S(2)}, u32[]{:S(2)}) collective-permute-start(f32[24,128]{1,0:T(8,128)S(1)} %get-tuple-element.38), channel_id=1, source_target_pairs={{0,16},{16,0},{1,17},{17,1},{2,18},{18,2},{3,19},{19,3},{4,20},{20... | collective-permute-start | bytes 36872 | tf_op jit(solution)/shard_map/ppermute | solution.py:16

commit v2 on v1

v2 whole, which is shorter than its diff:
```python
import functools

import jax
import jax.numpy as jnp
from jax import lax
from jax.experimental import pallas as pl
from jax.experimental.pallas import tpu as pltpu
from jax.sharding import PartitionSpec as P

F32 = jnp.float32
WEIGHTS = [0, 0, 0, 20, 20]
LANES = 128
TOP, BOTTOM, ASCENDING, PARITY, SELF, NORTH, SOUTH, EAST, WEST, NORTH_ROW, SOUTH_ROW = range(11)


def swap_over(value, axis, bit):
    return lax.ppermute(value, axis, [(i, i ^ bit) for i in range(lax.axis_size(axis))])


def shift_over(value, axis, steps):
    count = lax.axis_size(axis)
    return lax.ppermute(value, axis, [(i, (i + steps) % count) for i in range(count)])


def meridian_rings(lon_count, lat_count, steps):
    pairs = []
    for lon in range(lon_count // 2):
        ring = [lon * lat_count + lat for lat in range(lat_count)]
        ring += [(lon + lon_count // 2) * lat_count + lat for lat in reversed(range(lat_count))]
        pairs += [(ring[i], ring[(i + steps) % len(ring)]) for i in range(len(ring))]
    return pairs


def exchange_rows(forward, back):
    lon_count, lat_count = lax.axis_size("lon"), lax.axis_size("lat")
    return (
        lax.ppermute(forward, ("lon", "lat"), meridian_rings(lon_count, lat_count, 1)),
        lax.ppermute(back, ("lon", "lat"), meridian_rings(lon_count, lat_count, -1)),
    )


def exchange_columns(columns):
    if lax.axis_size("lon") == 2:
        other = swap_over(columns, "lon", 1)
        return other, other
    return shift_over(columns, "lon", -1), shift_over(columns, "lon", 1)


def pair_kernel(a, b, *refs):
    refs[-1][0] = a[...]
    refs[-1][1] = b[...]


def pair(a, b, *after):
    vmem = pl.BlockSpec(memory_space=pltpu.VMEM)
    return pl.pallas_call(
        pair_kernel,
        out_shape=jax.ShapeDtypeStruct((2, *a.shape), a.dtype),
        in_specs=[vmem, vmem] + [pl.BlockSpec(memory_space=pl.ANY)] * len(after),
        out_specs=vmem,
        compiler_params=pltpu.CompilerParams(vmem_limit_bytes=4 * 1024 * 1024),
    )(a, b, *after)


def gather_blocks(blocks, axis):
    count = lax.axis_size(axis)
    if count not in (2, 4):
        return lax.all_gather(blocks, axis, axis=0, tiled=True)
    return jnp.concatenate([blocks] + [swap_over(blocks, axis, bit) for bit in range(1, count)], axis=0)


def add_kernel(waited, a, b, *refs):
    refs[-1][...] = a[...] + b[...]


def add(a, b, *after):
    vmem = pl.BlockSpec(memory_space=pltpu.VMEM)
    return pl.pallas_call(
        functools.partial(add_kernel, len(after)),
        out_shape=jax.ShapeDtypeStruct(a.shape, a.dtype),
        in_specs=[vmem, vmem] + [pl.BlockSpec(memory_space=pl.ANY)] * len(after),
        out_specs=vmem,
        compiler_params=pltpu.CompilerParams(vmem_limit_bytes=4 * 1024 * 1024),
    )(a, b, *after)


def lane_and_row(rows):
    return (
        lax.broadcasted_iota(jnp.int32, (rows, LANES), 1),
        lax.broadcasted_iota(jnp.int32, (rows, LANES), 0),
    )


def shifted(x, side, north, south):
    rows = x.shape[0]
    lane, row = lane_and_row(rows)
    east = jnp.where(lane == LANES - 1, side, pltpu.roll(x, LANES - 1, 1))
    west = jnp.where(lane == 0, side, pltpu.roll(x, 1, 1))
    above = jnp.where(row == rows - 1, north, pltpu.roll(x, rows - 1, 0))
    below = jnp.where(row == 0, south, pltpu.roll(x, 1, 0))
    return east, west, above, below


def turned_round(x):
    rows = x.shape[0]
    return pltpu.roll(x, LANES - 1, 1), pltpu.roll(x, 1, 1), pltpu.roll(x, rows - 1, 0), pltpu.roll(x, 1, 0)


def stencil(coefs, x, side, north, south):
    east, west, above, below = shifted(x, side, north, south)
    own, to_east, to_west, to_north, to_south = coefs
    return own * x + to_east * east + to_west * west + to_north * above + to_south * below


class Columns:
    def __init__(self, rows):
        self.rows = rows
        self.per = LANES // rows
        self.blocks = [jnp.zeros((rows, LANES), F32)] * self.per
        self.lane = lane_and_row(rows)[0]

    def put(self, index, slab):
        group, place = divmod(index, self.per)
        turned = pltpu.roll(slab, 2 * group + 1, 1)
        self.blocks[place] = jnp.where(self.lane // 2 == group, turned, self.blocks[place])

    def get(self, rows):
        return jnp.transpose(jnp.concatenate(self.blocks, axis=0))[:rows]


def sides_of(eastern, western):
    rows = eastern.shape[0]
    row = lane_and_row(rows)[1]
    return jnp.where(row % 2 == 0, pltpu.roll(eastern, rows - 1, 0), pltpu.roll(western, 1, 0))


def turn(rows):
    pad = jnp.zeros((LANES - rows.shape[0], LANES), F32)
    return jnp.transpose(jnp.concatenate([rows, pad], axis=0))


def side_of(turned, index, rows):
    group, place = divmod(index, LANES // rows)
    return pltpu.roll(turned[place * rows : (place + 1) * rows], (LANES - 2 * group - 1) % LANES, 1)


def tiled(x, rows, block=0):
    if block:
        x = pltpu.roll(x, LANES - block * rows, 1)
    x = jnp.where(lax.broadcasted_iota(jnp.int32, x.shape, 1) < rows, x, 0.0)
    width = rows
    while width < LANES:
        x = x + pltpu.roll(x, width, 1)
        width *= 2
    return x


def first_kernel(
    tracers, levels, rows, flags, counts, owners_in, cells_in, forcing_in, field_in, detrain_in, mix_in, east_in, north_in,
    pole_in, keep_first, send_first, keep_second, send_second, slots, field, detrain, mix, east, north, pole,
    first, second, owners, cells, forcing, sems,
):
    pairs = [(detrain_in, detrain), (mix_in, mix), (east_in, east), (north_in, north)]
    pairs += [(owners_in, owners), (cells_in, cells), (forcing_in, forcing), (pole_in, pole)]
    pairs += [(field_in.at[t], field.at[t]) for t in range(tracers)]
    copies = [pltpu.make_async_copy(source, target, sems.at[i]) for i, (source, target) in enumerate(pairs)]
    for copy in copies:
        copy.start()
    static, loads = copies[:8], copies[8:]
    half = tracers // 2
    for copy in static:
        copy.wait()
    slots[...] = jnp.zeros(slots.shape, F32)
    steps, slot_count = cells.shape
    slot_rows = slots.shape[0] * LANES // slot_count
    slot = lax.broadcasted_iota(jnp.int32, (levels, LANES), 1)
    for part in range(slot_count // LANES):
        lanes = slice(part * LANES, (part + 1) * LANES)
        for step in range(steps):
            at = part * slot_rows + step * (levels + 2)
            live = slot + part * LANES < counts[step]
            slots[at : at + levels, :] = jnp.where(live, forcing[:, step, lanes], 0.0)
            slots[at + levels : at + levels + 1, :] = owners[step, :, lanes].astype(F32)
            slots[at + levels + 1 : at + levels + 2, :] = cells[step : step + 1, lanes].astype(F32)
    lane, row = lane_and_row(rows)
    weights = [detrain[k] for k in range(levels)]
    stay = [1.0 - mix[k] for k in range(levels)]
    inside, spread = [], None
    for k in range(levels):
        to_east = jnp.maximum(east[k], 0.0)
        to_west = jnp.where(lane == 0, 0.0, jnp.maximum(-pltpu.roll(east[k], 1, 1), 0.0))
        to_north = jnp.maximum(north[k], 0.0)
        to_south = jnp.where(row == 0, 0.0, jnp.maximum(-pltpu.roll(north[k], 1, 0), 0.0))
        own = 1.0 - to_east - to_west - to_north - to_south
        five = [
            own,
            jnp.where(lane == LANES - 1, 0.0, to_east),
            to_west,
            jnp.where(row == rows - 1, 0.0, to_north),
            to_south,
        ]
        inside.append([weights[k] * c for c in five])
        terms = [c * s for c, s in zip(inside[k], (mix[k],) + turned_round(mix[k]))]
        spread = terms if spread is None else [p + q for p, q in zip(spread, terms)]
    start = half * rows
    for i in range(5):
        for h in range(2):
            at = start + i * (rows // 2)
            second[h, at : at + rows // 2, :] = spread[i][h * rows // 2 : (h + 1) * rows // 2]
    total = functools.reduce(lambda p, q: p + q, weights)
    for h in range(2):
        first[h, start:, :] = total[h * rows // 2 : (h + 1) * rows // 2]
    for t in range(tracers):
        loads[t].wait()
        partial = later = None
        for k in range(levels):
            slab = field[t, k]
            term = weights[k] * slab
            partial = term if partial is None else partial + term
            slab = stay[k] * slab
            for c, x in zip(inside[k], (slab,) + turned_round(slab)):
                later = c * x if later is None else later + c * x
        at = (t % half) * rows
        first[t // half, at : at + rows, :] = partial
        second[t // half, at : at + rows, :] = later
    parity = flags[PARITY]
    keep_first[...] = first[parity]
    send_first[...] = first[1 - parity]
    keep_second[...] = second[parity]
    send_second[...] = second[1 - parity]


def edge_kernel(
    tracers, levels, rows, flags, slots, field, kept, detrain, mix, east, north, pole, forward, back, columns, ring
):
    slabs = tracers * levels
    base = slabs + tracers + 1
    per = LANES // rows
    group = -(-base // per)
    column_rows = up8(2 * (group + 3))
    columns[column_rows:] = slots[...]
    ring[...] = jnp.zeros(ring.shape, F32)
    weights = [detrain[k] for k in range(levels)]
    cols = Columns(rows)

    def edge_rows(place, slab):
        ring[0, place : place + 1, :] = slab[rows - 1 : rows]
        ring[1, place : place + 1, :] = slab[:1]

    total = functools.reduce(lambda p, q: p + q, weights)
    cols.put(slabs + tracers, total)
    edge_rows(slabs + tracers, total)
    for k in range(levels):
        edge_rows(base + k, mix[k])
        edge_rows(base + levels + k, detrain[k])
        ring[0, base + 2 * levels + k : base + 2 * levels + k + 1, :] = north[k, rows - 1 : rows, :]
        ring[1, base + 2 * levels + k : base + 2 * levels + k + 1, :] = pole[k : k + 1, :]
        cols.put(group * per + k, mix[k])
        cols.put((group + 1) * per + k, detrain[k])
        cols.put((group + 2) * per + k, east[k])
    for t in range(tracers):
        partial = None
        for k in range(levels):
            term = weights[k] * field[t, k]
            partial = term if partial is None else partial + term
            slab = kept[t, k]
            cols.put(k * tracers + t, slab)
            edge_rows(k * tracers + t, slab)
        cols.put(slabs + t, partial)
        edge_rows(slabs + t, partial)
    ascending = flags[ASCENDING]
    forward[...] = ring[1 - ascending]
    back[...] = ring[ascending]
    columns[:column_rows] = cols.get(column_rows)


def second_kernel(
    tracers, levels, rows, flags, first, second, detrain, mix, east, north, pole,
    own_forward, own_back, own_columns, forward, back, eastern, western,
    late, coefs, edges, turned,
):
    slabs = tracers * levels
    base = slabs + tracers + 1
    per = LANES // rows
    group = -(-base // per)
    ascending = flags[ASCENDING] == 1
    from_north = jnp.where(ascending, back[...], forward[...])
    from_south = jnp.where(ascending, forward[...], back[...])
    own_north = jnp.where(ascending, own_forward[...], own_back[...])
    own_south = jnp.where(ascending, own_back[...], own_forward[...])
    edges[0] = from_north
    edges[1] = from_south
    sides = sides_of(eastern[...], western[...])
    mine = own_columns[...]
    around = turn(sides)
    turned[...] = around
    lane, row = lane_and_row(rows)
    top, bottom = flags[TOP] == 1, flags[BOTTOM] == 1
    is_top = jnp.logical_and(row == rows - 1, top)
    is_bottom = jnp.logical_and(row == 0, bottom)
    west_row = lane_and_row(2)[1] == 1
    groups = tracers // per
    zero = jnp.zeros((1, LANES), F32)
    add_north = add_south = spread_north = spread_south = less_north = less_south = 0.0
    add_sides = [0.0] * groups
    spread_sides = less_sides = 0.0
    for k in range(levels):
        place = base + 2 * levels + k
        wind = east[k]
        behind = jnp.where(lane == 0, side_of(around, (group + 2) * per + k, rows), pltpu.roll(wind, 1, 1))
        to_east = jnp.maximum(wind, 0.0)
        to_west = jnp.maximum(-behind, 0.0)
        wind = north[k]
        pole_north = jnp.where(top, jnp.maximum(-from_north[place : place + 1], 0.0), zero)
        to_north = jnp.maximum(wind, 0.0) + jnp.where(is_top, pole_north, 0.0)
        below = from_south[place : place + 1]
        pole_south = jnp.maximum(pole[k : k + 1, :], 0.0) + jnp.maximum(-below, 0.0)
        behind = jnp.where(row == 0, below, pltpu.roll(wind, 1, 0))
        to_south = jnp.where(is_bottom, pole_south, jnp.maximum(-behind, 0.0))
        for i, c in enumerate([1.0 - to_east - to_west - to_north - to_south, to_east, to_west, to_north, to_south]):
            coefs[i, k] = c

        level = slice(k * tracers, (k + 1) * tracers)
        weight = detrain[k, rows - 1 : rows, :]
        taken, given = weight * to_north[rows - 1 : rows], weight * pole_north
        add_north = add_north + taken * from_north[level] - given * own_north[level]
        spread_north = spread_north + taken * from_north[base + k : base + k + 1]
        less_north = less_north - given * mix[k, rows - 1 : rows, :]
        taken = detrain[k, :1, :] * to_south[:1]
        add_south = add_south + taken * (from_south[level] - own_south[level])
        spread_south = spread_south + taken * from_south[base + k : base + k + 1]
        less_south = less_south - taken * mix[k, :1, :]

        winds = slice(2 * (group + 2), 2 * (group + 3))
        shares = slice(2 * group, 2 * (group + 1))
        weight = tiled(mine[2 * (group + 1) : 2 * (group + 2)], rows, k)
        wind = jnp.where(west_row, jnp.maximum(-sides[winds], 0.0), jnp.maximum(mine[winds], 0.0))
        taken = weight * tiled(wind, rows, k)
        given = jnp.where(west_row, taken, 0.0)
        for g in range(groups):
            pair = slice(2 * (k * groups + g), 2 * (k * groups + g + 1))
            add_sides[g] = add_sides[g] + taken * sides[pair] - given * mine[pair]
        spread_sides = spread_sides + taken * tiled(sides[shares], rows, k)
        less_sides = less_sides - given * tiled(mine[shares], rows, k)
    parts = [sides[2 * (slabs // per) : 2 * group]] + add_sides
    parts += [spread_sides, less_sides, spread_north, spread_south, less_north, less_south]
    parts += [add_north, add_south, from_north[slabs : slabs + tracers + 1], from_south[slabs : slabs + tracers + 1]]
    at = 0
    for part in parts:
        late[at : at + part.shape[0]] = part
        at += part.shape[0]
    if at < late.shape[0]:
        late[at:] = jnp.zeros((late.shape[0] - at, LANES), F32)


def pieces(x):
    high = x.astype(jnp.bfloat16)
    rest = x - high.astype(F32)
    middle = rest.astype(jnp.bfloat16)
    low = (rest - middle.astype(F32)).astype(jnp.bfloat16)
    return [high, middle, low]


def product(a, b):
    return lax.dot_general(a, b, (((1,), (1,)), ((), ())), preferred_element_type=F32)


def forcing_kernel(levels, rows, steps, flags, slots, detrain, mix, coefs, edges, turned, base, grids, edge_rows, sums):
    parts = min(8, slots.shape[0])
    count = parts * LANES
    per = LANES // rows
    row_ids = lax.broadcasted_iota(jnp.int32, (rows, count), 0)
    lane_ids = lax.broadcasted_iota(jnp.int32, (LANES, count), 0)
    group = -(-base // per)

    def add_block(index, carry):
        late, early, ring_sides = carry
        block = jnp.concatenate([slots[parts * index + part] for part in range(parts)], axis=1)
        results = []
        for step in range(steps):
            first = step * (levels + 2)
            values = [block[first + k : first + k + 1] for k in range(levels)]
            owner = block[first + levels : first + levels + 1].astype(jnp.int32)
            cell = block[first + levels + 1 : first + levels + 2].astype(jnp.int32)
            slot_row, slot_lane = cell // LANES, cell % LANES
            lanes = (lane_ids == slot_lane).astype(F32).astype(jnp.bfloat16)
            here = jnp.logical_and(row_ids == slot_row, owner == flags[SELF])
            left = [jnp.where(here, value, 0.0) for value in values]
            if step == steps - 1:
                in_north = jnp.logical_and(owner == flags[NORTH], slot_row == flags[NORTH_ROW])
                in_south = jnp.logical_and(owner == flags[SOUTH], slot_row == flags[SOUTH_ROW])
                left += [jnp.where(in_north, value, 0.0) for value in values]
                left += [jnp.where(in_south, value, 0.0) for value in values]
                left += [jnp.zeros((8 - 2 * levels, count), F32)]
            left = jnp.concatenate(left, axis=0)
            results.append(sum(product(piece, lanes) for piece in pieces(left)))
            if step == steps - 1:
                in_east = jnp.logical_and(owner == flags[EAST], slot_lane == 0)
                in_west = jnp.logical_and(owner == flags[WEST], slot_lane == LANES - 1)
                right = [jnp.where(in_east, value, 0.0) for value in values]
                right += [jnp.where(in_west, value, 0.0) for value in values]
                right += [jnp.zeros((8 - 2 * levels, count), F32)]
                right = jnp.concatenate(right, axis=0)
                at_row = (row_ids == slot_row).astype(F32).astype(jnp.bfloat16)
                ring_sides = ring_sides + sum(product(at_row, piece) for piece in pieces(right))
        return late + results[1], early + results[0], ring_sides

    late, early, ring_sides = lax.fori_loop(
        0,
        slots.shape[0] // parts,
        add_block,
        (
            jnp.zeros((levels * rows + 8, LANES), F32),
            jnp.zeros((levels * rows, LANES), F32),
            jnp.zeros((rows, 8), F32),
        ),
    )
    lane, _ = lane_and_row(rows)
    north_rows = late[levels * rows : levels * rows + levels]
    south_rows = late[levels * rows + levels : levels * rows + 2 * levels]
    edge_rows[...] = late[levels * rows :]
    around = turned[...]
    at_end = at_first = None
    ring = jnp.zeros((rows, LANES), F32)
    ring_north = jnp.zeros((1, LANES), F32)
    ring_south = jnp.zeros((1, LANES), F32)
    for k in range(levels):
        own = late[k * rows : (k + 1) * rows]
        now = early[k * rows : (k + 1) * rows]
        east_side = jnp.broadcast_to(ring_sides[:, k : k + 1], (rows, LANES))
        west_side = jnp.broadcast_to(ring_sides[:, levels + k : levels + k + 1], (rows, LANES))
        side = jnp.where(lane == LANES - 1, east_side, jnp.where(lane == 0, west_side, 0.0))
        grids[k] = own
        grids[levels + k] = now
        grids[2 * levels + k] = side
        mix_side = side_of(around, group * per + k, rows)
        detrain_side = side_of(around, (group + 1) * per + k, rows)
        north, south = north_rows[k : k + 1], south_rows[k : k + 1]
        moved = stencil(
            [coefs[i, k] for i in range(5)],
            (1.0 - mix[k]) * own,
            (1.0 - mix_side) * side,
            (1.0 - edges[0, base + k : base + k + 1, :]) * north,
            (1.0 - edges[1, base + k : base + k + 1, :]) * south,
        )
        first = detrain[k] * own
        second = detrain[k] * (moved + now)
        at_first = first if at_first is None else at_first + first
        at_end = second if at_end is None else at_end + second
        ring = ring + detrain_side * side
        place = base + levels + k
        ring_north = ring_north + edges[0, place : place + 1, :] * north
        ring_south = ring_south + edges[1, place : place + 1, :] * south
    sums[:rows] = at_first
    sums[rows : 2 * rows] = at_end
    flat = jnp.transpose(jnp.concatenate([ring] + [jnp.zeros((rows, LANES), F32)] * (per - 1), axis=0))
    sums[2 * rows :] = jnp.concatenate(
        [ring_north, ring_south, flat[LANES - 1 :], flat[:1], jnp.zeros((4, LANES), F32)], axis=0
    )


def third_kernel(
    tracers, levels, rows, flags, field, mix, coefs, edges, turned, mine, other, moved_out, column_out, inverse_out, first,
):
    half = tracers // 2
    parity = flags[PARITY]
    first[parity] = mine[...]
    first[1 - parity] = other[...]
    total = jnp.concatenate([first[0, half * rows :, :], first[1, half * rows :, :]], axis=0)
    inverse = 1.0 / total
    inverse_out[...] = inverse
    around = turned[...]
    stay = [1.0 - mix[k] for k in range(levels)]
    five = [[coefs[i, k] for i in range(5)] for k in range(levels)]
    for t in range(tracers):
        column = first[t // half, (t % half) * rows : (t % half + 1) * rows, :] * inverse
        column_out[t] = column
        for k in range(levels):
            place = k * tracers + t
            moved = stencil(
                five[k],
                stay[k] * field[t, k] + mix[k] * column,
                side_of(around, place, rows),
                edges[0, place : place + 1, :],
                edges[1, place : place + 1, :],
            )
            moved_out[t, k] = stay[k] * moved


def fourth_kernel(
    tracers, levels, rows, flags, moved, column, inverse_in, mix, coefs, edges, turned, grids, edge_rows,
    mine, other, forced_1, forced_2, forced_3, forced_4, mixed_out, forward, back, columns, second, ring,
):
    half = tracers // 2
    slabs = tracers * levels
    base = slabs + tracers + 1
    per = LANES // rows
    group = -(-base // per)
    groups = tracers // per
    parity = flags[PARITY]
    second_rows = second.shape[1]
    second[parity] = mine[:second_rows]
    second[1 - parity] = other[:second_rows]
    late = mine[second_rows:] + other[second_rows:]
    forced = (forced_1[...] + forced_2[...]) + (forced_3[...] + forced_4[...])
    inverse = inverse_in[...]
    lane, row = lane_and_row(rows)
    at_side = jnp.logical_or(lane == 0, lane == LANES - 1)
    last, initial = row == rows - 1, row == 0

    at = 2 * (group - slabs // per)
    inverse_side = 1.0 / tiled(late[2 * groups : 2 * groups + 2], rows)
    forced_sides = tiled(forced[2 * rows + 2 : 2 * rows + 4], rows)
    side_rows = [(late[2 * g : 2 * g + 2] + forced_sides) * inverse_side for g in range(groups)]
    side_rows += [late[at : at + 2 * groups + 4]]
    at += 2 * groups + 4
    around_late = turn(jnp.concatenate(side_rows, axis=0))
    spread_side = side_of(around_late, 2 * groups * per, rows)
    less_side = side_of(around_late, (2 * groups + 1) * per, rows)
    north, south, less_north, less_south = [late[at + i : at + i + 1] for i in range(4)]
    at += 4
    add_ends = [late[at + e * tracers : at + (e + 1) * tracers] for e in range(2)]
    at += 2 * tracers
    column_ends = []
    for e in range(2):
        sums = late[at : at + tracers + 1]
        column_ends.append((sums[:tracers] + forced[2 * rows + e : 2 * rows + e + 1]) / sums[tracers:])
        at += tracers + 1

    spread = []
    start = half * rows
    for i in range(5):
        at = start + i * (rows // 2)
        spread.append(jnp.concatenate([second[h, at : at + rows // 2, :] for h in range(2)], axis=0))
    spread[0] = spread[0] + jnp.where(last, less_north, 0.0) + jnp.where(initial, less_south, 0.0)
    spread[0] = spread[0] + jnp.where(lane == 0, less_side, 0.0)
    spread[1] = jnp.where(lane == LANES - 1, spread_side, spread[1])
    spread[2] = spread[2] + jnp.where(lane == 0, spread_side, 0.0)
    spread[3] = jnp.where(last, north, spread[3])
    spread[4] = spread[4] + jnp.where(initial, south, 0.0)

    forced_column = forced[:rows] * inverse
    forced_later = forced[rows : 2 * rows]
    around = turned[...]
    stay = [1.0 - mix[k] for k in range(levels)]
    forced_moved, to_sides, to_ends = [], [], []
    for k in range(levels):
        five = [coefs[i, k] for i in range(5)]
        mix_side = side_of(around, group * per + k, rows)
        shares = [edges[e, base + k : base + k + 1, :] for e in range(2)]
        ends = [(1.0 - shares[e]) * edge_rows[e * levels + k : e * levels + k + 1, :] for e in range(2)]
        moved_forcing = stencil(
            five,
            stay[k] * grids[k] + mix[k] * forced_column,
            (1.0 - mix_side) * grids[2 * levels + k],
            ends[0],
            ends[1],
        )
        forced_moved.append(stay[k] * (moved_forcing + grids[levels + k]))
        to_side = jnp.where(lane == LANES - 1, five[1], jnp.where(lane == 0, five[2], 0.0))
        to_sides.append(stay[k] * to_side * mix_side)
        to_ends.append(
            [
                jnp.where(last, stay[k] * five[3] * shares[0], 0.0)[rows - 8 :],
                jnp.where(initial, stay[k] * five[4] * shares[1], 0.0)[:8],
            ]
        )

    cols = Columns(rows)
    ring[...] = jnp.zeros(ring.shape, F32)
    for t in range(tracers):
        h, at = t // half, (t % half) * rows
        column_side = side_of(around_late, t, rows)
        column_north, column_south = column_ends[0][t : t + 1], column_ends[1][t : t + 1]
        later = second[h, at : at + rows, :] + forced_later
        later = later + jnp.where(at_side, side_of(around_late, (groups + t // per) * per + t % per, rows), 0.0)
        later = later + jnp.where(last, add_ends[0][t : t + 1], 0.0)
        later = later + jnp.where(initial, add_ends[1][t : t + 1], 0.0)
        later = later + stencil(spread, column[t] + forced_column, column_side, column_north, column_south)
        later = later * inverse
        for k in range(levels):
            place = k * tracers + t
            mixed = moved[t, k] + forced_moved[k] + mix[k] * later + to_sides[k] * column_side
            mixed = jnp.concatenate(
                [
                    mixed[:8] + to_ends[k][1] * column_south,
                    mixed[8 : rows - 8],
                    mixed[rows - 8 :] + to_ends[k][0] * column_north,
                ],
                axis=0,
            )
            mixed_out[t, k] = mixed
            cols.put(place, mixed)
            ring[0, place : place + 1, :] = mixed[rows - 1 : rows]
            ring[1, place : place + 1, :] = mixed[:1]
    ascending = flags[ASCENDING]
    forward[...] = ring[1 - ascending]
    back[...] = ring[ascending]
    columns[...] = cols.get(columns.shape[0])


def inner_kernel(tracers, levels, rows, flags, mixed, coefs, out):
    lane, row = lane_and_row(rows)
    for k in range(levels):
        own, to_east, to_west, to_north, to_south = [coefs[i, k] for i in range(5)]
        five = [
            own,
            jnp.where(lane == LANES - 1, 0.0, to_east),
            jnp.where(lane == 0, 0.0, to_west),
            jnp.where(row == rows - 1, 0.0, to_north),
            jnp.where(row == 0, 0.0, to_south),
        ]
        for t in range(tracers):
            slab = mixed[t, k]
            total = None
            for c, x in zip(five, (slab,) + turned_round(slab)):
                total = c * x if total is None else total + c * x
            out[t, k] = total


def last_kernel(tracers, levels, rows, flags, inner, coefs, forward, back, eastern, western, out, result, sems):
    ascending = flags[ASCENDING] == 1
    from_north = jnp.where(ascending, back[...], forward[...])
    from_south = jnp.where(ascending, forward[...], back[...])
    around = turn(sides_of(eastern[...], western[...]))
    lane, row = lane_and_row(rows)
    last, initial = row == rows - 1, row == 0
    to_sides = [
        jnp.where(lane == LANES - 1, coefs[1, k], jnp.where(lane == 0, coefs[2, k], 0.0)) for k in range(levels)
    ]
    to_north = [jnp.where(last, coefs[3, k], 0.0) for k in range(levels)]
    to_south = [jnp.where(initial, coefs[4, k], 0.0) for k in range(levels)]
    copies = []
    for t in range(tracers):
        for k in range(levels):
            place = k * tracers + t
            total = inner[t, k] + to_sides[k] * side_of(around, place, rows)
            total = total + to_north[k] * from_north[place : place + 1]
            result[t, k] = total + to_south[k] * from_south[place : place + 1]
        copy = pltpu.make_async_copy(result.at[t], out.at[t], sems.at[t])
        copy.start()
        copies.append(copy)
    for copy in copies:
        copy.wait()


def up8(count):
    return -(-count // 8) * 8


def call(kernel, scalars, args, outs, scratch=(), placed=(), copies=0, placed_out=False, weight=0):
    vmem, free = pl.BlockSpec(memory_space=pltpu.VMEM), pl.BlockSpec(memory_space=pl.ANY)
    return pl.pallas_call(
        kernel,
        out_shape=[jax.ShapeDtypeStruct(shape, F32) for shape in outs],
        in_specs=[pl.BlockSpec(memory_space=pltpu.SMEM)] * len(scalars) + [free] * len(placed) + [vmem] * len(args),
        out_specs=[free if placed_out else vmem] * len(outs),
        scratch_shapes=[pltpu.VMEM(x.shape, x.dtype) if hasattr(x, "dtype") else pltpu.VMEM(x, F32) for x in scratch]
        + ([pltpu.SemaphoreType.DMA((copies,))] if copies else []),
        compiler_params=pltpu.CompilerParams(vmem_limit_bytes=16 * 1024 * 1024),
        cost_estimate=pl.CostEstimate(flops=int(weight * 1e9), bytes_accessed=0, transcendentals=0),
    )(*scalars, *placed, *args)


def on_device(
    adjoint_field,
    east_courant,
    north_courant,
    pole_courant,
    mix_fraction,
    detrain_share,
    sounding_owner,
    sounding_cell,
    sounding_count,
    sounding_forcing,
):
    lon_count, lat_count = lax.axis_size("lon"), lax.axis_size("lat")
    lon, lat, lev = lax.axis_index("lon"), lax.axis_index("lat"), lax.axis_index("lev")
    tracers, levels, rows, lanes = adjoint_field.shape
    steps, slot_count = sounding_cell.shape
    slabs = tracers * levels
    base = slabs + tracers + 1
    per = lanes // rows
    size = (tracers, levels, rows)

    top, bottom = lat == lat_count - 1, lat == 0
    partner = (lon + lon_count // 2) % lon_count
    flags = [
        top,
        bottom,
        lon < lon_count // 2,
        (lev ^ (lev >> 1)) & 1,
        lon * lat_count + lat,
        jnp.where(top, partner * lat_count + lat, lon * lat_count + lat + 1),
        jnp.where(bottom, partner * lat_count + lat, lon * lat_count + lat - 1),
        (lon + 1) % lon_count * lat_count + lat,
        (lon + lon_count - 1) % lon_count * lat_count + lat,
        jnp.where(top, rows - 1, 0),
        jnp.where(bottom, 0, rows - 1),
    ]
    flags = jnp.stack([jnp.asarray(flag, jnp.int32) for flag in flags])

    ring_rows = up8(base + 3 * levels)
    column_rows = up8(2 * (-(-base // per) + 3))
    slot_rows = up8(steps * (levels + 2))
    first_rows = tracers // 2 * rows + rows // 2
    second_rows = tracers // 2 * rows + 5 * (rows // 2)
    soundings = [jnp.swapaxes(sounding_owner, 1, 2), sounding_cell, jnp.swapaxes(sounding_forcing, 0, 1)]
    static = [detrain_share, mix_fraction, east_courant, north_courant, pole_courant]
    keep_first, send_first, keep_second, send_second, slots, field, *static = call(
        functools.partial(first_kernel, *size),
        [flags, sounding_count[:, 0]],
        [],
        [(first_rows, lanes)] * 2
        + [(second_rows, lanes)] * 2
        + [(slot_count // lanes * slot_rows, lanes)]
        + [x.shape for x in [adjoint_field] + static],
        [(2, first_rows, lanes), (2, second_rows, lanes)] + soundings,
        [pltpu.with_memory_space_constraint(x, pltpu.HBM) for x in soundings + [adjoint_field] + static],
        tracers + len(soundings) + len(static),
        weight=WEIGHTS[0],
    )
    detrain, mix = static[:2]
    kept = (1.0 - mix)[None] * field
    own_forward, own_back, columns = call(
        functools.partial(edge_kernel, *size),
        [flags],
        [slots, field, kept] + static,
        [(ring_rows, lanes)] * 2 + [(column_rows + slots.shape[0], lanes)],
        [(2, ring_rows, lanes)],
        weight=WEIGHTS[1],
    )
    first = add(keep_first, swap_over(send_first, "lev", 1))
    second = add(keep_second, swap_over(send_second, "lev", 1))
    eastern, western = exchange_columns(columns)
    forward, back = exchange_rows(own_forward, own_back)
    other_first = swap_over(first, "lev", 3)

    late_rows = 2 * (-(-base // per) - slabs // per) + 2 * (tracers // per) + 8 + 4 * tracers + 2
    late, coefs, edges, turned = call(
        functools.partial(second_kernel, *size),
        [flags],
        static
        + [own_forward, own_back, columns[:column_rows]]
        + [forward, back, eastern[:column_rows], western[:column_rows]],
        [(up8(late_rows), lanes), (5, levels, rows, lanes), (2, ring_rows, lanes), (lanes, lanes)],
        placed=[first, second],
        weight=WEIGHTS[2],
    )
    second = jnp.concatenate([second, late], axis=0)
    other_second = swap_over(second, "lev", 3)
    slots = columns[column_rows:][None]
    if lon_count == 2:
        slots = pair(columns[column_rows:], eastern[column_rows:], first)
    else:
        slots = gather_blocks(slots, "lon")
    slots = gather_blocks(slots, "lat").reshape(-1, slot_rows, lanes)
    grids, edge_rows, sums = call(
        lambda *refs: forcing_kernel(levels, rows, steps, *refs[:7], base, *refs[7:]),
        [flags],
        [slots, detrain, mix, coefs, edges, turned],
        [(3 * levels, rows, lanes), (8, lanes), (2 * rows + 8, lanes)],
        weight=WEIGHTS[3],
    )
    sums = [sums] + [swap_over(sums, "lev", bit) for bit in (1, 2, 3)]
    first = add(first, other_first, sums[0])
    other_first = swap_over(first, "lev", 1)
    second = add(second, other_second, first)
    other_second = swap_over(second, "lev", 1)

    moved, column, inverse = call(
        functools.partial(third_kernel, *size),
        [flags],
        [field, mix, coefs, edges, turned, first, other_first],
        [adjoint_field.shape, (tracers, rows, lanes), (rows, lanes)],
        [(2, first_rows, lanes)],
        weight=WEIGHTS[4],
    )
    slab_rows = up8(slabs)
    mixed, forward, back, columns = call(
        functools.partial(fourth_kernel, *size),
        [flags],
        [
            moved, column, inverse, mix, coefs, edges, turned, grids, edge_rows,
            second, other_second, *sums,
        ],
        [adjoint_field.shape] + [(slab_rows, lanes)] * 2 + [(up8(2 * (slabs // per)), lanes)],
        [(2, second_rows, lanes), (2, slab_rows, lanes)],
    )
    eastern, western = exchange_columns(columns)
    forward, back = exchange_rows(forward, back)
    (inner,) = call(functools.partial(inner_kernel, *size), [flags], [mixed, coefs], [adjoint_field.shape])
    (out,) = call(
        functools.partial(last_kernel, *size),
        [flags],
        [inner, coefs, forward, back, eastern, western],
        [adjoint_field.shape],
        [adjoint_field.shape],
        copies=tracers,
        placed_out=True,
    )
    return out


def solution(mesh):
    return jax.shard_map(
        on_device,
        mesh=mesh,
        in_specs=(
            P(None, "lev", "lat", "lon"),
            P("lev", "lat", "lon"),
            P("lev", "lat", "lon"),
            P("lev", "lon"),
            P("lev", "lat", "lon"),
            P("lev", "lat", "lon"),
            P(None, ("lon", "lat"), None),
            P(None, ("lon", "lat")),
            P(None, ("lon", "lat")),
            P(None, "lev", ("lon", "lat")),
        ),
        out_specs=P(None, "lev", "lat", "lon"),
        check_vma=False,
    )
```

time: 53.6 us -> 46.6 us (0.87)
  waiting for transfers between devices: 17.5 us -> 13.7 us
  local copies, waits for them, and re-layouts: 3.26 us -> 0.75 us
  starting transfers between devices: 21.7 us -> 19.3 us
  Pallas kernels: 10.5 us -> 12.4 us
    ppermute x11 -> x14, waiting for transfers between devices: 17.5 us -> 13.6 us  [swap_over(): lax.ppermute(value, axis, [(i, i ^ bit) for i in range(lax.axis_size(axis...]
    unnamed x23 -> x2, local copies, waits for them, and re-layouts: 3.16 us -> 0.66 us
    ppermute x11 -> x14, starting transfers between devices: 17.6 us -> 15.2 us  [swap_over(): lax.ppermute(value, axis, [(i, i ^ bit) for i in range(lax.axis_size(axis...]
    pallas_call x5 -> x13, Pallas kernels: 10.5 us -> 12.4 us  [the longest x8 12.4 us: call(): pl.pallas_call(kernel, out_shape=[jax.ShapeDtypeStruct(shape, F32) for sh...]
  transfers between devices with their start and end apart: 15 -> 18, of which waited for: 8 -> 7; matrix products, arithmetic and copies ran while one was open for 0% -> 0% of each run, Pallas kernels for 10% -> 14%
where the time goes in v2:
time: 46.6 us; the launch traced here: 46.4 us
  starting transfers between devices  19.3 us (41%)
  waiting for transfers between devices  13.7 us (29%)
  Pallas kernels  12.4 us (27%)
  local copies, waits for them, and re-layouts  0.75 us (2%)
    ppermute x14, starting transfers between devices, swap_over(): lax.ppermute(value, axis, [(i, i ^ bit) for i in range(lax.axis_size(axis...  15.2 us
    ppermute x14, waiting for transfers between devices, swap_over(): lax.ppermute(value, axis, [(i, i ^ bit) for i in range(lax.axis_size(axis...  13.6 us
    pallas_call x8, Pallas kernels, call(): pl.pallas_call(kernel, out_shape=[jax.ShapeDtypeStruct(shape, F32) for sh...  12.4 us
    ppermute x2, starting transfers between devices, exchange_rows(): lax.ppermute(back, ('lon', 'lat'), meridian_rings(lon_count, lat_count, -1))  4.01 us
  transfers between devices with their start and end apart: 18, of which 7 were waited for; matrix products, arithmetic and copies ran while one was open for 0% of the time, Pallas kernels for 14%

profile of v2, /device:TPU:0, one launch (start us, length us, event | category | flops | bytes accessed | tf_op | source)
XLA Modules:
  0.0 46.4 jit_solution(13144183973160132887)
XLA Ops:
  0.0 0.1 stack.56.flags.refs_0_
  0.1 0.0 copy-start
  0.1 0.7 %copy-done = s32[2,1]{0,1:T(1,128)S(1)} copy-done((s32[2,1]{0,1:T(1,128)S(1)}, s32[2,1]{0,1:T(1,128)}, u32[]{:S(2)}) %copy-start) | copy-done | bytes 32
  0.7 2.9 %shard_map.100 = (f32[208,128]{1,0:T(8,128)S(1)}, f32[208,128]{1,0:T(8,128)S(1)}, f32[272,128]{1,0:T(8,128)S(1)}, f32[272,128]{1,0:T(8,128)S(1)}, f32[32,128]{1,...) custom-call(s32[11]{0:T(128)S(1)} %stack.56.flags.refs_0_, ...), custom_call_target="tpu_custom_call" | custom-call | tf_op jit(solution)/shard_map/pallas_call | solution.py:653
  3.7 3.1 %collective-permute-start = (f32[208,128]{1,0:T(8,128)S(1)}, f32[208,128]{1,0:T(8,128)S(1)}, u32[]{:S(2)}, u32[]{:S(2)}) collective-permute-start(f32[208,128]{1,0:T(8,128)S(1)} %get-tuple-element.36), channel_id=1, source_target_pairs={{0,1},{1,0},{2,3},{3,2},{4,5},{5,4},{6,7},{7,6},{8,9},{9,8},{10,11... | collective-permute-start | bytes 319496 | tf_op jit(solution)/shard_map/ppermute | solution.py:17
  6.8 0.1 collective-permute-start.1
  6.9 0.1 broadcast_multiply_fusion.kept
  6.9 0.9 %shard_map.103 = (f32[64,128]{1,0:T(8,128)S(1)}, f32[64,128]{1,0:T(8,128)S(1)}, f32[64,128]{1,0:T(8,128)S(1)}) custom-call(s32[11]{0:T(128)S(1)} %stack.56.flags.refs_0_, f32[32,128]{1,0:T(8,128)S(1)} %get-tuple-element.43.slots, f32[12,3,32,128]{3,2,1,0:T(8,128)S(1)} %get-tuple-element.33.field, f32[12,3,32,128]{3,2,1,0:T(8,128)S(1)} %broadcast_multiply_fusion.kept, ...), custom_call_target="tpu_custom_call" | custom-call | tf_op jit(solution)/shard_map/pallas_call | solution.py:653
  7.8 0.0 collective-permute-start.2
  7.9 2.0 %collective-permute-start.3 = (f32[64,128]{1,0:T(8,128)S(1)}, f32[64,128]{1,0:T(8,128)S(1)}, u32[]{:S(2)}, u32[]{:S(2)}) collective-permute-start(f32[64,128]{1,0:T(8,128)S(1)} %get-tuple-element.45.own_back), channel_id=1, source_target_pairs={{0,16},{4,0},{8,4},{12,8},{28,12},{24,28},{20,24},{16,20},{1,17},{... | collective-permute-start | bytes 98312 | tf_op jit(solution)/shard_map/ppermute | solution.py:38
  9.9 0.3 collective-permute-start.4
  10.2 3.6 %collective-permute-done.4 = f32[64,128]{1,0:T(8,128)S(1)} collective-permute-done((f32[64,128]{1,0:T(8,128)S(1)}, f32[64,128]{1,0:T(8,128)S(1)}, u32[]{:S(2)}, u32[]{:S(2)}) %collective-permute-start.4) | collective-permute-done | bytes 32800 | tf_op jit(solution)/shard_map/ppermute | solution.py:17
  13.8 0.0 collective-permute-done.b
  13.8 4.0 %collective-permute-start.5 = (f32[208,128]{1,0:T(8,128)S(1)}, f32[208,128]{1,0:T(8,128)S(1)}, u32[]{:S(2)}, u32[]{:S(2)}) collective-permute-start(f32[208,128]{1,0:T(8,128)S(1)} %shard_map.101.first.refs_0_.a), channel_id=1, source_target_pairs={{0,3},{1,2},{2,1},{3,0},{4,7},{5,6},{6,5},{7,4},{8,11},{9,10},{10,... | collective-permute-start | bytes 319496 | tf_op jit(solution)/shard_map/ppermute | solution.py:17
  17.9 0.0 collective-permute-start.8
  17.9 0.0 collective-permute-done.1.b
  17.9 1.3 %collective-permute-start.7 = (f32[2,32,128]{2,1,0:T(8,128)S(1)}, f32[2,32,128]{2,1,0:T(8,128)S(1)}, u32[]{:S(2)}, u32[]{:S(2)}) collective-permute-start(f32[2,32,128]{2,1,0:T(8,128)S(1)} %shard_map.105), channel_id=1, source_target_pairs={{0,8},{4,12},{8,0},{12,4},{1,9},{5,13},{9,1},{13,5},{2,10},{6,14},... | collective-permute-start | bytes 98312 | tf_op jit(solution)/shard_map/ppermute | solution.py:17
  19.2 0.0 collective-permute-done.2.forward
  19.2 0.6 %collective-permute-start.6 = (f32[2,32,128]{2,1,0:T(8,128)S(1)}, f32[2,32,128]{2,1,0:T(8,128)S(1)}, u32[]{:S(2)}, u32[]{:S(2)}) collective-permute-start(f32[2,32,128]{2,1,0:T(8,128)S(1)} %shard_map.105), channel_id=1, source_target_pairs={{0,4},{4,0},{8,12},{12,8},{1,5},{5,1},{9,13},{13,9},{2,6},{6,2},{1... | collective-permute-start | bytes 98312 | tf_op jit(solution)/shard_map/ppermute | solution.py:17
  19.8 0.0 collective-permute-done.3.back
  19.8 0.9 %shard_map.104 = (f32[72,128]{1,0:T(8,128)S(1)}, f32[5,3,32,128]{3,2,1,0:T(8,128)S(1)}, f32[2,64,128]{2,1,0:T(8,128)S(1)}, f32[128,128]{1,0:T(8,128)S(1)}) custom-call(s32[11]{0:T(128)S(1)} %stack.56.flags.refs_0_, f32[208,128]{1,0:T(8,128)S(1)} %shard_map.101.first.refs_0_.a, f32[272,128]{1,0:T(8,128)S(1)} %shard_map.102.second, ...), custom_call_target="tpu_custom_call" | custom-call | tf_op jit(solution)/shard_map/pallas_call | solution.py:653
  20.7 0.2 collective-permute-start.10
  20.9 0.5 collective-permute-done.8
  21.4 0.5 %collective-permute-done.7 = f32[2,32,128]{2,1,0:T(8,128)S(1)} collective-permute-done((f32[2,32,128]{2,1,0:T(8,128)S(1)}, f32[2,32,128]{2,1,0:T(8,128)S(1)}, u32[]{:S(2)}, u32[]{:S(2)}) %collective-permute-start.7) | collective-permute-done | bytes 32800 | tf_op jit(solution)/shard_map/ppermute | solution.py:17
  21.9 0.0 collective-permute-done.6
  21.9 2.5 %shard_map.106 = (f32[9,32,128]{2,1,0:T(8,128)S(1)}, f32[8,128]{1,0:T(8,128)S(1)}, f32[72,128]{1,0:T(8,128)S(1)}) custom-call(s32[11]{0:T(128)S(1)} %stack.56.flags.refs_0_, f32[16,16,128]{2,1,0:T(8,128)S(1)} %bitcast.14, f32[3,32,128]{2,1,0:T(8,128)S(1)} %get-tuple-element.39.detrain.refs_2_, f32[3,32,128]{2,1,0:T(8,128)S(1)} %get-tuple-element.34.mix.refs_3_, ...), custom_call_target="tpu_custom_call" | custom-call | flops 20000000000 | tf_op jit(solution)/shard_map/pallas_call | solution.py:653
  24.4 0.0 collective-permute-done.5.b
  24.4 0.1 collective-permute-start.9
  24.5 2.8 %collective-permute-start.14 = (f32[72,128]{1,0:T(8,128)S(1)}, f32[72,128]{1,0:T(8,128)S(1)}, u32[]{:S(2)}, u32[]{:S(2)}) collective-permute-start(f32[72,128]{1,0:T(8,128)S(1)} %get-tuple-element.50.refs_0_.forced_1), channel_id=1, source_target_pairs={{0,3},{1,2},{2,1},{3,0},{4,7},{5,6},{6,5},{7,4},{8,11},{9,10},{10,... | collective-permute-start | bytes 110600 | tf_op jit(solution)/shard_map/ppermute | solution.py:17
  27.3 0.7 %collective-permute-start.13 = (f32[72,128]{1,0:T(8,128)S(1)}, f32[72,128]{1,0:T(8,128)S(1)}, u32[]{:S(2)}, u32[]{:S(2)}) collective-permute-start(f32[72,128]{1,0:T(8,128)S(1)} %get-tuple-element.50.refs_0_.forced_1), channel_id=1, source_target_pairs={{0,2},{1,3},{2,0},{3,1},{4,6},{5,7},{6,4},{7,5},{8,10},{9,11},{10,... | collective-permute-start | bytes 110600 | tf_op jit(solution)/shard_map/ppermute | solution.py:17
  28.0 1.0 %collective-permute-start.12 = (f32[72,128]{1,0:T(8,128)S(1)}, f32[72,128]{1,0:T(8,128)S(1)}, u32[]{:S(2)}, u32[]{:S(2)}) collective-permute-start(f32[72,128]{1,0:T(8,128)S(1)} %get-tuple-element.50.refs_0_.forced_1), channel_id=1, source_target_pairs={{0,1},{1,0},{2,3},{3,2},{4,5},{5,4},{6,7},{7,6},{8,9},{9,8},{10,11... | collective-permute-start | bytes 110600 | tf_op jit(solution)/shard_map/ppermute | solution.py:17
  29.0 1.0 %collective-permute-done.10.b = f32[344,128]{1,0:T(8,128)S(1)} collective-permute-done((f32[344,128]{1,0:T(8,128)S(1)}, f32[344,128]{1,0:T(8,128)S(1)}, u32[]{:S(2)}, u32[]{:S(2)}) %collective-permute-start.10) | collective-permute-done | bytes 176160 | tf_op jit(solution)/shard_map/ppermute | solution.py:17
  30.0 1.0 %collective-permute-start.11 = (f32[344,128]{1,0:T(8,128)S(1)}, f32[344,128]{1,0:T(8,128)S(1)}, u32[]{:S(2)}, u32[]{:S(2)}) collective-permute-start(f32[344,128]{1,0:T(8,128)S(1)} %shard_map.109.mine), channel_id=1, source_target_pairs={{0,1},{1,0},{2,3},{3,2},{4,5},{5,4},{6,7},{7,6},{8,9},{9,8},{10,11... | collective-permute-start | bytes 528392 | tf_op jit(solution)/shard_map/ppermute | solution.py:17
  31.0 2.0 %collective-permute-done.9.other = f32[208,128]{1,0:T(8,128)S(1)} collective-permute-done((f32[208,128]{1,0:T(8,128)S(1)}, f32[208,128]{1,0:T(8,128)S(1)}, u32[]{:S(2)}, u32[]{:S(2)}) %collective-permute-start.9) | collective-permute-done | bytes 106528 | tf_op jit(solution)/shard_map/ppermute | solution.py:17
  33.0 1.2 %shard_map.108 = (f32[12,3,32,128]{3,2,1,0:T(8,128)S(1)}, f32[12,32,128]{2,1,0:T(8,128)S(1)}, f32[32,128]{1,0:T(8,128)S(1)}) custom-call(s32[11]{0:T(128)S(1)} %stack.56.flags.refs_0_, f32[12,3,32,128]{3,2,1,0:T(8,128)S(1)} %get-tuple-element.33.field, f32[3,32,128]{2,1,0:T(8,128)S(1)} %get-tuple-element.34.mix.refs_3_, ...), custom_call_target="tpu_custom_call" | custom-call | flops 20000000000 | tf_op jit(solution)/shard_map/pallas_call | solution.py:653
  34.2 0.0 collective-permute-done.14.forced_4
  34.2 0.0 collective-permute-done.13.forced_3
  34.2 0.0 collective-permute-done.12.forced_2
  34.3 3.3 %collective-permute-done.11.other = f32[344,128]{1,0:T(8,128)S(1)} collective-permute-done((f32[344,128]{1,0:T(8,128)S(1)}, f32[344,128]{1,0:T(8,128)S(1)}, u32[]{:S(2)}, u32[]{:S(2)}) %collective-permute-start.11) | collective-permute-done | bytes 176160 | tf_op jit(solution)/shard_map/ppermute | solution.py:17
  37.5 1.5 %shard_map.110 = (f32[12,3,32,128]{3,2,1,0:T(8,128)S(1)}, f32[40,128]{1,0:T(8,128)S(1)}, f32[40,128]{1,0:T(8,128)S(1)}, f32[24,128]{1,0:T(8,128)S(1)}) custom-call(s32[11]{0:T(128)S(1)} %stack.56.flags.refs_0_, f32[12,3,32,128]{3,2,1,0:T(8,128)S(1)} %get-tuple-element.51.moved, f32[12,32,128]{2,1,0:T(8,128)S(1)} %get-tuple-element.52.column, ...), custom_call_target="tpu_custom_call" | custom-call | tf_op jit(solution)/shard_map/pallas_call | solution.py:653
  39.0 0.1 collective-permute-start.15
  39.1 2.0 %collective-permute-start.16 = (f32[40,128]{1,0:T(8,128)S(1)}, f32[40,128]{1,0:T(8,128)S(1)}, u32[]{:S(2)}, u32[]{:S(2)}) collective-permute-start(f32[40,128]{1,0:T(8,128)S(1)} %get-tuple-element.59), channel_id=1, source_target_pairs={{0,16},{4,0},{8,4},{12,8},{28,12},{24,28},{20,24},{16,20},{1,17},{... | collective-permute-start | bytes 61448 | tf_op jit(solution)/shard_map/ppermute | solution.py:38
  41.1 0.0 collective-permute-start.17
  41.1 0.9 %shard_map.111.inner = f32[12,3,32,128]{3,2,1,0:T(8,128)S(1)} custom-call(s32[11]{0:T(128)S(1)} %stack.56.flags.refs_0_, f32[12,3,32,128]{3,2,1,0:T(8,128)S(1)} %get-tuple-element.57.mixed, f32[5,3,32,128]{3,2,1,0:T(8,128)S(1)} %get-tuple-element.47.refs_4_.coefs), custom_call_target="tpu_custom_call" | custom-call | tf_op jit(solution)/shard_map/pallas_call | solution.py:653
  42.0 2.7 %collective-permute-done.17.eastern.western = f32[24,128]{1,0:T(8,128)S(1)} collective-permute-done((f32[24,128]{1,0:T(8,128)S(1)}, f32[24,128]{1,0:T(8,128)S(1)}, u32[]{:S(2)}, u32[]{:S(2)}) %collective-permute-start.17) | collective-permute-done | bytes 12320 | tf_op jit(solution)/shard_map/ppermute | solution.py:17
  44.8 0.0 collective-permute-done.15.forward
  44.8 0.0 collective-permute-done.16.back
  44.8 1.6 %shard_map.112 = f32[12,3,32,128]{3,2,1,0:T(8,128)} custom-call(s32[11]{0:T(128)S(1)} %stack.56.flags.refs_0_, f32[12,3,32,128]{3,2,1,0:T(8,128)S(1)} %shard_map.111.inner, f32[5,3,32,128]{3,2,1,0:T(8,128)S(1)} %get-tuple-element.47.refs_4_.coefs, f32[40,128]{1,0:T(8,128)S(1)} %collective-permute-done.15.forward, ...), custom_call_target="tpu_custom_call" | custom-call | tf_op jit(solution)/shard_map/pallas_call | solution.py:653
  (10 shorter events, 0.1 us)
Async XLA Ops:
  0.1 0.7 %copy-start = (s32[2,1]{0,1:T(1,128)S(1)}, s32[2,1]{0,1:T(1,128)}, u32[]{:S(2)}) copy-start(s32[2,1]{0,1:T(1,128)} %param.18) | copy-start | bytes 28
  3.7 10.1 %collective-permute-start = (f32[208,128]{1,0:T(8,128)S(1)}, f32[208,128]{1,0:T(8,128)S(1)}, u32[]{:S(2)}, u32[]{:S(2)}) collective-permute-start(f32[208,128]{1,0:T(8,128)S(1)} %get-tuple-element.36), channel_id=1, source_target_pairs={{0,1},{1,0},{2,3},{3,2},{4,5},{5,4},{6,7},{7,6},{8,9},{9,8},{10,11... | collective-permute-start | bytes 319496 | tf_op jit(solution)/shard_map/ppermute | solution.py:17
  6.8 11.1 %collective-permute-start.1 = (f32[272,128]{1,0:T(8,128)S(1)}, f32[272,128]{1,0:T(8,128)S(1)}, u32[]{:S(2)}, u32[]{:S(2)}) collective-permute-start(f32[272,128]{1,0:T(8,128)S(1)} %get-tuple-element.38), channel_id=1, source_target_pairs={{0,1},{1,0},{2,3},{3,2},{4,5},{5,4},{6,7},{7,6},{8,9},{9,8},{10,11... | collective-permute-start | bytes 417800 | tf_op jit(solution)/shard_map/ppermute | solution.py:17
  7.8 11.4 %collective-permute-start.2 = (f32[64,128]{1,0:T(8,128)S(1)}, f32[64,128]{1,0:T(8,128)S(1)}, u32[]{:S(2)}, u32[]{:S(2)}) collective-permute-start(f32[64,128]{1,0:T(8,128)S(1)} %get-tuple-element.44.own_forward), channel_id=1, source_target_pairs={{0,4},{4,8},{8,12},{12,28},{28,24},{24,20},{20,16},{16,0},{1,5},{5... | collective-permute-start | bytes 98312 | tf_op jit(solution)/shard_map/ppermute | solution.py:37
  7.9 12.0 %collective-permute-start.3 = (f32[64,128]{1,0:T(8,128)S(1)}, f32[64,128]{1,0:T(8,128)S(1)}, u32[]{:S(2)}, u32[]{:S(2)}) collective-permute-start(f32[64,128]{1,0:T(8,128)S(1)} %get-tuple-element.45.own_back), channel_id=1, source_target_pairs={{0,16},{4,0},{8,4},{12,8},{28,12},{24,28},{20,24},{16,20},{1,17},{... | collective-permute-start | bytes 98312 | tf_op jit(solution)/shard_map/ppermute | solution.py:38
  9.9 3.9 %collective-permute-start.4 = (f32[64,128]{1,0:T(8,128)S(1)}, f32[64,128]{1,0:T(8,128)S(1)}, u32[]{:S(2)}, u32[]{:S(2)}) collective-permute-start(f32[64,128]{1,0:T(8,128)S(1)} %get-tuple-element.46), channel_id=1, source_target_pairs={{0,16},{16,0},{1,17},{17,1},{2,18},{18,2},{3,19},{19,3},{4,20},{20... | collective-permute-start | bytes 98312 | tf_op jit(solution)/shard_map/ppermute | solution.py:17
  13.8 10.6 %collective-permute-start.5 = (f32[208,128]{1,0:T(8,128)S(1)}, f32[208,128]{1,0:T(8,128)S(1)}, u32[]{:S(2)}, u32[]{:S(2)}) collective-permute-start(f32[208,128]{1,0:T(8,128)S(1)} %shard_map.101.first.refs_0_.a), channel_id=1, source_target_pairs={{0,3},{1,2},{2,1},{3,0},{4,7},{5,6},{6,5},{7,4},{8,11},{9,10},{10,... | collective-permute-start | bytes 319496 | tf_op jit(solution)/shard_map/ppermute | solution.py:17
  17.9 3.5 %collective-permute-start.8 = (f32[2,32,128]{2,1,0:T(8,128)S(1)}, f32[2,32,128]{2,1,0:T(8,128)S(1)}, u32[]{:S(2)}, u32[]{:S(2)}) collective-permute-start(f32[2,32,128]{2,1,0:T(8,128)S(1)} %shard_map.105), channel_id=1, source_target_pairs={{0,12},{4,8},{8,4},{12,0},{1,13},{5,9},{9,5},{13,1},{2,14},{6,10},... | collective-permute-start | bytes 98312 | tf_op jit(solution)/shard_map/ppermute | solution.py:17
  17.9 4.0 %collective-permute-start.7 = (f32[2,32,128]{2,1,0:T(8,128)S(1)}, f32[2,32,128]{2,1,0:T(8,128)S(1)}, u32[]{:S(2)}, u32[]{:S(2)}) collective-permute-start(f32[2,32,128]{2,1,0:T(8,128)S(1)} %shard_map.105), channel_id=1, source_target_pairs={{0,8},{4,12},{8,0},{12,4},{1,9},{5,13},{9,1},{13,5},{2,10},{6,14},... | collective-permute-start | bytes 98312 | tf_op jit(solution)/shard_map/ppermute | solution.py:17
  19.2 2.7 %collective-permute-start.6 = (f32[2,32,128]{2,1,0:T(8,128)S(1)}, f32[2,32,128]{2,1,0:T(8,128)S(1)}, u32[]{:S(2)}, u32[]{:S(2)}) collective-permute-start(f32[2,32,128]{2,1,0:T(8,128)S(1)} %shard_map.105), channel_id=1, source_target_pairs={{0,4},{4,0},{8,12},{12,8},{1,5},{5,1},{9,13},{13,9},{2,6},{6,2},{1... | collective-permute-start | bytes 98312 | tf_op jit(solution)/shard_map/ppermute | solution.py:17
  20.7 9.2 %collective-permute-start.10 = (f32[344,128]{1,0:T(8,128)S(1)}, f32[344,128]{1,0:T(8,128)S(1)}, u32[]{:S(2)}, u32[]{:S(2)}) collective-permute-start(f32[344,128]{1,0:T(8,128)S(1)} %pad_maximum_fusion.a), channel_id=1, source_target_pairs={{0,3},{1,2},{2,1},{3,0},{4,7},{5,6},{6,5},{7,4},{8,11},{9,10},{10,... | collective-permute-start | bytes 528392 | tf_op jit(solution)/shard_map/ppermute | solution.py:17
  24.4 8.6 %collective-permute-start.9 = (f32[208,128]{1,0:T(8,128)S(1)}, f32[208,128]{1,0:T(8,128)S(1)}, u32[]{:S(2)}, u32[]{:S(2)}) collective-permute-start(f32[208,128]{1,0:T(8,128)S(1)} %shard_map.107.mine.refs_0_), channel_id=1, source_target_pairs={{0,1},{1,0},{2,3},{3,2},{4,5},{5,4},{6,7},{7,6},{8,9},{9,8},{10,11... | collective-permute-start | bytes 319496 | tf_op jit(solution)/shard_map/ppermute | solution.py:17
  24.5 9.7 %collective-permute-start.14 = (f32[72,128]{1,0:T(8,128)S(1)}, f32[72,128]{1,0:T(8,128)S(1)}, u32[]{:S(2)}, u32[]{:S(2)}) collective-permute-start(f32[72,128]{1,0:T(8,128)S(1)} %get-tuple-element.50.refs_0_.forced_1), channel_id=1, source_target_pairs={{0,3},{1,2},{2,1},{3,0},{4,7},{5,6},{6,5},{7,4},{8,11},{9,10},{10,... | collective-permute-start | bytes 110600 | tf_op jit(solution)/shard_map/ppermute | solution.py:17
  27.3 6.9 %collective-permute-start.13 = (f32[72,128]{1,0:T(8,128)S(1)}, f32[72,128]{1,0:T(8,128)S(1)}, u32[]{:S(2)}, u32[]{:S(2)}) collective-permute-start(f32[72,128]{1,0:T(8,128)S(1)} %get-tuple-element.50.refs_0_.forced_1), channel_id=1, source_target_pairs={{0,2},{1,3},{2,0},{3,1},{4,6},{5,7},{6,4},{7,5},{8,10},{9,11},{10,... | collective-permute-start | bytes 110600 | tf_op jit(solution)/shard_map/ppermute | solution.py:17
  28.0 6.3 %collective-permute-start.12 = (f32[72,128]{1,0:T(8,128)S(1)}, f32[72,128]{1,0:T(8,128)S(1)}, u32[]{:S(2)}, u32[]{:S(2)}) collective-permute-start(f32[72,128]{1,0:T(8,128)S(1)} %get-tuple-element.50.refs_0_.forced_1), channel_id=1, source_target_pairs={{0,1},{1,0},{2,3},{3,2},{4,5},{5,4},{6,7},{7,6},{8,9},{9,8},{10,11... | collective-permute-start | bytes 110600 | tf_op jit(solution)/shard_map/ppermute | solution.py:17
  30.0 7.5 %collective-permute-start.11 = (f32[344,128]{1,0:T(8,128)S(1)}, f32[344,128]{1,0:T(8,128)S(1)}, u32[]{:S(2)}, u32[]{:S(2)}) collective-permute-start(f32[344,128]{1,0:T(8,128)S(1)} %shard_map.109.mine), channel_id=1, source_target_pairs={{0,1},{1,0},{2,3},{3,2},{4,5},{5,4},{6,7},{7,6},{8,9},{9,8},{10,11... | collective-permute-start | bytes 528392 | tf_op jit(solution)/shard_map/ppermute | solution.py:17
  39.0 5.8 %collective-permute-start.15 = (f32[40,128]{1,0:T(8,128)S(1)}, f32[40,128]{1,0:T(8,128)S(1)}, u32[]{:S(2)}, u32[]{:S(2)}) collective-permute-start(f32[40,128]{1,0:T(8,128)S(1)} %get-tuple-element.58), channel_id=1, source_target_pairs={{0,4},{4,8},{8,12},{12,28},{28,24},{24,20},{20,16},{16,0},{1,5},{5... | collective-permute-start | bytes 61448 | tf_op jit(solution)/shard_map/ppermute | solution.py:37
  39.1 5.7 %collective-permute-start.16 = (f32[40,128]{1,0:T(8,128)S(1)}, f32[40,128]{1,0:T(8,128)S(1)}, u32[]{:S(2)}, u32[]{:S(2)}) collective-permute-start(f32[40,128]{1,0:T(8,128)S(1)} %get-tuple-element.59), channel_id=1, source_target_pairs={{0,16},{4,0},{8,4},{12,8},{28,12},{24,28},{20,24},{16,20},{1,17},{... | collective-permute-start | bytes 61448 | tf_op jit(solution)/shard_map/ppermute | solution.py:38
  41.1 3.7 %collective-permute-start.17 = (f32[24,128]{1,0:T(8,128)S(1)}, f32[24,128]{1,0:T(8,128)S(1)}, u32[]{:S(2)}, u32[]{:S(2)}) collective-permute-start(f32[24,128]{1,0:T(8,128)S(1)} %get-tuple-element.60), channel_id=1, source_target_pairs={{0,16},{16,0},{1,17},{17,1},{2,18},{18,2},{3,19},{19,3},{4,20},{20... | collective-permute-start | bytes 36872 | tf_op jit(solution)/shard_map/ppermute | solution.py:17

commit v3 on v2

--- a/solution.py
+++ b/solution.py
@@ -156,21 +156,20 @@
 
 
 def first_kernel(
-    tracers, levels, rows, flags, counts, owners_in, cells_in, forcing_in, field_in, detrain_in, mix_in, east_in, north_in,
-    pole_in, keep_first, send_first, keep_second, send_second, slots, field, detrain, mix, east, north, pole,
-    first, second, owners, cells, forcing, sems,
+    tracers, levels, rows, flags, counts_in, owners_in, cells_in, forcing_in, detrain_in, field_in, mix_in, east_in,
+    north_in, pole_in, keep, send, slots, detrain, field, mix, east, north, pole,
+    halves, counts, owners, cells, forcing, sems,
 ):
-    pairs = [(detrain_in, detrain), (mix_in, mix), (east_in, east), (north_in, north)]
-    pairs += [(owners_in, owners), (cells_in, cells), (forcing_in, forcing), (pole_in, pole)]
+    pairs = [(counts_in, counts), (owners_in, owners), (cells_in, cells), (forcing_in, forcing), (detrain_in, detrain)]
     pairs += [(field_in.at[t], field.at[t]) for t in range(tracers)]
+    pairs += [(mix_in, mix), (east_in, east), (north_in, north), (pole_in, pole)]
     copies = [pltpu.make_async_copy(source, target, sems.at[i]) for i, (source, target) in enumerate(pairs)]
     for copy in copies:
         copy.start()
-    static, loads = copies[:8], copies[8:]
     half = tracers // 2
-    for copy in static:
+    slots[...] = jnp.zeros(slots.shape, F32)
+    for copy in copies[:5]:
         copy.wait()
-    slots[...] = jnp.zeros(slots.shape, F32)
     steps, slot_count = cells.shape
     slot_rows = slots.shape[0] * LANES // slot_count
     slot = lax.broadcasted_iota(jnp.int32, (levels, LANES), 1)
@@ -178,56 +177,62 @@
         lanes = slice(part * LANES, (part + 1) * LANES)
         for step in range(steps):
             at = part * slot_rows + step * (levels + 2)
-            live = slot + part * LANES < counts[step]
+            live = slot + part * LANES < jnp.broadcast_to(counts[:, step : step + 1], slot.shape)
             slots[at : at + levels, :] = jnp.where(live, forcing[:, step, lanes], 0.0)
             slots[at + levels : at + levels + 1, :] = owners[step, :, lanes].astype(F32)
             slots[at + levels + 1 : at + levels + 2, :] = cells[step : step + 1, lanes].astype(F32)
+    weights = [detrain[k] for k in range(levels)]
+    total = functools.reduce(lambda p, q: p + q, weights)
+    for h in range(2):
+        halves[h, half * rows :, :] = total[h * rows // 2 : (h + 1) * rows // 2]
+    for t in range(tracers):
+        copies[5 + t].wait()
+        at = (t % half) * rows
+        halves[t // half, at : at + rows, :] = functools.reduce(
+            lambda p, q: p + q, [weights[k] * field[t, k] for k in range(levels)]
+        )
+    parity = flags[PARITY]
+    keep[...] = halves[parity]
+    send[...] = halves[1 - parity]
+    for copy in copies[5 + tracers :]:
+        copy.wait()
+
+
+def inside_kernel(tracers, levels, rows, flags, after, field, kept, detrain, mix, east, north, keep, send, halves):
+    half = tracers // 2
     lane, row = lane_and_row(rows)
-    weights = [detrain[k] for k in range(levels)]
-    stay = [1.0 - mix[k] for k in range(levels)]
     inside, spread = [], None
     for k in range(levels):
+        weight = detrain[k]
         to_east = jnp.maximum(east[k], 0.0)
         to_west = jnp.where(lane == 0, 0.0, jnp.maximum(-pltpu.roll(east[k], 1, 1), 0.0))
         to_north = jnp.maximum(north[k], 0.0)
         to_south = jnp.where(row == 0, 0.0, jnp.maximum(-pltpu.roll(north[k], 1, 0), 0.0))
-        own = 1.0 - to_east - to_west - to_north - to_south
         five = [
-            own,
+            1.0 - to_east - to_west - to_north - to_south,
             jnp.where(lane == LANES - 1, 0.0, to_east),
             to_west,
             jnp.where(row == rows - 1, 0.0, to_north),
             to_south,
         ]
-        inside.append([weights[k] * c for c in five])
+        inside.append([weight * c for c in five])
         terms = [c * s for c, s in zip(inside[k], (mix[k],) + turned_round(mix[k]))]
         spread = terms if spread is None else [p + q for p, q in zip(spread, terms)]
-    start = half * rows
     for i in range(5):
         for h in range(2):
-            at = start + i * (rows // 2)
-            second[h, at : at + rows // 2, :] = spread[i][h * rows // 2 : (h + 1) * rows // 2]
-    total = functools.reduce(lambda p, q: p + q, weights)
-    for h in range(2):
-        first[h, start:, :] = total[h * rows // 2 : (h + 1) * rows // 2]
+            at = half * rows + i * (rows // 2)
+            halves[h, at : at + rows // 2, :] = spread[i][h * rows // 2 : (h + 1) * rows // 2]
     for t in range(tracers):
-        loads[t].wait()
-        partial = later = None
+        total = None
         for k in range(levels):
-            slab = field[t, k]
-            term = weights[k] * slab
-            partial = term if partial is None else partial + term
-            slab = stay[k] * slab
+            slab = kept[t, k]
             for c, x in zip(inside[k], (slab,) + turned_round(slab)):
-                later = c * x if later is None else later + c * x
+                total = c * x if total is None else total + c * x
         at = (t % half) * rows
-        first[t // half, at : at + rows, :] = partial
-        second[t // half, at : at + rows, :] = later
+        halves[t // half, at : at + rows, :] = total
     parity = flags[PARITY]
-    keep_first[...] = first[parity]
-    send_first[...] = first[1 - parity]
-    keep_second[...] = second[parity]
-    send_second[...] = second[1 - parity]
+    keep[...] = halves[parity]
+    send[...] = halves[1 - parity]
 
 
 def edge_kernel(
@@ -355,10 +360,7 @@
 
 def pieces(x):
     high = x.astype(jnp.bfloat16)
-    rest = x - high.astype(F32)
-    middle = rest.astype(jnp.bfloat16)
-    low = (rest - middle.astype(F32)).astype(jnp.bfloat16)
-    return [high, middle, low]
+    return [high, (x - high.astype(F32)).astype(jnp.bfloat16)]
 
 
 def product(a, b):
@@ -414,6 +416,7 @@
             jnp.zeros((levels * rows, LANES), F32),
             jnp.zeros((rows, 8), F32),
         ),
+        unroll=slots.shape[0] // parts <= 2,
     )
     lane, _ = lane_and_row(rows)
     north_rows = late[levels * rows : levels * rows + levels]
@@ -628,15 +631,16 @@
     to_sides = [
         jnp.where(lane == LANES - 1, coefs[1, k], jnp.where(lane == 0, coefs[2, k], 0.0)) for k in range(levels)
     ]
-    to_north = [jnp.where(last, coefs[3, k], 0.0) for k in range(levels)]
-    to_south = [jnp.where(initial, coefs[4, k], 0.0) for k in range(levels)]
+    to_north = [jnp.where(last, coefs[3, k], 0.0)[rows - 8 :] for k in range(levels)]
+    to_south = [jnp.where(initial, coefs[4, k], 0.0)[:8] for k in range(levels)]
     copies = []
     for t in range(tracers):
         for k in range(levels):
             place = k * tracers + t
             total = inner[t, k] + to_sides[k] * side_of(around, place, rows)
-            total = total + to_north[k] * from_north[place : place + 1]
-            result[t, k] = total + to_south[k] * from_south[place : place + 1]
+            result[t, k, :8, :] = total[:8] + to_south[k] * from_south[place : place + 1]
+            result[t, k, 8 : rows - 8, :] = total[8 : rows - 8]
+            result[t, k, rows - 8 :, :] = total[rows - 8 :] + to_north[k] * from_north[place : place + 1]
         copy = pltpu.make_async_copy(result.at[t], out.at[t], sems.at[t])
         copy.start()
         copies.append(copy)
@@ -705,22 +709,23 @@
     slot_rows = up8(steps * (levels + 2))
     first_rows = tracers // 2 * rows + rows // 2
     second_rows = tracers // 2 * rows + 5 * (rows // 2)
-    soundings = [jnp.swapaxes(sounding_owner, 1, 2), sounding_cell, jnp.swapaxes(sounding_forcing, 0, 1)]
-    static = [detrain_share, mix_fraction, east_courant, north_courant, pole_courant]
-    keep_first, send_first, keep_second, send_second, slots, field, *static = call(
+    soundings = [
+        jnp.swapaxes(sounding_count, 0, 1),
+        jnp.swapaxes(sounding_owner, 1, 2),
+        sounding_cell,
+        jnp.swapaxes(sounding_forcing, 0, 1),
+    ]
+    inputs = [detrain_share, adjoint_field, mix_fraction, east_courant, north_courant, pole_courant]
+    keep_first, send_first, slots, detrain, field, mix, east, north, pole = call(
         functools.partial(first_kernel, *size),
-        [flags, sounding_count[:, 0]],
+        [flags],
         [],
-        [(first_rows, lanes)] * 2
-        + [(second_rows, lanes)] * 2
-        + [(slot_count // lanes * slot_rows, lanes)]
-        + [x.shape for x in [adjoint_field] + static],
-        [(2, first_rows, lanes), (2, second_rows, lanes)] + soundings,
-        [pltpu.with_memory_space_constraint(x, pltpu.HBM) for x in soundings + [adjoint_field] + static],
-        tracers + len(soundings) + len(static),
-        weight=WEIGHTS[0],
-    )
-    detrain, mix = static[:2]
+        [(first_rows, lanes)] * 2 + [(slot_count // lanes * slot_rows, lanes)] + [x.shape for x in inputs],
+        [(2, first_rows, lanes)] + soundings,
+        [pltpu.with_memory_space_constraint(x, pltpu.HBM) for x in soundings + inputs],
+        tracers - 1 + len(soundings) + len(inputs),
+    )
+    static = [detrain, mix, east, north, pole]
     kept = (1.0 - mix)[None] * field
     own_forward, own_back, columns = call(
         functools.partial(edge_kernel, *size),
@@ -729,6 +734,15 @@
         [(ring_rows, lanes)] * 2 + [(column_rows + slots.shape[0], lanes)],
         [(2, ring_rows, lanes)],
         weight=WEIGHTS[1],
+    )
+    keep_second, send_second = call(
+        functools.partial(inside_kernel, *size),
+        [flags],
+        [field, kept, detrain, mix, east, north],
+        [(second_rows, lanes)] * 2,
+        [(2, second_rows, lanes)],
+        [columns],
+        weight=WEIGHTS[0],
     )
     first = add(keep_first, swap_over(send_first, "lev", 1))
     second = add(keep_second, swap_over(send_second, "lev", 1))

time: 46.6 us -> 45.7 us (0.981)
  starting transfers between devices: 19.3 us -> 23.7 us
  waiting for transfers between devices: 13.7 us -> 9.53 us
  local copies, waits for them, and re-layouts: 0.75 us -> 0.09 us
  Pallas kernels: 12.4 us -> 11.9 us
    ppermute x14, starting transfers between devices: 15.2 us -> 19.6 us  [swap_over(): lax.ppermute(value, axis, [(i, i ^ bit) for i in range(lax.axis_size(axis...]
    ppermute x14, waiting for transfers between devices: 13.6 us -> 9.52 us  [swap_over(): lax.ppermute(value, axis, [(i, i ^ bit) for i in range(lax.axis_size(axis...]
    unnamed x2 -> x0, local copies, waits for them, and re-layouts: 0.66 us -> none
    pallas_call x8 -> x9, Pallas kernels: 12.4 us -> 11.8 us  [call(): pl.pallas_call(kernel, out_shape=[jax.ShapeDtypeStruct(shape, F32) for sh...]
  transfers between devices with their start and end apart: 18 -> 18, of which waited for: 7 -> 4; matrix products, arithmetic and copies ran while one was open for 0% -> 0% of each run, Pallas kernels for 14% -> 15%
where the time goes in v3:
time: 45.7 us; the launch traced here: 45.5 us
  starting transfers between devices  23.7 us (52%)
  Pallas kernels  11.9 us (26%)
  waiting for transfers between devices  9.53 us (21%)
    ppermute x14, starting transfers between devices, swap_over(): lax.ppermute(value, axis, [(i, i ^ bit) for i in range(lax.axis_size(axis...  19.6 us
    pallas_call x9, Pallas kernels, call(): pl.pallas_call(kernel, out_shape=[jax.ShapeDtypeStruct(shape, F32) for sh...  11.8 us
    ppermute x14, waiting for transfers between devices, swap_over(): lax.ppermute(value, axis, [(i, i ^ bit) for i in range(lax.axis_size(axis...  9.52 us
    ppermute x2, starting transfers between devices, exchange_rows(): lax.ppermute(back, ('lon', 'lat'), meridian_rings(lon_count, lat_count, -1))  4.03 us
  transfers between devices with their start and end apart: 18, of which 4 were waited for; matrix products, arithmetic and copies ran while one was open for 0% of the time, Pallas kernels for 15%

profile of v3, /device:TPU:0, one launch (start us, length us, event | category | flops | bytes accessed | tf_op | source)
XLA Modules:
  0.0 45.5 jit_solution(4974884320178523412)
XLA Ops:
  0.0 0.1 stack.56.flags.refs_0_
  0.1 1.9 %shard_map.100 = (f32[208,128]{1,0:T(8,128)S(1)}, f32[208,128]{1,0:T(8,128)S(1)}, f32[32,128]{1,0:T(8,128)S(1)}, f32[3,32,128]{2,1,0:T(8,128)S(1)}, f32[12,3,32,...) custom-call(s32[11]{0:T(128)S(1)} %stack.56.flags.refs_0_, ...), custom_call_target="tpu_custom_call" | custom-call | tf_op jit(solution)/shard_map/pallas_call | solution.py:657
  2.0 3.1 %collective-permute-start = (f32[208,128]{1,0:T(8,128)S(1)}, f32[208,128]{1,0:T(8,128)S(1)}, u32[]{:S(2)}, u32[]{:S(2)}) collective-permute-start(f32[208,128]{1,0:T(8,128)S(1)} %get-tuple-element.36), channel_id=1, source_target_pairs={{0,1},{1,0},{2,3},{3,2},{4,5},{5,4},{6,7},{7,6},{8,9},{9,8},{10,11... | collective-permute-start | bytes 319496 | tf_op jit(solution)/shard_map/ppermute | solution.py:17
  5.2 0.9 %shard_map.102 = (f32[64,128]{1,0:T(8,128)S(1)}, f32[64,128]{1,0:T(8,128)S(1)}, f32[64,128]{1,0:T(8,128)S(1)}) custom-call(s32[11]{0:T(128)S(1)} %stack.56.flags.refs_0_, f32[32,128]{1,0:T(8,128)S(1)} %get-tuple-element.37.slots, f32[12,3,32,128]{3,2,1,0:T(8,128)S(1)} %get-tuple-element.33.field, f32[12,3,32,128]{3,2,1,0:T(8,128)S(1)} %broadcast_multiply_fusion.kept, ...), custom_call_target="tpu_custom_call" | custom-call | tf_op jit(solution)/shard_map/pallas_call | solution.py:657
  6.1 0.0 collective-permute-start.2
  6.1 2.0 %collective-permute-start.3 = (f32[64,128]{1,0:T(8,128)S(1)}, f32[64,128]{1,0:T(8,128)S(1)}, u32[]{:S(2)}, u32[]{:S(2)}) collective-permute-start(f32[64,128]{1,0:T(8,128)S(1)} %get-tuple-element.46.own_back), channel_id=1, source_target_pairs={{0,16},{4,0},{8,4},{12,8},{28,12},{24,28},{20,24},{16,20},{1,17},{... | collective-permute-start | bytes 98312 | tf_op jit(solution)/shard_map/ppermute | solution.py:38
  8.1 0.0 collective-permute-start.4
  8.2 1.0 %shard_map.103 = (f32[272,128]{1,0:T(8,128)S(1)}, f32[272,128]{1,0:T(8,128)S(1)}) custom-call(s32[11]{0:T(128)S(1)} %stack.56.flags.refs_0_, f32[64,128]{1,0:T(8,128)S(1)} %get-tuple-element.42.after, f32[12,3,32,128]{3,2,1,0:T(8,128)S(1)} %get-tuple-element.33.field, f32[12,3,32,128]{3,2,1,0:T(8,128)S(1)} %broadcast_multiply_fusion.kept, ...), custom_call_target="tpu_custom_call" | custom-call | tf_op jit(solution)/shard_map/pallas_call | solution.py:657
  9.1 0.5 %collective-permute-start.1 = (f32[272,128]{1,0:T(8,128)S(1)}, f32[272,128]{1,0:T(8,128)S(1)}, u32[]{:S(2)}, u32[]{:S(2)}) collective-permute-start(f32[272,128]{1,0:T(8,128)S(1)} %get-tuple-element.44), channel_id=1, source_target_pairs={{0,1},{1,0},{2,3},{3,2},{4,5},{5,4},{6,7},{7,6},{8,9},{9,8},{10,11... | collective-permute-start | bytes 417800 | tf_op jit(solution)/shard_map/ppermute | solution.py:17
  9.6 2.4 %collective-permute-done.4 = f32[64,128]{1,0:T(8,128)S(1)} collective-permute-done((f32[64,128]{1,0:T(8,128)S(1)}, f32[64,128]{1,0:T(8,128)S(1)}, u32[]{:S(2)}, u32[]{:S(2)}) %collective-permute-start.4) | collective-permute-done | bytes 32800 | tf_op jit(solution)/shard_map/ppermute | solution.py:17
  12.0 0.0 collective-permute-done.b
  12.1 2.5 %collective-permute-start.5 = (f32[208,128]{1,0:T(8,128)S(1)}, f32[208,128]{1,0:T(8,128)S(1)}, u32[]{:S(2)}, u32[]{:S(2)}) collective-permute-start(f32[208,128]{1,0:T(8,128)S(1)} %shard_map.101.first.refs_0_.a), channel_id=1, source_target_pairs={{0,3},{1,2},{2,1},{3,0},{4,7},{5,6},{6,5},{7,4},{8,11},{9,10},{10,... | collective-permute-start | bytes 319496 | tf_op jit(solution)/shard_map/ppermute | solution.py:17
  14.6 0.0 collective-permute-start.8
  14.6 1.0 %collective-permute-done.1.b = f32[272,128]{1,0:T(8,128)S(1)} collective-permute-done((f32[272,128]{1,0:T(8,128)S(1)}, f32[272,128]{1,0:T(8,128)S(1)}, u32[]{:S(2)}, u32[]{:S(2)}) %collective-permute-start.1) | collective-permute-done | bytes 139296 | tf_op jit(solution)/shard_map/ppermute | solution.py:17
  15.7 0.8 %collective-permute-start.7 = (f32[2,32,128]{2,1,0:T(8,128)S(1)}, f32[2,32,128]{2,1,0:T(8,128)S(1)}, u32[]{:S(2)}, u32[]{:S(2)}) collective-permute-start(f32[2,32,128]{2,1,0:T(8,128)S(1)} %shard_map.106), channel_id=1, source_target_pairs={{0,8},{4,12},{8,0},{12,4},{1,9},{5,13},{9,1},{13,5},{2,10},{6,14},... | collective-permute-start | bytes 98312 | tf_op jit(solution)/shard_map/ppermute | solution.py:17
  16.5 0.0 collective-permute-done.2.forward
  16.5 0.1 collective-permute-start.6
  16.6 0.0 collective-permute-done.3.back
  16.6 0.9 %shard_map.105 = (f32[72,128]{1,0:T(8,128)S(1)}, f32[5,3,32,128]{3,2,1,0:T(8,128)S(1)}, f32[2,64,128]{2,1,0:T(8,128)S(1)}, f32[128,128]{1,0:T(8,128)S(1)}) custom-call(s32[11]{0:T(128)S(1)} %stack.56.flags.refs_0_, f32[208,128]{1,0:T(8,128)S(1)} %shard_map.101.first.refs_0_.a, f32[272,128]{1,0:T(8,128)S(1)} %shard_map.104.second, ...), custom_call_target="tpu_custom_call" | custom-call | tf_op jit(solution)/shard_map/pallas_call | solution.py:657
  17.5 2.5 %collective-permute-start.10 = (f32[344,128]{1,0:T(8,128)S(1)}, f32[344,128]{1,0:T(8,128)S(1)}, u32[]{:S(2)}, u32[]{:S(2)}) collective-permute-start(f32[344,128]{1,0:T(8,128)S(1)} %pad_maximum_fusion.a), channel_id=1, source_target_pairs={{0,3},{1,2},{2,1},{3,0},{4,7},{5,6},{6,5},{7,4},{8,11},{9,10},{10,... | collective-permute-start | bytes 528392 | tf_op jit(solution)/shard_map/ppermute | solution.py:17
  20.1 0.0 collective-permute-done.8
  20.1 0.0 collective-permute-done.7
  20.1 0.0 collective-permute-done.6
  20.1 2.0 %shard_map.107 = (f32[9,32,128]{2,1,0:T(8,128)S(1)}, f32[8,128]{1,0:T(8,128)S(1)}, f32[72,128]{1,0:T(8,128)S(1)}) custom-call(s32[11]{0:T(128)S(1)} %stack.56.flags.refs_0_, f32[16,16,128]{2,1,0:T(8,128)S(1)} %bitcast.14, f32[3,32,128]{2,1,0:T(8,128)S(1)} %get-tuple-element.38.detrain.refs_2_, f32[3,32,128]{2,1,0:T(8,128)S(1)} %get-tuple-element.34.mix.refs_3_, ...), custom_call_target="tpu_custom_call" | custom-call | flops 20000000000 | tf_op jit(solution)/shard_map/pallas_call | solution.py:657
  22.1 0.0 collective-permute-done.5.b
  22.1 1.4 %collective-permute-start.9 = (f32[208,128]{1,0:T(8,128)S(1)}, f32[208,128]{1,0:T(8,128)S(1)}, u32[]{:S(2)}, u32[]{:S(2)}) collective-permute-start(f32[208,128]{1,0:T(8,128)S(1)} %shard_map.108.mine.refs_0_), channel_id=1, source_target_pairs={{0,1},{1,0},{2,3},{3,2},{4,5},{5,4},{6,7},{7,6},{8,9},{9,8},{10,11... | collective-permute-start | bytes 319496 | tf_op jit(solution)/shard_map/ppermute | solution.py:17
  23.6 2.3 %collective-permute-start.14 = (f32[72,128]{1,0:T(8,128)S(1)}, f32[72,128]{1,0:T(8,128)S(1)}, u32[]{:S(2)}, u32[]{:S(2)}) collective-permute-start(f32[72,128]{1,0:T(8,128)S(1)} %get-tuple-element.50.refs_0_.forced_1), channel_id=1, source_target_pairs={{0,3},{1,2},{2,1},{3,0},{4,7},{5,6},{6,5},{7,4},{8,11},{9,10},{10,... | collective-permute-start | bytes 110600 | tf_op jit(solution)/shard_map/ppermute | solution.py:17
  25.8 0.0 collective-permute-start.13
  25.8 2.1 %collective-permute-start.12 = (f32[72,128]{1,0:T(8,128)S(1)}, f32[72,128]{1,0:T(8,128)S(1)}, u32[]{:S(2)}, u32[]{:S(2)}) collective-permute-start(f32[72,128]{1,0:T(8,128)S(1)} %get-tuple-element.50.refs_0_.forced_1), channel_id=1, source_target_pairs={{0,1},{1,0},{2,3},{3,2},{4,5},{5,4},{6,7},{7,6},{8,9},{9,8},{10,11... | collective-permute-start | bytes 110600 | tf_op jit(solution)/shard_map/ppermute | solution.py:17
  28.0 0.0 collective-permute-done.10.b
  28.0 4.2 %collective-permute-start.11 = (f32[344,128]{1,0:T(8,128)S(1)}, f32[344,128]{1,0:T(8,128)S(1)}, u32[]{:S(2)}, u32[]{:S(2)}) collective-permute-start(f32[344,128]{1,0:T(8,128)S(1)} %shard_map.110.mine), channel_id=1, source_target_pairs={{0,1},{1,0},{2,3},{3,2},{4,5},{5,4},{6,7},{7,6},{8,9},{9,8},{10,11... | collective-permute-start | bytes 528392 | tf_op jit(solution)/shard_map/ppermute | solution.py:17
  32.2 0.0 collective-permute-done.9.other
  32.2 1.2 %shard_map.109 = (f32[12,3,32,128]{3,2,1,0:T(8,128)S(1)}, f32[12,32,128]{2,1,0:T(8,128)S(1)}, f32[32,128]{1,0:T(8,128)S(1)}) custom-call(s32[11]{0:T(128)S(1)} %stack.56.flags.refs_0_, f32[12,3,32,128]{3,2,1,0:T(8,128)S(1)} %get-tuple-element.33.field, f32[3,32,128]{2,1,0:T(8,128)S(1)} %get-tuple-element.34.mix.refs_3_, ...), custom_call_target="tpu_custom_call" | custom-call | flops 20000000000 | tf_op jit(solution)/shard_map/pallas_call | solution.py:657
  33.4 0.0 collective-permute-done.14.forced_4
  33.4 0.0 collective-permute-done.13.forced_3
  33.4 0.0 collective-permute-done.12.forced_2
  33.4 3.3 %collective-permute-done.11.other = f32[344,128]{1,0:T(8,128)S(1)} collective-permute-done((f32[344,128]{1,0:T(8,128)S(1)}, f32[344,128]{1,0:T(8,128)S(1)}, u32[]{:S(2)}, u32[]{:S(2)}) %collective-permute-start.11) | collective-permute-done | bytes 176160 | tf_op jit(solution)/shard_map/ppermute | solution.py:17
  36.7 1.5 %shard_map.111 = (f32[12,3,32,128]{3,2,1,0:T(8,128)S(1)}, f32[40,128]{1,0:T(8,128)S(1)}, f32[40,128]{1,0:T(8,128)S(1)}, f32[24,128]{1,0:T(8,128)S(1)}) custom-call(s32[11]{0:T(128)S(1)} %stack.56.flags.refs_0_, f32[12,3,32,128]{3,2,1,0:T(8,128)S(1)} %get-tuple-element.51.moved, f32[12,32,128]{2,1,0:T(8,128)S(1)} %get-tuple-element.52.column, ...), custom_call_target="tpu_custom_call" | custom-call | tf_op jit(solution)/shard_map/pallas_call | solution.py:657
  38.2 0.0 collective-permute-start.15
  38.2 2.0 %collective-permute-start.16 = (f32[40,128]{1,0:T(8,128)S(1)}, f32[40,128]{1,0:T(8,128)S(1)}, u32[]{:S(2)}, u32[]{:S(2)}) collective-permute-start(f32[40,128]{1,0:T(8,128)S(1)} %get-tuple-element.59), channel_id=1, source_target_pairs={{0,16},{4,0},{8,4},{12,8},{28,12},{24,28},{20,24},{16,20},{1,17},{... | collective-permute-start | bytes 61448 | tf_op jit(solution)/shard_map/ppermute | solution.py:38
  40.2 0.0 collective-permute-start.17
  40.3 0.9 %shard_map.112.inner = f32[12,3,32,128]{3,2,1,0:T(8,128)S(1)} custom-call(s32[11]{0:T(128)S(1)} %stack.56.flags.refs_0_, f32[12,3,32,128]{3,2,1,0:T(8,128)S(1)} %get-tuple-element.57.mixed, f32[5,3,32,128]{3,2,1,0:T(8,128)S(1)} %get-tuple-element.47.refs_4_.coefs), custom_call_target="tpu_custom_call" | custom-call | tf_op jit(solution)/shard_map/pallas_call | solution.py:657
  41.2 2.7 %collective-permute-done.17.eastern.western = f32[24,128]{1,0:T(8,128)S(1)} collective-permute-done((f32[24,128]{1,0:T(8,128)S(1)}, f32[24,128]{1,0:T(8,128)S(1)}, u32[]{:S(2)}, u32[]{:S(2)}) %collective-permute-start.17) | collective-permute-done | bytes 12320 | tf_op jit(solution)/shard_map/ppermute | solution.py:17
  43.9 0.0 collective-permute-done.15.forward
  43.9 0.0 collective-permute-done.16.back
  43.9 1.6 %shard_map.113 = f32[12,3,32,128]{3,2,1,0:T(8,128)} custom-call(s32[11]{0:T(128)S(1)} %stack.56.flags.refs_0_, f32[12,3,32,128]{3,2,1,0:T(8,128)S(1)} %shard_map.112.inner, f32[5,3,32,128]{3,2,1,0:T(8,128)S(1)} %get-tuple-element.47.refs_4_.coefs, f32[40,128]{1,0:T(8,128)S(1)} %collective-permute-done.15.forward, ...), custom_call_target="tpu_custom_call" | custom-call | tf_op jit(solution)/shard_map/pallas_call | solution.py:657
  (11 shorter events, 0.2 us)
Async XLA Ops:
  2.0 10.0 %collective-permute-start = (f32[208,128]{1,0:T(8,128)S(1)}, f32[208,128]{1,0:T(8,128)S(1)}, u32[]{:S(2)}, u32[]{:S(2)}) collective-permute-start(f32[208,128]{1,0:T(8,128)S(1)} %get-tuple-element.36), channel_id=1, source_target_pairs={{0,1},{1,0},{2,3},{3,2},{4,5},{5,4},{6,7},{7,6},{8,9},{9,8},{10,11... | collective-permute-start | bytes 319496 | tf_op jit(solution)/shard_map/ppermute | solution.py:17
  6.1 10.4 %collective-permute-start.2 = (f32[64,128]{1,0:T(8,128)S(1)}, f32[64,128]{1,0:T(8,128)S(1)}, u32[]{:S(2)}, u32[]{:S(2)}) collective-permute-start(f32[64,128]{1,0:T(8,128)S(1)} %get-tuple-element.45.own_forward), channel_id=1, source_target_pairs={{0,4},{4,8},{8,12},{12,28},{28,24},{24,20},{20,16},{16,0},{1,5},{5... | collective-permute-start | bytes 98312 | tf_op jit(solution)/shard_map/ppermute | solution.py:37
  6.1 10.5 %collective-permute-start.3 = (f32[64,128]{1,0:T(8,128)S(1)}, f32[64,128]{1,0:T(8,128)S(1)}, u32[]{:S(2)}, u32[]{:S(2)}) collective-permute-start(f32[64,128]{1,0:T(8,128)S(1)} %get-tuple-element.46.own_back), channel_id=1, source_target_pairs={{0,16},{4,0},{8,4},{12,8},{28,12},{24,28},{20,24},{16,20},{1,17},{... | collective-permute-start | bytes 98312 | tf_op jit(solution)/shard_map/ppermute | solution.py:38
  8.1 3.9 %collective-permute-start.4 = (f32[64,128]{1,0:T(8,128)S(1)}, f32[64,128]{1,0:T(8,128)S(1)}, u32[]{:S(2)}, u32[]{:S(2)}) collective-permute-start(f32[64,128]{1,0:T(8,128)S(1)} %get-tuple-element.42.after), channel_id=1, source_target_pairs={{0,16},{16,0},{1,17},{17,1},{2,18},{18,2},{3,19},{19,3},{4,20},{20... | collective-permute-start | bytes 98312 | tf_op jit(solution)/shard_map/ppermute | solution.py:17
  9.1 6.5 %collective-permute-start.1 = (f32[272,128]{1,0:T(8,128)S(1)}, f32[272,128]{1,0:T(8,128)S(1)}, u32[]{:S(2)}, u32[]{:S(2)}) collective-permute-start(f32[272,128]{1,0:T(8,128)S(1)} %get-tuple-element.44), channel_id=1, source_target_pairs={{0,1},{1,0},{2,3},{3,2},{4,5},{5,4},{6,7},{7,6},{8,9},{9,8},{10,11... | collective-permute-start | bytes 417800 | tf_op jit(solution)/shard_map/ppermute | solution.py:17
  12.1 10.0 %collective-permute-start.5 = (f32[208,128]{1,0:T(8,128)S(1)}, f32[208,128]{1,0:T(8,128)S(1)}, u32[]{:S(2)}, u32[]{:S(2)}) collective-permute-start(f32[208,128]{1,0:T(8,128)S(1)} %shard_map.101.first.refs_0_.a), channel_id=1, source_target_pairs={{0,3},{1,2},{2,1},{3,0},{4,7},{5,6},{6,5},{7,4},{8,11},{9,10},{10,... | collective-permute-start | bytes 319496 | tf_op jit(solution)/shard_map/ppermute | solution.py:17
  14.6 5.5 %collective-permute-start.8 = (f32[2,32,128]{2,1,0:T(8,128)S(1)}, f32[2,32,128]{2,1,0:T(8,128)S(1)}, u32[]{:S(2)}, u32[]{:S(2)}) collective-permute-start(f32[2,32,128]{2,1,0:T(8,128)S(1)} %shard_map.106), channel_id=1, source_target_pairs={{0,12},{4,8},{8,4},{12,0},{1,13},{5,9},{9,5},{13,1},{2,14},{6,10},... | collective-permute-start | bytes 98312 | tf_op jit(solution)/shard_map/ppermute | solution.py:17
  15.7 4.4 %collective-permute-start.7 = (f32[2,32,128]{2,1,0:T(8,128)S(1)}, f32[2,32,128]{2,1,0:T(8,128)S(1)}, u32[]{:S(2)}, u32[]{:S(2)}) collective-permute-start(f32[2,32,128]{2,1,0:T(8,128)S(1)} %shard_map.106), channel_id=1, source_target_pairs={{0,8},{4,12},{8,0},{12,4},{1,9},{5,13},{9,1},{13,5},{2,10},{6,14},... | collective-permute-start | bytes 98312 | tf_op jit(solution)/shard_map/ppermute | solution.py:17
  16.5 3.6 %collective-permute-start.6 = (f32[2,32,128]{2,1,0:T(8,128)S(1)}, f32[2,32,128]{2,1,0:T(8,128)S(1)}, u32[]{:S(2)}, u32[]{:S(2)}) collective-permute-start(f32[2,32,128]{2,1,0:T(8,128)S(1)} %shard_map.106), channel_id=1, source_target_pairs={{0,4},{4,0},{8,12},{12,8},{1,5},{5,1},{9,13},{13,9},{2,6},{6,2},{1... | collective-permute-start | bytes 98312 | tf_op jit(solution)/shard_map/ppermute | solution.py:17
  17.5 10.4 %collective-permute-start.10 = (f32[344,128]{1,0:T(8,128)S(1)}, f32[344,128]{1,0:T(8,128)S(1)}, u32[]{:S(2)}, u32[]{:S(2)}) collective-permute-start(f32[344,128]{1,0:T(8,128)S(1)} %pad_maximum_fusion.a), channel_id=1, source_target_pairs={{0,3},{1,2},{2,1},{3,0},{4,7},{5,6},{6,5},{7,4},{8,11},{9,10},{10,... | collective-permute-start | bytes 528392 | tf_op jit(solution)/shard_map/ppermute | solution.py:17
  22.1 10.1 %collective-permute-start.9 = (f32[208,128]{1,0:T(8,128)S(1)}, f32[208,128]{1,0:T(8,128)S(1)}, u32[]{:S(2)}, u32[]{:S(2)}) collective-permute-start(f32[208,128]{1,0:T(8,128)S(1)} %shard_map.108.mine.refs_0_), channel_id=1, source_target_pairs={{0,1},{1,0},{2,3},{3,2},{4,5},{5,4},{6,7},{7,6},{8,9},{9,8},{10,11... | collective-permute-start | bytes 319496 | tf_op jit(solution)/shard_map/ppermute | solution.py:17
  23.6 9.8 %collective-permute-start.14 = (f32[72,128]{1,0:T(8,128)S(1)}, f32[72,128]{1,0:T(8,128)S(1)}, u32[]{:S(2)}, u32[]{:S(2)}) collective-permute-start(f32[72,128]{1,0:T(8,128)S(1)} %get-tuple-element.50.refs_0_.forced_1), channel_id=1, source_target_pairs={{0,3},{1,2},{2,1},{3,0},{4,7},{5,6},{6,5},{7,4},{8,11},{9,10},{10,... | collective-permute-start | bytes 110600 | tf_op jit(solution)/shard_map/ppermute | solution.py:17
  25.8 7.5 %collective-permute-start.13 = (f32[72,128]{1,0:T(8,128)S(1)}, f32[72,128]{1,0:T(8,128)S(1)}, u32[]{:S(2)}, u32[]{:S(2)}) collective-permute-start(f32[72,128]{1,0:T(8,128)S(1)} %get-tuple-element.50.refs_0_.forced_1), channel_id=1, source_target_pairs={{0,2},{1,3},{2,0},{3,1},{4,6},{5,7},{6,4},{7,5},{8,10},{9,11},{10,... | collective-permute-start | bytes 110600 | tf_op jit(solution)/shard_map/ppermute | solution.py:17
  25.8 7.6 %collective-permute-start.12 = (f32[72,128]{1,0:T(8,128)S(1)}, f32[72,128]{1,0:T(8,128)S(1)}, u32[]{:S(2)}, u32[]{:S(2)}) collective-permute-start(f32[72,128]{1,0:T(8,128)S(1)} %get-tuple-element.50.refs_0_.forced_1), channel_id=1, source_target_pairs={{0,1},{1,0},{2,3},{3,2},{4,5},{5,4},{6,7},{7,6},{8,9},{9,8},{10,11... | collective-permute-start | bytes 110600 | tf_op jit(solution)/shard_map/ppermute | solution.py:17
  28.0 8.7 %collective-permute-start.11 = (f32[344,128]{1,0:T(8,128)S(1)}, f32[344,128]{1,0:T(8,128)S(1)}, u32[]{:S(2)}, u32[]{:S(2)}) collective-permute-start(f32[344,128]{1,0:T(8,128)S(1)} %shard_map.110.mine), channel_id=1, source_target_pairs={{0,1},{1,0},{2,3},{3,2},{4,5},{5,4},{6,7},{7,6},{8,9},{9,8},{10,11... | collective-permute-start | bytes 528392 | tf_op jit(solution)/shard_map/ppermute | solution.py:17
  38.2 5.8 %collective-permute-start.15 = (f32[40,128]{1,0:T(8,128)S(1)}, f32[40,128]{1,0:T(8,128)S(1)}, u32[]{:S(2)}, u32[]{:S(2)}) collective-permute-start(f32[40,128]{1,0:T(8,128)S(1)} %get-tuple-element.58), channel_id=1, source_target_pairs={{0,4},{4,8},{8,12},{12,28},{28,24},{24,20},{20,16},{16,0},{1,5},{5... | collective-permute-start | bytes 61448 | tf_op jit(solution)/shard_map/ppermute | solution.py:37
  38.2 5.7 %collective-permute-start.16 = (f32[40,128]{1,0:T(8,128)S(1)}, f32[40,128]{1,0:T(8,128)S(1)}, u32[]{:S(2)}, u32[]{:S(2)}) collective-permute-start(f32[40,128]{1,0:T(8,128)S(1)} %get-tuple-element.59), channel_id=1, source_target_pairs={{0,16},{4,0},{8,4},{12,8},{28,12},{24,28},{20,24},{16,20},{1,17},{... | collective-permute-start | bytes 61448 | tf_op jit(solution)/shard_map/ppermute | solution.py:38
  40.2 3.7 %collective-permute-start.17 = (f32[24,128]{1,0:T(8,128)S(1)}, f32[24,128]{1,0:T(8,128)S(1)}, u32[]{:S(2)}, u32[]{:S(2)}) collective-permute-start(f32[24,128]{1,0:T(8,128)S(1)} %get-tuple-element.60), channel_id=1, source_target_pairs={{0,16},{16,0},{1,17},{17,1},{2,18},{18,2},{3,19},{19,3},{4,20},{20... | collective-permute-start | bytes 36872 | tf_op jit(solution)/shard_map/ppermute | solution.py:17

commit v4 on v3

--- a/solution.py
+++ b/solution.py
@@ -10,7 +10,7 @@
 F32 = jnp.float32
 WEIGHTS = [0, 0, 0, 20, 20]
 LANES = 128
-TOP, BOTTOM, ASCENDING, PARITY, SELF, NORTH, SOUTH, EAST, WEST, NORTH_ROW, SOUTH_ROW = range(11)
+TOP, BOTTOM, ASCENDING, PARITY, SELF, NORTH, SOUTH, EAST, WEST, NORTH_ROW, SOUTH_ROW, LATER_PARITY = range(12)
 
 
 def swap_over(value, axis, bit):
@@ -230,7 +230,7 @@
                 total = c * x if total is None else total + c * x
         at = (t % half) * rows
         halves[t // half, at : at + rows, :] = total
-    parity = flags[PARITY]
+    parity = flags[LATER_PARITY]
     keep[...] = halves[parity]
     send[...] = halves[1 - parity]
 
@@ -500,7 +500,7 @@
     per = LANES // rows
     group = -(-base // per)
     groups = tracers // per
-    parity = flags[PARITY]
+    parity = flags[LATER_PARITY]
     second_rows = second.shape[1]
     second[parity] = mine[:second_rows]
     second[1 - parity] = other[:second_rows]
@@ -693,7 +693,7 @@
         top,
         bottom,
         lon < lon_count // 2,
-        (lev ^ (lev >> 1)) & 1,
+        lev & 1,
         lon * lat_count + lat,
         jnp.where(top, partner * lat_count + lat, lon * lat_count + lat + 1),
         jnp.where(bottom, partner * lat_count + lat, lon * lat_count + lat - 1),
@@ -701,6 +701,7 @@
         (lon + lon_count - 1) % lon_count * lat_count + lat,
         jnp.where(top, rows - 1, 0),
         jnp.where(bottom, 0, rows - 1),
+        (lev ^ (lev >> 1)) & 1,
     ]
     flags = jnp.stack([jnp.asarray(flag, jnp.int32) for flag in flags])
 
@@ -748,7 +749,7 @@
     second = add(keep_second, swap_over(send_second, "lev", 1))
     eastern, western = exchange_columns(columns)
     forward, back = exchange_rows(own_forward, own_back)
-    other_first = swap_over(first, "lev", 3)
+    other_first = swap_over(first, "lev", 2)
 
     late_rows = 2 * (-(-base // per) - slabs // per) + 2 * (tracers // per) + 8 + 4 * tracers + 2
     late, coefs, edges, turned = call(

time: 45.7 us -> 45.2 us (0.989)
  starting transfers between devices: 23.7 us -> 20 us
  waiting for transfers between devices: 9.53 us -> 12.8 us
    ppermute x14, starting transfers between devices: 19.6 us -> 15.9 us  [swap_over(): lax.ppermute(value, axis, [(i, i ^ bit) for i in range(lax.axis_size(axis...]
    ppermute x14, waiting for transfers between devices: 9.52 us -> 12.8 us  [swap_over(): lax.ppermute(value, axis, [(i, i ^ bit) for i in range(lax.axis_size(axis...]
  transfers between devices with their start and end apart: 18 -> 18, of which waited for: 4 -> 6; matrix products, arithmetic and copies ran while one was open for 0% -> 0% of each run, Pallas kernels for 15% -> 15%
where the time goes in v4:
time: 45.2 us; the launch traced here: 45 us
  starting transfers between devices  20 us (44%)
  waiting for transfers between devices  12.8 us (28%)
  Pallas kernels  11.9 us (26%)
    ppermute x14, starting transfers between devices, swap_over(): lax.ppermute(value, axis, [(i, i ^ bit) for i in range(lax.axis_size(axis...  15.9 us
    ppermute x14, waiting for transfers between devices, swap_over(): lax.ppermute(value, axis, [(i, i ^ bit) for i in range(lax.axis_size(axis...  12.8 us
    pallas_call x9, Pallas kernels, call(): pl.pallas_call(kernel, out_shape=[jax.ShapeDtypeStruct(shape, F32) for sh...  11.9 us
    ppermute x2, starting transfers between devices, exchange_rows(): lax.ppermute(back, ('lon', 'lat'), meridian_rings(lon_count, lat_count, -1))  4.03 us
  transfers between devices with their start and end apart: 18, of which 6 were waited for; matrix products, arithmetic and copies ran while one was open for 0% of the time, Pallas kernels for 15%

profile of v4, /device:TPU:0, one launch (start us, length us, event | category | flops | bytes accessed | tf_op | source)
XLA Modules:
  0.0 45.0 jit_solution(16527662742808355062)
XLA Ops:
  0.0 0.1 stack.60.flags.refs_0_
  0.1 1.9 %shard_map.100 = (f32[208,128]{1,0:T(8,128)S(1)}, f32[208,128]{1,0:T(8,128)S(1)}, f32[32,128]{1,0:T(8,128)S(1)}, f32[3,32,128]{2,1,0:T(8,128)S(1)}, f32[12,3,32,...) custom-call(s32[12]{0:T(128)S(1)} %stack.60.flags.refs_0_, ...), custom_call_target="tpu_custom_call" | custom-call | tf_op jit(solution)/shard_map/pallas_call | solution.py:657
  2.0 3.1 %collective-permute-start = (f32[208,128]{1,0:T(8,128)S(1)}, f32[208,128]{1,0:T(8,128)S(1)}, u32[]{:S(2)}, u32[]{:S(2)}) collective-permute-start(f32[208,128]{1,0:T(8,128)S(1)} %get-tuple-element.36), channel_id=1, source_target_pairs={{0,1},{1,0},{2,3},{3,2},{4,5},{5,4},{6,7},{7,6},{8,9},{9,8},{10,11... | collective-permute-start | bytes 319496 | tf_op jit(solution)/shard_map/ppermute | solution.py:17
  5.2 0.9 %shard_map.102 = (f32[64,128]{1,0:T(8,128)S(1)}, f32[64,128]{1,0:T(8,128)S(1)}, f32[64,128]{1,0:T(8,128)S(1)}) custom-call(s32[12]{0:T(128)S(1)} %stack.60.flags.refs_0_, f32[32,128]{1,0:T(8,128)S(1)} %get-tuple-element.37.slots, f32[12,3,32,128]{3,2,1,0:T(8,128)S(1)} %get-tuple-element.33.field, f32[12,3,32,128]{3,2,1,0:T(8,128)S(1)} %broadcast_multiply_fusion.kept, ...), custom_call_target="tpu_custom_call" | custom-call | tf_op jit(solution)/shard_map/pallas_call | solution.py:657
  6.1 0.0 collective-permute-start.2
  6.1 2.0 %collective-permute-start.3 = (f32[64,128]{1,0:T(8,128)S(1)}, f32[64,128]{1,0:T(8,128)S(1)}, u32[]{:S(2)}, u32[]{:S(2)}) collective-permute-start(f32[64,128]{1,0:T(8,128)S(1)} %get-tuple-element.46.own_back), channel_id=1, source_target_pairs={{0,16},{4,0},{8,4},{12,8},{28,12},{24,28},{20,24},{16,20},{1,17},{... | collective-permute-start | bytes 98312 | tf_op jit(solution)/shard_map/ppermute | solution.py:38
  8.1 0.0 collective-permute-start.4
  8.2 1.0 %shard_map.103 = (f32[272,128]{1,0:T(8,128)S(1)}, f32[272,128]{1,0:T(8,128)S(1)}) custom-call(s32[12]{0:T(128)S(1)} %stack.60.flags.refs_0_, f32[64,128]{1,0:T(8,128)S(1)} %get-tuple-element.42.after, f32[12,3,32,128]{3,2,1,0:T(8,128)S(1)} %get-tuple-element.33.field, f32[12,3,32,128]{3,2,1,0:T(8,128)S(1)} %broadcast_multiply_fusion.kept, ...), custom_call_target="tpu_custom_call" | custom-call | tf_op jit(solution)/shard_map/pallas_call | solution.py:657
  9.2 0.5 %collective-permute-start.1 = (f32[272,128]{1,0:T(8,128)S(1)}, f32[272,128]{1,0:T(8,128)S(1)}, u32[]{:S(2)}, u32[]{:S(2)}) collective-permute-start(f32[272,128]{1,0:T(8,128)S(1)} %get-tuple-element.44), channel_id=1, source_target_pairs={{0,1},{1,0},{2,3},{3,2},{4,5},{5,4},{6,7},{7,6},{8,9},{9,8},{10,11... | collective-permute-start | bytes 417800 | tf_op jit(solution)/shard_map/ppermute | solution.py:17
  9.6 2.4 %collective-permute-done.4 = f32[64,128]{1,0:T(8,128)S(1)} collective-permute-done((f32[64,128]{1,0:T(8,128)S(1)}, f32[64,128]{1,0:T(8,128)S(1)}, u32[]{:S(2)}, u32[]{:S(2)}) %collective-permute-start.4) | collective-permute-done | bytes 32800 | tf_op jit(solution)/shard_map/ppermute | solution.py:17
  12.0 0.0 collective-permute-done.b
  12.1 2.7 %collective-permute-start.5 = (f32[208,128]{1,0:T(8,128)S(1)}, f32[208,128]{1,0:T(8,128)S(1)}, u32[]{:S(2)}, u32[]{:S(2)}) collective-permute-start(f32[208,128]{1,0:T(8,128)S(1)} %shard_map.101.first.refs_0_.a), channel_id=1, source_target_pairs={{0,2},{1,3},{2,0},{3,1},{4,6},{5,7},{6,4},{7,5},{8,10},{9,11},{10,... | collective-permute-start | bytes 319496 | tf_op jit(solution)/shard_map/ppermute | solution.py:17
  14.7 0.0 collective-permute-start.8
  14.7 3.1 %collective-permute-done.1.b = f32[272,128]{1,0:T(8,128)S(1)} collective-permute-done((f32[272,128]{1,0:T(8,128)S(1)}, f32[272,128]{1,0:T(8,128)S(1)}, u32[]{:S(2)}, u32[]{:S(2)}) %collective-permute-start.1) | collective-permute-done | bytes 139296 | tf_op jit(solution)/shard_map/ppermute | solution.py:17
  17.9 0.0 collective-permute-start.7
  17.9 0.0 collective-permute-done.2.forward
  17.9 0.1 collective-permute-start.6
  18.0 0.0 collective-permute-done.3.back
  18.0 0.9 %shard_map.105 = (f32[72,128]{1,0:T(8,128)S(1)}, f32[5,3,32,128]{3,2,1,0:T(8,128)S(1)}, f32[2,64,128]{2,1,0:T(8,128)S(1)}, f32[128,128]{1,0:T(8,128)S(1)}) custom-call(s32[12]{0:T(128)S(1)} %stack.60.flags.refs_0_, f32[208,128]{1,0:T(8,128)S(1)} %shard_map.101.first.refs_0_.a, f32[272,128]{1,0:T(8,128)S(1)} %shard_map.104.second, ...), custom_call_target="tpu_custom_call" | custom-call | tf_op jit(solution)/shard_map/pallas_call | solution.py:657
  18.9 1.7 %collective-permute-start.10 = (f32[344,128]{1,0:T(8,128)S(1)}, f32[344,128]{1,0:T(8,128)S(1)}, u32[]{:S(2)}, u32[]{:S(2)}) collective-permute-start(f32[344,128]{1,0:T(8,128)S(1)} %pad_maximum_fusion.a), channel_id=1, source_target_pairs={{0,3},{1,2},{2,1},{3,0},{4,7},{5,6},{6,5},{7,4},{8,11},{9,10},{10,... | collective-permute-start | bytes 528392 | tf_op jit(solution)/shard_map/ppermute | solution.py:17
  20.6 0.0 collective-permute-done.8
  20.6 1.2 %collective-permute-done.7 = f32[2,32,128]{2,1,0:T(8,128)S(1)} collective-permute-done((f32[2,32,128]{2,1,0:T(8,128)S(1)}, f32[2,32,128]{2,1,0:T(8,128)S(1)}, u32[]{:S(2)}, u32[]{:S(2)}) %collective-permute-start.7) | collective-permute-done | bytes 32800 | tf_op jit(solution)/shard_map/ppermute | solution.py:17
  21.8 0.0 collective-permute-done.6
  21.8 2.0 %shard_map.107 = (f32[9,32,128]{2,1,0:T(8,128)S(1)}, f32[8,128]{1,0:T(8,128)S(1)}, f32[72,128]{1,0:T(8,128)S(1)}) custom-call(s32[12]{0:T(128)S(1)} %stack.60.flags.refs_0_, f32[16,16,128]{2,1,0:T(8,128)S(1)} %bitcast.15, f32[3,32,128]{2,1,0:T(8,128)S(1)} %get-tuple-element.38.detrain.refs_2_, f32[3,32,128]{2,1,0:T(8,128)S(1)} %get-tuple-element.34.mix.refs_3_, ...), custom_call_target="tpu_custom_call" | custom-call | flops 20000000000 | tf_op jit(solution)/shard_map/pallas_call | solution.py:657
  23.8 0.0 collective-permute-done.5.b
  23.8 0.1 collective-permute-start.9
  23.9 1.9 %collective-permute-start.14 = (f32[72,128]{1,0:T(8,128)S(1)}, f32[72,128]{1,0:T(8,128)S(1)}, u32[]{:S(2)}, u32[]{:S(2)}) collective-permute-start(f32[72,128]{1,0:T(8,128)S(1)} %get-tuple-element.50.refs_0_.forced_1), channel_id=1, source_target_pairs={{0,3},{1,2},{2,1},{3,0},{4,7},{5,6},{6,5},{7,4},{8,11},{9,10},{10,... | collective-permute-start | bytes 110600 | tf_op jit(solution)/shard_map/ppermute | solution.py:17
  25.9 1.5 %collective-permute-start.13 = (f32[72,128]{1,0:T(8,128)S(1)}, f32[72,128]{1,0:T(8,128)S(1)}, u32[]{:S(2)}, u32[]{:S(2)}) collective-permute-start(f32[72,128]{1,0:T(8,128)S(1)} %get-tuple-element.50.refs_0_.forced_1), channel_id=1, source_target_pairs={{0,2},{1,3},{2,0},{3,1},{4,6},{5,7},{6,4},{7,5},{8,10},{9,11},{10,... | collective-permute-start | bytes 110600 | tf_op jit(solution)/shard_map/ppermute | solution.py:17
  27.4 1.0 %collective-permute-start.12 = (f32[72,128]{1,0:T(8,128)S(1)}, f32[72,128]{1,0:T(8,128)S(1)}, u32[]{:S(2)}, u32[]{:S(2)}) collective-permute-start(f32[72,128]{1,0:T(8,128)S(1)} %get-tuple-element.50.refs_0_.forced_1), channel_id=1, source_target_pairs={{0,1},{1,0},{2,3},{3,2},{4,5},{5,4},{6,7},{7,6},{8,9},{9,8},{10,11... | collective-permute-start | bytes 110600 | tf_op jit(solution)/shard_map/ppermute | solution.py:17
  28.4 0.0 collective-permute-done.10.b
  28.4 3.3 %collective-permute-start.11 = (f32[344,128]{1,0:T(8,128)S(1)}, f32[344,128]{1,0:T(8,128)S(1)}, u32[]{:S(2)}, u32[]{:S(2)}) collective-permute-start(f32[344,128]{1,0:T(8,128)S(1)} %shard_map.110.mine), channel_id=1, source_target_pairs={{0,1},{1,0},{2,3},{3,2},{4,5},{5,4},{6,7},{7,6},{8,9},{9,8},{10,11... | collective-permute-start | bytes 528392 | tf_op jit(solution)/shard_map/ppermute | solution.py:17
  31.7 0.0 collective-permute-done.9.other
  31.7 1.2 %shard_map.109 = (f32[12,3,32,128]{3,2,1,0:T(8,128)S(1)}, f32[12,32,128]{2,1,0:T(8,128)S(1)}, f32[32,128]{1,0:T(8,128)S(1)}) custom-call(s32[12]{0:T(128)S(1)} %stack.60.flags.refs_0_, f32[12,3,32,128]{3,2,1,0:T(8,128)S(1)} %get-tuple-element.33.field, f32[3,32,128]{2,1,0:T(8,128)S(1)} %get-tuple-element.34.mix.refs_3_, ...), custom_call_target="tpu_custom_call" | custom-call | flops 20000000000 | tf_op jit(solution)/shard_map/pallas_call | solution.py:657
  32.9 0.0 collective-permute-done.14.forced_4
  32.9 0.2 collective-permute-done.13.forced_3
  33.0 0.0 collective-permute-done.12.forced_2
  33.0 3.1 %collective-permute-done.11.other = f32[344,128]{1,0:T(8,128)S(1)} collective-permute-done((f32[344,128]{1,0:T(8,128)S(1)}, f32[344,128]{1,0:T(8,128)S(1)}, u32[]{:S(2)}, u32[]{:S(2)}) %collective-permute-start.11) | collective-permute-done | bytes 176160 | tf_op jit(solution)/shard_map/ppermute | solution.py:17
  36.1 1.5 %shard_map.111 = (f32[12,3,32,128]{3,2,1,0:T(8,128)S(1)}, f32[40,128]{1,0:T(8,128)S(1)}, f32[40,128]{1,0:T(8,128)S(1)}, f32[24,128]{1,0:T(8,128)S(1)}) custom-call(s32[12]{0:T(128)S(1)} %stack.60.flags.refs_0_, f32[12,3,32,128]{3,2,1,0:T(8,128)S(1)} %get-tuple-element.51.moved, f32[12,32,128]{2,1,0:T(8,128)S(1)} %get-tuple-element.52.column, ...), custom_call_target="tpu_custom_call" | custom-call | tf_op jit(solution)/shard_map/pallas_call | solution.py:657
  37.6 0.0 collective-permute-start.15
  37.7 2.0 %collective-permute-start.16 = (f32[40,128]{1,0:T(8,128)S(1)}, f32[40,128]{1,0:T(8,128)S(1)}, u32[]{:S(2)}, u32[]{:S(2)}) collective-permute-start(f32[40,128]{1,0:T(8,128)S(1)} %get-tuple-element.59), channel_id=1, source_target_pairs={{0,16},{4,0},{8,4},{12,8},{28,12},{24,28},{20,24},{16,20},{1,17},{... | collective-permute-start | bytes 61448 | tf_op jit(solution)/shard_map/ppermute | solution.py:38
  39.7 0.0 collective-permute-start.17
  39.7 0.9 %shard_map.112.inner = f32[12,3,32,128]{3,2,1,0:T(8,128)S(1)} custom-call(s32[12]{0:T(128)S(1)} %stack.60.flags.refs_0_, f32[12,3,32,128]{3,2,1,0:T(8,128)S(1)} %get-tuple-element.57.mixed, f32[5,3,32,128]{3,2,1,0:T(8,128)S(1)} %get-tuple-element.47.refs_4_.coefs), custom_call_target="tpu_custom_call" | custom-call | tf_op jit(solution)/shard_map/pallas_call | solution.py:657
  40.6 2.7 %collective-permute-done.17.eastern.western = f32[24,128]{1,0:T(8,128)S(1)} collective-permute-done((f32[24,128]{1,0:T(8,128)S(1)}, f32[24,128]{1,0:T(8,128)S(1)}, u32[]{:S(2)}, u32[]{:S(2)}) %collective-permute-start.17) | collective-permute-done | bytes 12320 | tf_op jit(solution)/shard_map/ppermute | solution.py:17
  43.4 0.0 collective-permute-done.15.forward
  43.4 0.0 collective-permute-done.16.back
  43.4 1.6 %shard_map.113 = f32[12,3,32,128]{3,2,1,0:T(8,128)} custom-call(s32[12]{0:T(128)S(1)} %stack.60.flags.refs_0_, f32[12,3,32,128]{3,2,1,0:T(8,128)S(1)} %shard_map.112.inner, f32[5,3,32,128]{3,2,1,0:T(8,128)S(1)} %get-tuple-element.47.refs_4_.coefs, f32[40,128]{1,0:T(8,128)S(1)} %collective-permute-done.15.forward, ...), custom_call_target="tpu_custom_call" | custom-call | tf_op jit(solution)/shard_map/pallas_call | solution.py:657
  (11 shorter events, 0.2 us)
Async XLA Ops:
  2.0 10.0 %collective-permute-start = (f32[208,128]{1,0:T(8,128)S(1)}, f32[208,128]{1,0:T(8,128)S(1)}, u32[]{:S(2)}, u32[]{:S(2)}) collective-permute-start(f32[208,128]{1,0:T(8,128)S(1)} %get-tuple-element.36), channel_id=1, source_target_pairs={{0,1},{1,0},{2,3},{3,2},{4,5},{5,4},{6,7},{7,6},{8,9},{9,8},{10,11... | collective-permute-start | bytes 319496 | tf_op jit(solution)/shard_map/ppermute | solution.py:17
  6.1 11.8 %collective-permute-start.2 = (f32[64,128]{1,0:T(8,128)S(1)}, f32[64,128]{1,0:T(8,128)S(1)}, u32[]{:S(2)}, u32[]{:S(2)}) collective-permute-start(f32[64,128]{1,0:T(8,128)S(1)} %get-tuple-element.45.own_forward), channel_id=1, source_target_pairs={{0,4},{4,8},{8,12},{12,28},{28,24},{24,20},{20,16},{16,0},{1,5},{5... | collective-permute-start | bytes 98312 | tf_op jit(solution)/shard_map/ppermute | solution.py:37
  6.1 11.9 %collective-permute-start.3 = (f32[64,128]{1,0:T(8,128)S(1)}, f32[64,128]{1,0:T(8,128)S(1)}, u32[]{:S(2)}, u32[]{:S(2)}) collective-permute-start(f32[64,128]{1,0:T(8,128)S(1)} %get-tuple-element.46.own_back), channel_id=1, source_target_pairs={{0,16},{4,0},{8,4},{12,8},{28,12},{24,28},{20,24},{16,20},{1,17},{... | collective-permute-start | bytes 98312 | tf_op jit(solution)/shard_map/ppermute | solution.py:38
  8.1 3.9 %collective-permute-start.4 = (f32[64,128]{1,0:T(8,128)S(1)}, f32[64,128]{1,0:T(8,128)S(1)}, u32[]{:S(2)}, u32[]{:S(2)}) collective-permute-start(f32[64,128]{1,0:T(8,128)S(1)} %get-tuple-element.42.after), channel_id=1, source_target_pairs={{0,16},{16,0},{1,17},{17,1},{2,18},{18,2},{3,19},{19,3},{4,20},{20... | collective-permute-start | bytes 98312 | tf_op jit(solution)/shard_map/ppermute | solution.py:17
  9.2 8.7 %collective-permute-start.1 = (f32[272,128]{1,0:T(8,128)S(1)}, f32[272,128]{1,0:T(8,128)S(1)}, u32[]{:S(2)}, u32[]{:S(2)}) collective-permute-start(f32[272,128]{1,0:T(8,128)S(1)} %get-tuple-element.44), channel_id=1, source_target_pairs={{0,1},{1,0},{2,3},{3,2},{4,5},{5,4},{6,7},{7,6},{8,9},{9,8},{10,11... | collective-permute-start | bytes 417800 | tf_op jit(solution)/shard_map/ppermute | solution.py:17
  12.1 11.7 %collective-permute-start.5 = (f32[208,128]{1,0:T(8,128)S(1)}, f32[208,128]{1,0:T(8,128)S(1)}, u32[]{:S(2)}, u32[]{:S(2)}) collective-permute-start(f32[208,128]{1,0:T(8,128)S(1)} %shard_map.101.first.refs_0_.a), channel_id=1, source_target_pairs={{0,2},{1,3},{2,0},{3,1},{4,6},{5,7},{6,4},{7,5},{8,10},{9,11},{10,... | collective-permute-start | bytes 319496 | tf_op jit(solution)/shard_map/ppermute | solution.py:17
  14.7 5.9 %collective-permute-start.8 = (f32[2,32,128]{2,1,0:T(8,128)S(1)}, f32[2,32,128]{2,1,0:T(8,128)S(1)}, u32[]{:S(2)}, u32[]{:S(2)}) collective-permute-start(f32[2,32,128]{2,1,0:T(8,128)S(1)} %shard_map.106), channel_id=1, source_target_pairs={{0,12},{4,8},{8,4},{12,0},{1,13},{5,9},{9,5},{13,1},{2,14},{6,10},... | collective-permute-start | bytes 98312 | tf_op jit(solution)/shard_map/ppermute | solution.py:17
  17.9 3.9 %collective-permute-start.7 = (f32[2,32,128]{2,1,0:T(8,128)S(1)}, f32[2,32,128]{2,1,0:T(8,128)S(1)}, u32[]{:S(2)}, u32[]{:S(2)}) collective-permute-start(f32[2,32,128]{2,1,0:T(8,128)S(1)} %shard_map.106), channel_id=1, source_target_pairs={{0,8},{4,12},{8,0},{12,4},{1,9},{5,13},{9,1},{13,5},{2,10},{6,14},... | collective-permute-start | bytes 98312 | tf_op jit(solution)/shard_map/ppermute | solution.py:17
  17.9 3.9 %collective-permute-start.6 = (f32[2,32,128]{2,1,0:T(8,128)S(1)}, f32[2,32,128]{2,1,0:T(8,128)S(1)}, u32[]{:S(2)}, u32[]{:S(2)}) collective-permute-start(f32[2,32,128]{2,1,0:T(8,128)S(1)} %shard_map.106), channel_id=1, source_target_pairs={{0,4},{4,0},{8,12},{12,8},{1,5},{5,1},{9,13},{13,9},{2,6},{6,2},{1... | collective-permute-start | bytes 98312 | tf_op jit(solution)/shard_map/ppermute | solution.py:17
  18.9 9.5 %collective-permute-start.10 = (f32[344,128]{1,0:T(8,128)S(1)}, f32[344,128]{1,0:T(8,128)S(1)}, u32[]{:S(2)}, u32[]{:S(2)}) collective-permute-start(f32[344,128]{1,0:T(8,128)S(1)} %pad_maximum_fusion.a), channel_id=1, source_target_pairs={{0,3},{1,2},{2,1},{3,0},{4,7},{5,6},{6,5},{7,4},{8,11},{9,10},{10,... | collective-permute-start | bytes 528392 | tf_op jit(solution)/shard_map/ppermute | solution.py:17
  23.8 7.8 %collective-permute-start.9 = (f32[208,128]{1,0:T(8,128)S(1)}, f32[208,128]{1,0:T(8,128)S(1)}, u32[]{:S(2)}, u32[]{:S(2)}) collective-permute-start(f32[208,128]{1,0:T(8,128)S(1)} %shard_map.108.mine.refs_0_), channel_id=1, source_target_pairs={{0,1},{1,0},{2,3},{3,2},{4,5},{5,4},{6,7},{7,6},{8,9},{9,8},{10,11... | collective-permute-start | bytes 319496 | tf_op jit(solution)/shard_map/ppermute | solution.py:17
  23.9 8.9 %collective-permute-start.14 = (f32[72,128]{1,0:T(8,128)S(1)}, f32[72,128]{1,0:T(8,128)S(1)}, u32[]{:S(2)}, u32[]{:S(2)}) collective-permute-start(f32[72,128]{1,0:T(8,128)S(1)} %get-tuple-element.50.refs_0_.forced_1), channel_id=1, source_target_pairs={{0,3},{1,2},{2,1},{3,0},{4,7},{5,6},{6,5},{7,4},{8,11},{9,10},{10,... | collective-permute-start | bytes 110600 | tf_op jit(solution)/shard_map/ppermute | solution.py:17
  25.9 7.2 %collective-permute-start.13 = (f32[72,128]{1,0:T(8,128)S(1)}, f32[72,128]{1,0:T(8,128)S(1)}, u32[]{:S(2)}, u32[]{:S(2)}) collective-permute-start(f32[72,128]{1,0:T(8,128)S(1)} %get-tuple-element.50.refs_0_.forced_1), channel_id=1, source_target_pairs={{0,2},{1,3},{2,0},{3,1},{4,6},{5,7},{6,4},{7,5},{8,10},{9,11},{10,... | collective-permute-start | bytes 110600 | tf_op jit(solution)/shard_map/ppermute | solution.py:17
  27.4 5.6 %collective-permute-start.12 = (f32[72,128]{1,0:T(8,128)S(1)}, f32[72,128]{1,0:T(8,128)S(1)}, u32[]{:S(2)}, u32[]{:S(2)}) collective-permute-start(f32[72,128]{1,0:T(8,128)S(1)} %get-tuple-element.50.refs_0_.forced_1), channel_id=1, source_target_pairs={{0,1},{1,0},{2,3},{3,2},{4,5},{5,4},{6,7},{7,6},{8,9},{9,8},{10,11... | collective-permute-start | bytes 110600 | tf_op jit(solution)/shard_map/ppermute | solution.py:17
  28.4 7.8 %collective-permute-start.11 = (f32[344,128]{1,0:T(8,128)S(1)}, f32[344,128]{1,0:T(8,128)S(1)}, u32[]{:S(2)}, u32[]{:S(2)}) collective-permute-start(f32[344,128]{1,0:T(8,128)S(1)} %shard_map.110.mine), channel_id=1, source_target_pairs={{0,1},{1,0},{2,3},{3,2},{4,5},{5,4},{6,7},{7,6},{8,9},{9,8},{10,11... | collective-permute-start | bytes 528392 | tf_op jit(solution)/shard_map/ppermute | solution.py:17
  37.6 5.8 %collective-permute-start.15 = (f32[40,128]{1,0:T(8,128)S(1)}, f32[40,128]{1,0:T(8,128)S(1)}, u32[]{:S(2)}, u32[]{:S(2)}) collective-permute-start(f32[40,128]{1,0:T(8,128)S(1)} %get-tuple-element.58), channel_id=1, source_target_pairs={{0,4},{4,8},{8,12},{12,28},{28,24},{24,20},{20,16},{16,0},{1,5},{5... | collective-permute-start | bytes 61448 | tf_op jit(solution)/shard_map/ppermute | solution.py:37
  37.7 5.7 %collective-permute-start.16 = (f32[40,128]{1,0:T(8,128)S(1)}, f32[40,128]{1,0:T(8,128)S(1)}, u32[]{:S(2)}, u32[]{:S(2)}) collective-permute-start(f32[40,128]{1,0:T(8,128)S(1)} %get-tuple-element.59), channel_id=1, source_target_pairs={{0,16},{4,0},{8,4},{12,8},{28,12},{24,28},{20,24},{16,20},{1,17},{... | collective-permute-start | bytes 61448 | tf_op jit(solution)/shard_map/ppermute | solution.py:38
  39.7 3.7 %collective-permute-start.17 = (f32[24,128]{1,0:T(8,128)S(1)}, f32[24,128]{1,0:T(8,128)S(1)}, u32[]{:S(2)}, u32[]{:S(2)}) collective-permute-start(f32[24,128]{1,0:T(8,128)S(1)} %get-tuple-element.60), channel_id=1, source_target_pairs={{0,16},{16,0},{1,17},{17,1},{2,18},{18,2},{3,19},{19,3},{4,20},{20... | collective-permute-start | bytes 36872 | tf_op jit(solution)/shard_map/ppermute | solution.py:17

commit v5 on v4

--- a/solution.py
+++ b/solution.py
@@ -280,7 +280,7 @@
 
 
 def second_kernel(
-    tracers, levels, rows, flags, first, second, detrain, mix, east, north, pole,
+    tracers, levels, rows, flags, first, detrain, mix, east, north, pole,
     own_forward, own_back, own_columns, forward, back, eastern, western,
     late, coefs, edges, turned,
 ):
@@ -759,7 +759,7 @@
         + [own_forward, own_back, columns[:column_rows]]
         + [forward, back, eastern[:column_rows], western[:column_rows]],
         [(up8(late_rows), lanes), (5, levels, rows, lanes), (2, ring_rows, lanes), (lanes, lanes)],
-        placed=[first, second],
+        placed=[first],
         weight=WEIGHTS[2],
     )
     second = jnp.concatenate([second, late], axis=0)

time: 45.2 us -> 43.3 us (0.958)
  waiting for transfers between devices: 12.8 us -> 10.3 us
  starting transfers between devices: 20 us -> 20.6 us
    ppermute x14, waiting for transfers between devices: 12.8 us -> 10.3 us  [swap_over(): lax.ppermute(value, axis, [(i, i ^ bit) for i in range(lax.axis_size(axis...]
    ppermute x14, starting transfers between devices: 15.9 us -> 16.5 us  [swap_over(): lax.ppermute(value, axis, [(i, i ^ bit) for i in range(lax.axis_size(axis...]
  transfers between devices with their start and end apart: 18 -> 18, of which waited for: 6 -> 5; matrix products, arithmetic and copies ran while one was open for 0% -> 0% of each run, Pallas kernels for 15% -> 16%
where the time goes in v5:
time: 43.3 us; the launch traced here: 43.2 us
  starting transfers between devices  20.6 us (48%)
  Pallas kernels  11.9 us (27%)
  waiting for transfers between devices  10.3 us (24%)
    ppermute x14, starting transfers between devices, swap_over(): lax.ppermute(value, axis, [(i, i ^ bit) for i in range(lax.axis_size(axis...  16.5 us
    pallas_call x9, Pallas kernels, call(): pl.pallas_call(kernel, out_shape=[jax.ShapeDtypeStruct(shape, F32) for sh...  11.9 us
    ppermute x14, waiting for transfers between devices, swap_over(): lax.ppermute(value, axis, [(i, i ^ bit) for i in range(lax.axis_size(axis...  10.3 us
    ppermute x2, starting transfers between devices, exchange_rows(): lax.ppermute(back, ('lon', 'lat'), meridian_rings(lon_count, lat_count, -1))  4.03 us
  transfers between devices with their start and end apart: 18, of which 5 were waited for; matrix products, arithmetic and copies ran while one was open for 0% of the time, Pallas kernels for 16%

profile of v5, /device:TPU:0, one launch (start us, length us, event | category | flops | bytes accessed | tf_op | source)
XLA Modules:
  0.0 43.2 jit_solution(1898767251049357757)
XLA Ops:
  0.0 0.1 stack.60.flags.refs_0_
  0.1 1.9 %shard_map.100 = (f32[208,128]{1,0:T(8,128)S(1)}, f32[208,128]{1,0:T(8,128)S(1)}, f32[32,128]{1,0:T(8,128)S(1)}, f32[3,32,128]{2,1,0:T(8,128)S(1)}, f32[12,3,32,...) custom-call(s32[12]{0:T(128)S(1)} %stack.60.flags.refs_0_, ...), custom_call_target="tpu_custom_call" | custom-call | tf_op jit(solution)/shard_map/pallas_call | solution.py:657
  2.0 3.1 %collective-permute-start = (f32[208,128]{1,0:T(8,128)S(1)}, f32[208,128]{1,0:T(8,128)S(1)}, u32[]{:S(2)}, u32[]{:S(2)}) collective-permute-start(f32[208,128]{1,0:T(8,128)S(1)} %get-tuple-element.36), channel_id=1, source_target_pairs={{0,1},{1,0},{2,3},{3,2},{4,5},{5,4},{6,7},{7,6},{8,9},{9,8},{10,11... | collective-permute-start | bytes 319496 | tf_op jit(solution)/shard_map/ppermute | solution.py:17
  5.2 0.9 %shard_map.102 = (f32[64,128]{1,0:T(8,128)S(1)}, f32[64,128]{1,0:T(8,128)S(1)}, f32[64,128]{1,0:T(8,128)S(1)}) custom-call(s32[12]{0:T(128)S(1)} %stack.60.flags.refs_0_, f32[32,128]{1,0:T(8,128)S(1)} %get-tuple-element.41.slots, f32[12,3,32,128]{3,2,1,0:T(8,128)S(1)} %get-tuple-element.33.field, f32[12,3,32,128]{3,2,1,0:T(8,128)S(1)} %broadcast_multiply_fusion.kept, ...), custom_call_target="tpu_custom_call" | custom-call | tf_op jit(solution)/shard_map/pallas_call | solution.py:657
  6.1 0.0 collective-permute-start.1
  6.1 2.0 %collective-permute-start.2 = (f32[64,128]{1,0:T(8,128)S(1)}, f32[64,128]{1,0:T(8,128)S(1)}, u32[]{:S(2)}, u32[]{:S(2)}) collective-permute-start(f32[64,128]{1,0:T(8,128)S(1)} %get-tuple-element.43.own_back), channel_id=1, source_target_pairs={{0,16},{4,0},{8,4},{12,8},{28,12},{24,28},{20,24},{16,20},{1,17},{... | collective-permute-start | bytes 98312 | tf_op jit(solution)/shard_map/ppermute | solution.py:38
  8.1 0.0 collective-permute-start.3
  8.2 1.0 %shard_map.108 = (f32[272,128]{1,0:T(8,128)S(1)}, f32[272,128]{1,0:T(8,128)S(1)}) custom-call(s32[12]{0:T(128)S(1)} %stack.60.flags.refs_0_, f32[64,128]{1,0:T(8,128)S(1)} %get-tuple-element.44.after, f32[12,3,32,128]{3,2,1,0:T(8,128)S(1)} %get-tuple-element.33.field, f32[12,3,32,128]{3,2,1,0:T(8,128)S(1)} %broadcast_multiply_fusion.kept, ...), custom_call_target="tpu_custom_call" | custom-call | tf_op jit(solution)/shard_map/pallas_call | solution.py:657
  9.2 0.5 %collective-permute-start.9 = (f32[272,128]{1,0:T(8,128)S(1)}, f32[272,128]{1,0:T(8,128)S(1)}, u32[]{:S(2)}, u32[]{:S(2)}) collective-permute-start(f32[272,128]{1,0:T(8,128)S(1)} %get-tuple-element.55), channel_id=1, source_target_pairs={{0,1},{1,0},{2,3},{3,2},{4,5},{5,4},{6,7},{7,6},{8,9},{9,8},{10,11... | collective-permute-start | bytes 417800 | tf_op jit(solution)/shard_map/ppermute | solution.py:17
  9.6 2.4 %collective-permute-done.3 = f32[64,128]{1,0:T(8,128)S(1)} collective-permute-done((f32[64,128]{1,0:T(8,128)S(1)}, f32[64,128]{1,0:T(8,128)S(1)}, u32[]{:S(2)}, u32[]{:S(2)}) %collective-permute-start.3) | collective-permute-done | bytes 32800 | tf_op jit(solution)/shard_map/ppermute | solution.py:17
  12.0 0.0 collective-permute-done.b
  12.1 2.7 %collective-permute-start.4 = (f32[208,128]{1,0:T(8,128)S(1)}, f32[208,128]{1,0:T(8,128)S(1)}, u32[]{:S(2)}, u32[]{:S(2)}) collective-permute-start(f32[208,128]{1,0:T(8,128)S(1)} %shard_map.101.first.refs_0_.a), channel_id=1, source_target_pairs={{0,2},{1,3},{2,0},{3,1},{4,6},{5,7},{6,4},{7,5},{8,10},{9,11},{10,... | collective-permute-start | bytes 319496 | tf_op jit(solution)/shard_map/ppermute | solution.py:17
  14.7 0.0 collective-permute-start.7
  14.7 0.0 collective-permute-done.1.forward
  14.7 1.3 %collective-permute-start.6 = (f32[2,32,128]{2,1,0:T(8,128)S(1)}, f32[2,32,128]{2,1,0:T(8,128)S(1)}, u32[]{:S(2)}, u32[]{:S(2)}) collective-permute-start(f32[2,32,128]{2,1,0:T(8,128)S(1)} %shard_map.104), channel_id=1, source_target_pairs={{0,8},{4,12},{8,0},{12,4},{1,9},{5,13},{9,1},{13,5},{2,10},{6,14},... | collective-permute-start | bytes 98312 | tf_op jit(solution)/shard_map/ppermute | solution.py:17
  16.0 0.0 collective-permute-done.2.back
  16.0 0.6 %collective-permute-start.5 = (f32[2,32,128]{2,1,0:T(8,128)S(1)}, f32[2,32,128]{2,1,0:T(8,128)S(1)}, u32[]{:S(2)}, u32[]{:S(2)}) collective-permute-start(f32[2,32,128]{2,1,0:T(8,128)S(1)} %shard_map.104), channel_id=1, source_target_pairs={{0,4},{4,0},{8,12},{12,8},{1,5},{5,1},{9,13},{13,9},{2,6},{6,2},{1... | collective-permute-start | bytes 98312 | tf_op jit(solution)/shard_map/ppermute | solution.py:17
  16.6 0.9 %shard_map.103 = (f32[72,128]{1,0:T(8,128)S(1)}, f32[5,3,32,128]{3,2,1,0:T(8,128)S(1)}, f32[2,64,128]{2,1,0:T(8,128)S(1)}, f32[128,128]{1,0:T(8,128)S(1)}) custom-call(s32[12]{0:T(128)S(1)} %stack.60.flags.refs_0_, f32[208,128]{1,0:T(8,128)S(1)} %shard_map.101.first.refs_0_.a, f32[3,32,128]{2,1,0:T(8,128)S(1)} %get-tuple-element.37.detrain.refs_2_, ...), custom_call_target="tpu_custom_call" | custom-call | tf_op jit(solution)/shard_map/pallas_call | solution.py:657
  17.5 0.4 collective-permute-done.9.b
  17.9 0.9 %collective-permute-start.10 = (f32[344,128]{1,0:T(8,128)S(1)}, f32[344,128]{1,0:T(8,128)S(1)}, u32[]{:S(2)}, u32[]{:S(2)}) collective-permute-start(f32[344,128]{1,0:T(8,128)S(1)} %pad_maximum_fusion.a), channel_id=1, source_target_pairs={{0,3},{1,2},{2,1},{3,0},{4,7},{5,6},{6,5},{7,4},{8,11},{9,10},{10,... | collective-permute-start | bytes 528392 | tf_op jit(solution)/shard_map/ppermute | solution.py:17
  18.8 0.0 collective-permute-done.7
  18.8 0.0 collective-permute-done.6
  18.8 0.0 collective-permute-done.5
  18.8 2.0 %shard_map.105 = (f32[9,32,128]{2,1,0:T(8,128)S(1)}, f32[8,128]{1,0:T(8,128)S(1)}, f32[72,128]{1,0:T(8,128)S(1)}) custom-call(s32[12]{0:T(128)S(1)} %stack.60.flags.refs_0_, f32[16,16,128]{2,1,0:T(8,128)S(1)} %bitcast.15, f32[3,32,128]{2,1,0:T(8,128)S(1)} %get-tuple-element.37.detrain.refs_2_, f32[3,32,128]{2,1,0:T(8,128)S(1)} %get-tuple-element.34.mix.refs_3_, ...), custom_call_target="tpu_custom_call" | custom-call | flops 20000000000 | tf_op jit(solution)/shard_map/pallas_call | solution.py:657
  20.8 0.0 collective-permute-done.4.b
  20.9 0.5 %collective-permute-start.8 = (f32[208,128]{1,0:T(8,128)S(1)}, f32[208,128]{1,0:T(8,128)S(1)}, u32[]{:S(2)}, u32[]{:S(2)}) collective-permute-start(f32[208,128]{1,0:T(8,128)S(1)} %shard_map.106.mine.refs_0_), channel_id=1, source_target_pairs={{0,1},{1,0},{2,3},{3,2},{4,5},{5,4},{6,7},{7,6},{8,9},{9,8},{10,11... | collective-permute-start | bytes 319496 | tf_op jit(solution)/shard_map/ppermute | solution.py:17
  21.3 2.7 %collective-permute-start.14 = (f32[72,128]{1,0:T(8,128)S(1)}, f32[72,128]{1,0:T(8,128)S(1)}, u32[]{:S(2)}, u32[]{:S(2)}) collective-permute-start(f32[72,128]{1,0:T(8,128)S(1)} %get-tuple-element.48.refs_0_.forced_1), channel_id=1, source_target_pairs={{0,3},{1,2},{2,1},{3,0},{4,7},{5,6},{6,5},{7,4},{8,11},{9,10},{10,... | collective-permute-start | bytes 110600 | tf_op jit(solution)/shard_map/ppermute | solution.py:17
  24.0 0.5 %collective-permute-start.13 = (f32[72,128]{1,0:T(8,128)S(1)}, f32[72,128]{1,0:T(8,128)S(1)}, u32[]{:S(2)}, u32[]{:S(2)}) collective-permute-start(f32[72,128]{1,0:T(8,128)S(1)} %get-tuple-element.48.refs_0_.forced_1), channel_id=1, source_target_pairs={{0,2},{1,3},{2,0},{3,1},{4,6},{5,7},{6,4},{7,5},{8,10},{9,11},{10,... | collective-permute-start | bytes 110600 | tf_op jit(solution)/shard_map/ppermute | solution.py:17
  24.5 1.2 %collective-permute-start.12 = (f32[72,128]{1,0:T(8,128)S(1)}, f32[72,128]{1,0:T(8,128)S(1)}, u32[]{:S(2)}, u32[]{:S(2)}) collective-permute-start(f32[72,128]{1,0:T(8,128)S(1)} %get-tuple-element.48.refs_0_.forced_1), channel_id=1, source_target_pairs={{0,1},{1,0},{2,3},{3,2},{4,5},{5,4},{6,7},{7,6},{8,9},{9,8},{10,11... | collective-permute-start | bytes 110600 | tf_op jit(solution)/shard_map/ppermute | solution.py:17
  25.7 1.5 %collective-permute-done.10.b = f32[344,128]{1,0:T(8,128)S(1)} collective-permute-done((f32[344,128]{1,0:T(8,128)S(1)}, f32[344,128]{1,0:T(8,128)S(1)}, u32[]{:S(2)}, u32[]{:S(2)}) %collective-permute-start.10) | collective-permute-done | bytes 176160 | tf_op jit(solution)/shard_map/ppermute | solution.py:17
  27.2 2.7 %collective-permute-start.11 = (f32[344,128]{1,0:T(8,128)S(1)}, f32[344,128]{1,0:T(8,128)S(1)}, u32[]{:S(2)}, u32[]{:S(2)}) collective-permute-start(f32[344,128]{1,0:T(8,128)S(1)} %shard_map.110.mine), channel_id=1, source_target_pairs={{0,1},{1,0},{2,3},{3,2},{4,5},{5,4},{6,7},{7,6},{8,9},{9,8},{10,11... | collective-permute-start | bytes 528392 | tf_op jit(solution)/shard_map/ppermute | solution.py:17
  29.9 0.0 collective-permute-done.8.other
  29.9 1.2 %shard_map.107 = (f32[12,3,32,128]{3,2,1,0:T(8,128)S(1)}, f32[12,32,128]{2,1,0:T(8,128)S(1)}, f32[32,128]{1,0:T(8,128)S(1)}) custom-call(s32[12]{0:T(128)S(1)} %stack.60.flags.refs_0_, f32[12,3,32,128]{3,2,1,0:T(8,128)S(1)} %get-tuple-element.33.field, f32[3,32,128]{2,1,0:T(8,128)S(1)} %get-tuple-element.34.mix.refs_3_, ...), custom_call_target="tpu_custom_call" | custom-call | flops 20000000000 | tf_op jit(solution)/shard_map/pallas_call | solution.py:657
  31.0 0.0 collective-permute-done.14.forced_4
  31.1 0.0 collective-permute-done.13.forced_3
  31.1 0.0 collective-permute-done.12.forced_2
  31.1 3.2 %collective-permute-done.11.other = f32[344,128]{1,0:T(8,128)S(1)} collective-permute-done((f32[344,128]{1,0:T(8,128)S(1)}, f32[344,128]{1,0:T(8,128)S(1)}, u32[]{:S(2)}, u32[]{:S(2)}) %collective-permute-start.11) | collective-permute-done | bytes 176160 | tf_op jit(solution)/shard_map/ppermute | solution.py:17
  34.3 1.5 %shard_map.111 = (f32[12,3,32,128]{3,2,1,0:T(8,128)S(1)}, f32[40,128]{1,0:T(8,128)S(1)}, f32[40,128]{1,0:T(8,128)S(1)}, f32[24,128]{1,0:T(8,128)S(1)}) custom-call(s32[12]{0:T(128)S(1)} %stack.60.flags.refs_0_, f32[12,3,32,128]{3,2,1,0:T(8,128)S(1)} %get-tuple-element.49.moved, f32[12,32,128]{2,1,0:T(8,128)S(1)} %get-tuple-element.50.column, ...), custom_call_target="tpu_custom_call" | custom-call | tf_op jit(solution)/shard_map/pallas_call | solution.py:657
  35.8 0.0 collective-permute-start.15
  35.8 2.0 %collective-permute-start.16 = (f32[40,128]{1,0:T(8,128)S(1)}, f32[40,128]{1,0:T(8,128)S(1)}, u32[]{:S(2)}, u32[]{:S(2)}) collective-permute-start(f32[40,128]{1,0:T(8,128)S(1)} %get-tuple-element.59), channel_id=1, source_target_pairs={{0,16},{4,0},{8,4},{12,8},{28,12},{24,28},{20,24},{16,20},{1,17},{... | collective-permute-start | bytes 61448 | tf_op jit(solution)/shard_map/ppermute | solution.py:38
  37.8 0.0 collective-permute-start.17
  37.9 0.9 %shard_map.112.inner = f32[12,3,32,128]{3,2,1,0:T(8,128)S(1)} custom-call(s32[12]{0:T(128)S(1)} %stack.60.flags.refs_0_, f32[12,3,32,128]{3,2,1,0:T(8,128)S(1)} %get-tuple-element.57.mixed, f32[5,3,32,128]{3,2,1,0:T(8,128)S(1)} %get-tuple-element.45.refs_4_.coefs), custom_call_target="tpu_custom_call" | custom-call | tf_op jit(solution)/shard_map/pallas_call | solution.py:657
  38.8 2.7 %collective-permute-done.17.eastern.western = f32[24,128]{1,0:T(8,128)S(1)} collective-permute-done((f32[24,128]{1,0:T(8,128)S(1)}, f32[24,128]{1,0:T(8,128)S(1)}, u32[]{:S(2)}, u32[]{:S(2)}) %collective-permute-start.17) | collective-permute-done | bytes 12320 | tf_op jit(solution)/shard_map/ppermute | solution.py:17
  41.5 0.0 collective-permute-done.15.forward
  41.5 0.0 collective-permute-done.16.back
  41.5 1.6 %shard_map.113 = f32[12,3,32,128]{3,2,1,0:T(8,128)} custom-call(s32[12]{0:T(128)S(1)} %stack.60.flags.refs_0_, f32[12,3,32,128]{3,2,1,0:T(8,128)S(1)} %shard_map.112.inner, f32[5,3,32,128]{3,2,1,0:T(8,128)S(1)} %get-tuple-element.45.refs_4_.coefs, f32[40,128]{1,0:T(8,128)S(1)} %collective-permute-done.15.forward, ...), custom_call_target="tpu_custom_call" | custom-call | tf_op jit(solution)/shard_map/pallas_call | solution.py:657
  (11 shorter events, 0.2 us)
Async XLA Ops:
  2.0 10.0 %collective-permute-start = (f32[208,128]{1,0:T(8,128)S(1)}, f32[208,128]{1,0:T(8,128)S(1)}, u32[]{:S(2)}, u32[]{:S(2)}) collective-permute-start(f32[208,128]{1,0:T(8,128)S(1)} %get-tuple-element.36), channel_id=1, source_target_pairs={{0,1},{1,0},{2,3},{3,2},{4,5},{5,4},{6,7},{7,6},{8,9},{9,8},{10,11... | collective-permute-start | bytes 319496 | tf_op jit(solution)/shard_map/ppermute | solution.py:17
  6.1 8.7 %collective-permute-start.1 = (f32[64,128]{1,0:T(8,128)S(1)}, f32[64,128]{1,0:T(8,128)S(1)}, u32[]{:S(2)}, u32[]{:S(2)}) collective-permute-start(f32[64,128]{1,0:T(8,128)S(1)} %get-tuple-element.42.own_forward), channel_id=1, source_target_pairs={{0,4},{4,8},{8,12},{12,28},{28,24},{24,20},{20,16},{16,0},{1,5},{5... | collective-permute-start | bytes 98312 | tf_op jit(solution)/shard_map/ppermute | solution.py:37
  6.1 9.9 %collective-permute-start.2 = (f32[64,128]{1,0:T(8,128)S(1)}, f32[64,128]{1,0:T(8,128)S(1)}, u32[]{:S(2)}, u32[]{:S(2)}) collective-permute-start(f32[64,128]{1,0:T(8,128)S(1)} %get-tuple-element.43.own_back), channel_id=1, source_target_pairs={{0,16},{4,0},{8,4},{12,8},{28,12},{24,28},{20,24},{16,20},{1,17},{... | collective-permute-start | bytes 98312 | tf_op jit(solution)/shard_map/ppermute | solution.py:38
  8.1 3.9 %collective-permute-start.3 = (f32[64,128]{1,0:T(8,128)S(1)}, f32[64,128]{1,0:T(8,128)S(1)}, u32[]{:S(2)}, u32[]{:S(2)}) collective-permute-start(f32[64,128]{1,0:T(8,128)S(1)} %get-tuple-element.44.after), channel_id=1, source_target_pairs={{0,16},{16,0},{1,17},{17,1},{2,18},{18,2},{3,19},{19,3},{4,20},{20... | collective-permute-start | bytes 98312 | tf_op jit(solution)/shard_map/ppermute | solution.py:17
  9.2 8.7 %collective-permute-start.9 = (f32[272,128]{1,0:T(8,128)S(1)}, f32[272,128]{1,0:T(8,128)S(1)}, u32[]{:S(2)}, u32[]{:S(2)}) collective-permute-start(f32[272,128]{1,0:T(8,128)S(1)} %get-tuple-element.55), channel_id=1, source_target_pairs={{0,1},{1,0},{2,3},{3,2},{4,5},{5,4},{6,7},{7,6},{8,9},{9,8},{10,11... | collective-permute-start | bytes 417800 | tf_op jit(solution)/shard_map/ppermute | solution.py:17
  12.1 8.8 %collective-permute-start.4 = (f32[208,128]{1,0:T(8,128)S(1)}, f32[208,128]{1,0:T(8,128)S(1)}, u32[]{:S(2)}, u32[]{:S(2)}) collective-permute-start(f32[208,128]{1,0:T(8,128)S(1)} %shard_map.101.first.refs_0_.a), channel_id=1, source_target_pairs={{0,2},{1,3},{2,0},{3,1},{4,6},{5,7},{6,4},{7,5},{8,10},{9,11},{10,... | collective-permute-start | bytes 319496 | tf_op jit(solution)/shard_map/ppermute | solution.py:17
  14.7 4.1 %collective-permute-start.7 = (f32[2,32,128]{2,1,0:T(8,128)S(1)}, f32[2,32,128]{2,1,0:T(8,128)S(1)}, u32[]{:S(2)}, u32[]{:S(2)}) collective-permute-start(f32[2,32,128]{2,1,0:T(8,128)S(1)} %shard_map.104), channel_id=1, source_target_pairs={{0,12},{4,8},{8,4},{12,0},{1,13},{5,9},{9,5},{13,1},{2,14},{6,10},... | collective-permute-start | bytes 98312 | tf_op jit(solution)/shard_map/ppermute | solution.py:17
  14.7 4.1 %collective-permute-start.6 = (f32[2,32,128]{2,1,0:T(8,128)S(1)}, f32[2,32,128]{2,1,0:T(8,128)S(1)}, u32[]{:S(2)}, u32[]{:S(2)}) collective-permute-start(f32[2,32,128]{2,1,0:T(8,128)S(1)} %shard_map.104), channel_id=1, source_target_pairs={{0,8},{4,12},{8,0},{12,4},{1,9},{5,13},{9,1},{13,5},{2,10},{6,14},... | collective-permute-start | bytes 98312 | tf_op jit(solution)/shard_map/ppermute | solution.py:17
  16.0 2.8 %collective-permute-start.5 = (f32[2,32,128]{2,1,0:T(8,128)S(1)}, f32[2,32,128]{2,1,0:T(8,128)S(1)}, u32[]{:S(2)}, u32[]{:S(2)}) collective-permute-start(f32[2,32,128]{2,1,0:T(8,128)S(1)} %shard_map.104), channel_id=1, source_target_pairs={{0,4},{4,0},{8,12},{12,8},{1,5},{5,1},{9,13},{13,9},{2,6},{6,2},{1... | collective-permute-start | bytes 98312 | tf_op jit(solution)/shard_map/ppermute | solution.py:17
  17.9 9.3 %collective-permute-start.10 = (f32[344,128]{1,0:T(8,128)S(1)}, f32[344,128]{1,0:T(8,128)S(1)}, u32[]{:S(2)}, u32[]{:S(2)}) collective-permute-start(f32[344,128]{1,0:T(8,128)S(1)} %pad_maximum_fusion.a), channel_id=1, source_target_pairs={{0,3},{1,2},{2,1},{3,0},{4,7},{5,6},{6,5},{7,4},{8,11},{9,10},{10,... | collective-permute-start | bytes 528392 | tf_op jit(solution)/shard_map/ppermute | solution.py:17
  20.9 9.0 %collective-permute-start.8 = (f32[208,128]{1,0:T(8,128)S(1)}, f32[208,128]{1,0:T(8,128)S(1)}, u32[]{:S(2)}, u32[]{:S(2)}) collective-permute-start(f32[208,128]{1,0:T(8,128)S(1)} %shard_map.106.mine.refs_0_), channel_id=1, source_target_pairs={{0,1},{1,0},{2,3},{3,2},{4,5},{5,4},{6,7},{7,6},{8,9},{9,8},{10,11... | collective-permute-start | bytes 319496 | tf_op jit(solution)/shard_map/ppermute | solution.py:17
  21.3 9.7 %collective-permute-start.14 = (f32[72,128]{1,0:T(8,128)S(1)}, f32[72,128]{1,0:T(8,128)S(1)}, u32[]{:S(2)}, u32[]{:S(2)}) collective-permute-start(f32[72,128]{1,0:T(8,128)S(1)} %get-tuple-element.48.refs_0_.forced_1), channel_id=1, source_target_pairs={{0,3},{1,2},{2,1},{3,0},{4,7},{5,6},{6,5},{7,4},{8,11},{9,10},{10,... | collective-permute-start | bytes 110600 | tf_op jit(solution)/shard_map/ppermute | solution.py:17
  24.0 7.1 %collective-permute-start.13 = (f32[72,128]{1,0:T(8,128)S(1)}, f32[72,128]{1,0:T(8,128)S(1)}, u32[]{:S(2)}, u32[]{:S(2)}) collective-permute-start(f32[72,128]{1,0:T(8,128)S(1)} %get-tuple-element.48.refs_0_.forced_1), channel_id=1, source_target_pairs={{0,2},{1,3},{2,0},{3,1},{4,6},{5,7},{6,4},{7,5},{8,10},{9,11},{10,... | collective-permute-start | bytes 110600 | tf_op jit(solution)/shard_map/ppermute | solution.py:17
  24.5 6.6 %collective-permute-start.12 = (f32[72,128]{1,0:T(8,128)S(1)}, f32[72,128]{1,0:T(8,128)S(1)}, u32[]{:S(2)}, u32[]{:S(2)}) collective-permute-start(f32[72,128]{1,0:T(8,128)S(1)} %get-tuple-element.48.refs_0_.forced_1), channel_id=1, source_target_pairs={{0,1},{1,0},{2,3},{3,2},{4,5},{5,4},{6,7},{7,6},{8,9},{9,8},{10,11... | collective-permute-start | bytes 110600 | tf_op jit(solution)/shard_map/ppermute | solution.py:17
  27.2 7.1 %collective-permute-start.11 = (f32[344,128]{1,0:T(8,128)S(1)}, f32[344,128]{1,0:T(8,128)S(1)}, u32[]{:S(2)}, u32[]{:S(2)}) collective-permute-start(f32[344,128]{1,0:T(8,128)S(1)} %shard_map.110.mine), channel_id=1, source_target_pairs={{0,1},{1,0},{2,3},{3,2},{4,5},{5,4},{6,7},{7,6},{8,9},{9,8},{10,11... | collective-permute-start | bytes 528392 | tf_op jit(solution)/shard_map/ppermute | solution.py:17
  35.8 5.8 %collective-permute-start.15 = (f32[40,128]{1,0:T(8,128)S(1)}, f32[40,128]{1,0:T(8,128)S(1)}, u32[]{:S(2)}, u32[]{:S(2)}) collective-permute-start(f32[40,128]{1,0:T(8,128)S(1)} %get-tuple-element.58), channel_id=1, source_target_pairs={{0,4},{4,8},{8,12},{12,28},{28,24},{24,20},{20,16},{16,0},{1,5},{5... | collective-permute-start | bytes 61448 | tf_op jit(solution)/shard_map/ppermute | solution.py:37
  35.8 5.7 %collective-permute-start.16 = (f32[40,128]{1,0:T(8,128)S(1)}, f32[40,128]{1,0:T(8,128)S(1)}, u32[]{:S(2)}, u32[]{:S(2)}) collective-permute-start(f32[40,128]{1,0:T(8,128)S(1)} %get-tuple-element.59), channel_id=1, source_target_pairs={{0,16},{4,0},{8,4},{12,8},{28,12},{24,28},{20,24},{16,20},{1,17},{... | collective-permute-start | bytes 61448 | tf_op jit(solution)/shard_map/ppermute | solution.py:38
  37.8 3.7 %collective-permute-start.17 = (f32[24,128]{1,0:T(8,128)S(1)}, f32[24,128]{1,0:T(8,128)S(1)}, u32[]{:S(2)}, u32[]{:S(2)}) collective-permute-start(f32[24,128]{1,0:T(8,128)S(1)} %get-tuple-element.60), channel_id=1, source_target_pairs={{0,16},{16,0},{1,17},{17,1},{2,18},{18,2},{3,19},{19,3},{4,20},{20... | collective-permute-start | bytes 36872 | tf_op jit(solution)/shard_map/ppermute | solution.py:17

commit v6 on v5

--- a/solution.py
+++ b/solution.py
@@ -164,7 +164,7 @@
     pairs += [(field_in.at[t], field.at[t]) for t in range(tracers)]
     pairs += [(mix_in, mix), (east_in, east), (north_in, north), (pole_in, pole)]
     copies = [pltpu.make_async_copy(source, target, sems.at[i]) for i, (source, target) in enumerate(pairs)]
-    for copy in copies:
+    for copy in copies[4 : 5 + tracers] + copies[:4] + copies[5 + tracers :]:
         copy.start()
     half = tracers // 2
     slots[...] = jnp.zeros(slots.shape, F32)
@@ -777,7 +777,7 @@
         [(3 * levels, rows, lanes), (8, lanes), (2 * rows + 8, lanes)],
         weight=WEIGHTS[3],
     )
-    sums = [sums] + [swap_over(sums, "lev", bit) for bit in (1, 2, 3)]
+    sums = [sums] + [swap_over(sums, "lev", bit) for bit in (3, 2, 1)]
     first = add(first, other_first, sums[0])
     other_first = swap_over(first, "lev", 1)
     second = add(second, other_second, first)

time: 43.3 us -> 43.3 us (level)
  starting transfers between devices: 20.6 us -> 21.3 us
  waiting for transfers between devices: 10.3 us -> 9.62 us
    ppermute x14, starting transfers between devices: 16.5 us -> 17.2 us  [swap_over(): lax.ppermute(value, axis, [(i, i ^ bit) for i in range(lax.axis_size(axis...]
    ppermute x14, waiting for transfers between devices: 10.3 us -> 9.61 us  [swap_over(): lax.ppermute(value, axis, [(i, i ^ bit) for i in range(lax.axis_size(axis...]
where the time goes in v6:
time: 43.3 us; the launch traced here: 43.2 us
  starting transfers between devices  21.3 us (49%)
  Pallas kernels  11.9 us (27%)
  waiting for transfers between devices  9.62 us (22%)
    ppermute x14, starting transfers between devices, swap_over(): lax.ppermute(value, axis, [(i, i ^ bit) for i in range(lax.axis_size(axis...  17.2 us
    pallas_call x9, Pallas kernels, call(): pl.pallas_call(kernel, out_shape=[jax.ShapeDtypeStruct(shape, F32) for sh...  11.8 us
    ppermute x14, waiting for transfers between devices, swap_over(): lax.ppermute(value, axis, [(i, i ^ bit) for i in range(lax.axis_size(axis...  9.61 us
    ppermute x2, starting transfers between devices, exchange_rows(): lax.ppermute(back, ('lon', 'lat'), meridian_rings(lon_count, lat_count, -1))  4.03 us
  transfers between devices with their start and end apart: 18, of which 5 were waited for; matrix products, arithmetic and copies ran while one was open for 0% of the time, Pallas kernels for 16%

profile of v6, /device:TPU:0, one launch (start us, length us, event | category | flops | bytes accessed | tf_op | source)
XLA Modules:
  0.0 43.2 jit_solution(10233780874087852418)
XLA Ops:
  0.0 0.1 stack.60.flags.refs_0_
  0.1 1.9 %shard_map.100 = (f32[208,128]{1,0:T(8,128)S(1)}, f32[208,128]{1,0:T(8,128)S(1)}, f32[32,128]{1,0:T(8,128)S(1)}, f32[3,32,128]{2,1,0:T(8,128)S(1)}, f32[12,3,32,...) custom-call(s32[12]{0:T(128)S(1)} %stack.60.flags.refs_0_, ...), custom_call_target="tpu_custom_call" | custom-call | tf_op jit(solution)/shard_map/pallas_call | solution.py:657
  2.0 3.1 %collective-permute-start = (f32[208,128]{1,0:T(8,128)S(1)}, f32[208,128]{1,0:T(8,128)S(1)}, u32[]{:S(2)}, u32[]{:S(2)}) collective-permute-start(f32[208,128]{1,0:T(8,128)S(1)} %get-tuple-element.36), channel_id=1, source_target_pairs={{0,1},{1,0},{2,3},{3,2},{4,5},{5,4},{6,7},{7,6},{8,9},{9,8},{10,11... | collective-permute-start | bytes 319496 | tf_op jit(solution)/shard_map/ppermute | solution.py:17
  5.2 0.9 %shard_map.102 = (f32[64,128]{1,0:T(8,128)S(1)}, f32[64,128]{1,0:T(8,128)S(1)}, f32[64,128]{1,0:T(8,128)S(1)}) custom-call(s32[12]{0:T(128)S(1)} %stack.60.flags.refs_0_, f32[32,128]{1,0:T(8,128)S(1)} %get-tuple-element.41.slots, f32[12,3,32,128]{3,2,1,0:T(8,128)S(1)} %get-tuple-element.33.field, f32[12,3,32,128]{3,2,1,0:T(8,128)S(1)} %broadcast_multiply_fusion.kept, ...), custom_call_target="tpu_custom_call" | custom-call | tf_op jit(solution)/shard_map/pallas_call | solution.py:657
  6.1 0.0 collective-permute-start.1
  6.1 2.0 %collective-permute-start.2 = (f32[64,128]{1,0:T(8,128)S(1)}, f32[64,128]{1,0:T(8,128)S(1)}, u32[]{:S(2)}, u32[]{:S(2)}) collective-permute-start(f32[64,128]{1,0:T(8,128)S(1)} %get-tuple-element.43.own_back), channel_id=1, source_target_pairs={{0,16},{4,0},{8,4},{12,8},{28,12},{24,28},{20,24},{16,20},{1,17},{... | collective-permute-start | bytes 98312 | tf_op jit(solution)/shard_map/ppermute | solution.py:38
  8.1 0.0 collective-permute-start.3
  8.2 1.0 %shard_map.108 = (f32[272,128]{1,0:T(8,128)S(1)}, f32[272,128]{1,0:T(8,128)S(1)}) custom-call(s32[12]{0:T(128)S(1)} %stack.60.flags.refs_0_, f32[64,128]{1,0:T(8,128)S(1)} %get-tuple-element.44.after, f32[12,3,32,128]{3,2,1,0:T(8,128)S(1)} %get-tuple-element.33.field, f32[12,3,32,128]{3,2,1,0:T(8,128)S(1)} %broadcast_multiply_fusion.kept, ...), custom_call_target="tpu_custom_call" | custom-call | tf_op jit(solution)/shard_map/pallas_call | solution.py:657
  9.2 0.5 %collective-permute-start.9 = (f32[272,128]{1,0:T(8,128)S(1)}, f32[272,128]{1,0:T(8,128)S(1)}, u32[]{:S(2)}, u32[]{:S(2)}) collective-permute-start(f32[272,128]{1,0:T(8,128)S(1)} %get-tuple-element.55), channel_id=1, source_target_pairs={{0,1},{1,0},{2,3},{3,2},{4,5},{5,4},{6,7},{7,6},{8,9},{9,8},{10,11... | collective-permute-start | bytes 417800 | tf_op jit(solution)/shard_map/ppermute | solution.py:17
  9.6 2.4 %collective-permute-done.3 = f32[64,128]{1,0:T(8,128)S(1)} collective-permute-done((f32[64,128]{1,0:T(8,128)S(1)}, f32[64,128]{1,0:T(8,128)S(1)}, u32[]{:S(2)}, u32[]{:S(2)}) %collective-permute-start.3) | collective-permute-done | bytes 32800 | tf_op jit(solution)/shard_map/ppermute | solution.py:17
  12.0 0.0 collective-permute-done.b
  12.1 2.7 %collective-permute-start.4 = (f32[208,128]{1,0:T(8,128)S(1)}, f32[208,128]{1,0:T(8,128)S(1)}, u32[]{:S(2)}, u32[]{:S(2)}) collective-permute-start(f32[208,128]{1,0:T(8,128)S(1)} %shard_map.101.first.refs_0_.a), channel_id=1, source_target_pairs={{0,2},{1,3},{2,0},{3,1},{4,6},{5,7},{6,4},{7,5},{8,10},{9,11},{10,... | collective-permute-start | bytes 319496 | tf_op jit(solution)/shard_map/ppermute | solution.py:17
  14.7 0.0 collective-permute-start.7
  14.7 0.0 collective-permute-done.1.forward
  14.7 1.3 %collective-permute-start.6 = (f32[2,32,128]{2,1,0:T(8,128)S(1)}, f32[2,32,128]{2,1,0:T(8,128)S(1)}, u32[]{:S(2)}, u32[]{:S(2)}) collective-permute-start(f32[2,32,128]{2,1,0:T(8,128)S(1)} %shard_map.104), channel_id=1, source_target_pairs={{0,8},{4,12},{8,0},{12,4},{1,9},{5,13},{9,1},{13,5},{2,10},{6,14},... | collective-permute-start | bytes 98312 | tf_op jit(solution)/shard_map/ppermute | solution.py:17
  16.0 0.0 collective-permute-done.2.back
  16.0 0.6 %collective-permute-start.5 = (f32[2,32,128]{2,1,0:T(8,128)S(1)}, f32[2,32,128]{2,1,0:T(8,128)S(1)}, u32[]{:S(2)}, u32[]{:S(2)}) collective-permute-start(f32[2,32,128]{2,1,0:T(8,128)S(1)} %shard_map.104), channel_id=1, source_target_pairs={{0,4},{4,0},{8,12},{12,8},{1,5},{5,1},{9,13},{13,9},{2,6},{6,2},{1... | collective-permute-start | bytes 98312 | tf_op jit(solution)/shard_map/ppermute | solution.py:17
  16.6 0.9 %shard_map.103 = (f32[72,128]{1,0:T(8,128)S(1)}, f32[5,3,32,128]{3,2,1,0:T(8,128)S(1)}, f32[2,64,128]{2,1,0:T(8,128)S(1)}, f32[128,128]{1,0:T(8,128)S(1)}) custom-call(s32[12]{0:T(128)S(1)} %stack.60.flags.refs_0_, f32[208,128]{1,0:T(8,128)S(1)} %shard_map.101.first.refs_0_.a, f32[3,32,128]{2,1,0:T(8,128)S(1)} %get-tuple-element.37.detrain.refs_2_, ...), custom_call_target="tpu_custom_call" | custom-call | tf_op jit(solution)/shard_map/pallas_call | solution.py:657
  17.5 0.4 collective-permute-done.9.b
  17.9 0.9 %collective-permute-start.10 = (f32[344,128]{1,0:T(8,128)S(1)}, f32[344,128]{1,0:T(8,128)S(1)}, u32[]{:S(2)}, u32[]{:S(2)}) collective-permute-start(f32[344,128]{1,0:T(8,128)S(1)} %pad_maximum_fusion.a), channel_id=1, source_target_pairs={{0,3},{1,2},{2,1},{3,0},{4,7},{5,6},{6,5},{7,4},{8,11},{9,10},{10,... | collective-permute-start | bytes 528392 | tf_op jit(solution)/shard_map/ppermute | solution.py:17
  18.8 0.0 collective-permute-done.7
  18.8 0.0 collective-permute-done.6
  18.8 0.0 collective-permute-done.5
  18.8 2.0 %shard_map.105 = (f32[9,32,128]{2,1,0:T(8,128)S(1)}, f32[8,128]{1,0:T(8,128)S(1)}, f32[72,128]{1,0:T(8,128)S(1)}) custom-call(s32[12]{0:T(128)S(1)} %stack.60.flags.refs_0_, f32[16,16,128]{2,1,0:T(8,128)S(1)} %bitcast.15, f32[3,32,128]{2,1,0:T(8,128)S(1)} %get-tuple-element.37.detrain.refs_2_, f32[3,32,128]{2,1,0:T(8,128)S(1)} %get-tuple-element.34.mix.refs_3_, ...), custom_call_target="tpu_custom_call" | custom-call | flops 20000000000 | tf_op jit(solution)/shard_map/pallas_call | solution.py:657
  20.8 0.0 collective-permute-done.4.b
  20.9 0.5 %collective-permute-start.8 = (f32[208,128]{1,0:T(8,128)S(1)}, f32[208,128]{1,0:T(8,128)S(1)}, u32[]{:S(2)}, u32[]{:S(2)}) collective-permute-start(f32[208,128]{1,0:T(8,128)S(1)} %shard_map.106.mine.refs_0_), channel_id=1, source_target_pairs={{0,1},{1,0},{2,3},{3,2},{4,5},{5,4},{6,7},{7,6},{8,9},{9,8},{10,11... | collective-permute-start | bytes 319496 | tf_op jit(solution)/shard_map/ppermute | solution.py:17
  21.3 1.6 %collective-permute-start.14 = (f32[72,128]{1,0:T(8,128)S(1)}, f32[72,128]{1,0:T(8,128)S(1)}, u32[]{:S(2)}, u32[]{:S(2)}) collective-permute-start(f32[72,128]{1,0:T(8,128)S(1)} %get-tuple-element.48.refs_0_.forced_1), channel_id=1, source_target_pairs={{0,1},{1,0},{2,3},{3,2},{4,5},{5,4},{6,7},{7,6},{8,9},{9,8},{10,11... | collective-permute-start | bytes 110600 | tf_op jit(solution)/shard_map/ppermute | solution.py:17
  23.0 1.6 %collective-permute-start.13 = (f32[72,128]{1,0:T(8,128)S(1)}, f32[72,128]{1,0:T(8,128)S(1)}, u32[]{:S(2)}, u32[]{:S(2)}) collective-permute-start(f32[72,128]{1,0:T(8,128)S(1)} %get-tuple-element.48.refs_0_.forced_1), channel_id=1, source_target_pairs={{0,2},{1,3},{2,0},{3,1},{4,6},{5,7},{6,4},{7,5},{8,10},{9,11},{10,... | collective-permute-start | bytes 110600 | tf_op jit(solution)/shard_map/ppermute | solution.py:17
  24.6 1.4 %collective-permute-start.12 = (f32[72,128]{1,0:T(8,128)S(1)}, f32[72,128]{1,0:T(8,128)S(1)}, u32[]{:S(2)}, u32[]{:S(2)}) collective-permute-start(f32[72,128]{1,0:T(8,128)S(1)} %get-tuple-element.48.refs_0_.forced_1), channel_id=1, source_target_pairs={{0,3},{1,2},{2,1},{3,0},{4,7},{5,6},{6,5},{7,4},{8,11},{9,10},{10,... | collective-permute-start | bytes 110600 | tf_op jit(solution)/shard_map/ppermute | solution.py:17
  26.0 1.2 %collective-permute-done.10.b = f32[344,128]{1,0:T(8,128)S(1)} collective-permute-done((f32[344,128]{1,0:T(8,128)S(1)}, f32[344,128]{1,0:T(8,128)S(1)}, u32[]{:S(2)}, u32[]{:S(2)}) %collective-permute-start.10) | collective-permute-done | bytes 176160 | tf_op jit(solution)/shard_map/ppermute | solution.py:17
  27.2 2.7 %collective-permute-start.11 = (f32[344,128]{1,0:T(8,128)S(1)}, f32[344,128]{1,0:T(8,128)S(1)}, u32[]{:S(2)}, u32[]{:S(2)}) collective-permute-start(f32[344,128]{1,0:T(8,128)S(1)} %shard_map.110.mine), channel_id=1, source_target_pairs={{0,1},{1,0},{2,3},{3,2},{4,5},{5,4},{6,7},{7,6},{8,9},{9,8},{10,11... | collective-permute-start | bytes 528392 | tf_op jit(solution)/shard_map/ppermute | solution.py:17
  29.9 0.0 collective-permute-done.8.other
  29.9 1.2 %shard_map.107 = (f32[12,3,32,128]{3,2,1,0:T(8,128)S(1)}, f32[12,32,128]{2,1,0:T(8,128)S(1)}, f32[32,128]{1,0:T(8,128)S(1)}) custom-call(s32[12]{0:T(128)S(1)} %stack.60.flags.refs_0_, f32[12,3,32,128]{3,2,1,0:T(8,128)S(1)} %get-tuple-element.33.field, f32[3,32,128]{2,1,0:T(8,128)S(1)} %get-tuple-element.34.mix.refs_3_, ...), custom_call_target="tpu_custom_call" | custom-call | flops 20000000000 | tf_op jit(solution)/shard_map/pallas_call | solution.py:657
  31.0 0.0 collective-permute-done.14.forced_4
  31.1 0.0 collective-permute-done.13.forced_3
  31.1 0.0 collective-permute-done.12.forced_2
  31.1 3.2 %collective-permute-done.11.other = f32[344,128]{1,0:T(8,128)S(1)} collective-permute-done((f32[344,128]{1,0:T(8,128)S(1)}, f32[344,128]{1,0:T(8,128)S(1)}, u32[]{:S(2)}, u32[]{:S(2)}) %collective-permute-start.11) | collective-permute-done | bytes 176160 | tf_op jit(solution)/shard_map/ppermute | solution.py:17
  34.3 1.5 %shard_map.111 = (f32[12,3,32,128]{3,2,1,0:T(8,128)S(1)}, f32[40,128]{1,0:T(8,128)S(1)}, f32[40,128]{1,0:T(8,128)S(1)}, f32[24,128]{1,0:T(8,128)S(1)}) custom-call(s32[12]{0:T(128)S(1)} %stack.60.flags.refs_0_, f32[12,3,32,128]{3,2,1,0:T(8,128)S(1)} %get-tuple-element.49.moved, f32[12,32,128]{2,1,0:T(8,128)S(1)} %get-tuple-element.50.column, ...), custom_call_target="tpu_custom_call" | custom-call | tf_op jit(solution)/shard_map/pallas_call | solution.py:657
  35.8 0.0 collective-permute-start.15
  35.8 2.0 %collective-permute-start.16 = (f32[40,128]{1,0:T(8,128)S(1)}, f32[40,128]{1,0:T(8,128)S(1)}, u32[]{:S(2)}, u32[]{:S(2)}) collective-permute-start(f32[40,128]{1,0:T(8,128)S(1)} %get-tuple-element.59), channel_id=1, source_target_pairs={{0,16},{4,0},{8,4},{12,8},{28,12},{24,28},{20,24},{16,20},{1,17},{... | collective-permute-start | bytes 61448 | tf_op jit(solution)/shard_map/ppermute | solution.py:38
  37.8 0.4 collective-permute-start.17
  38.2 0.9 %shard_map.112.inner = f32[12,3,32,128]{3,2,1,0:T(8,128)S(1)} custom-call(s32[12]{0:T(128)S(1)} %stack.60.flags.refs_0_, f32[12,3,32,128]{3,2,1,0:T(8,128)S(1)} %get-tuple-element.57.mixed, f32[5,3,32,128]{3,2,1,0:T(8,128)S(1)} %get-tuple-element.45.refs_4_.coefs), custom_call_target="tpu_custom_call" | custom-call | tf_op jit(solution)/shard_map/pallas_call | solution.py:657
  39.2 2.4 %collective-permute-done.17.eastern.western = f32[24,128]{1,0:T(8,128)S(1)} collective-permute-done((f32[24,128]{1,0:T(8,128)S(1)}, f32[24,128]{1,0:T(8,128)S(1)}, u32[]{:S(2)}, u32[]{:S(2)}) %collective-permute-start.17) | collective-permute-done | bytes 12320 | tf_op jit(solution)/shard_map/ppermute | solution.py:17
  41.5 0.0 collective-permute-done.15.forward
  41.5 0.0 collective-permute-done.16.back
  41.5 1.6 %shard_map.113 = f32[12,3,32,128]{3,2,1,0:T(8,128)} custom-call(s32[12]{0:T(128)S(1)} %stack.60.flags.refs_0_, f32[12,3,32,128]{3,2,1,0:T(8,128)S(1)} %shard_map.112.inner, f32[5,3,32,128]{3,2,1,0:T(8,128)S(1)} %get-tuple-element.45.refs_4_.coefs, f32[40,128]{1,0:T(8,128)S(1)} %collective-permute-done.15.forward, ...), custom_call_target="tpu_custom_call" | custom-call | tf_op jit(solution)/shard_map/pallas_call | solution.py:657
  (11 shorter events, 0.2 us)
Async XLA Ops:
  2.0 10.0 %collective-permute-start = (f32[208,128]{1,0:T(8,128)S(1)}, f32[208,128]{1,0:T(8,128)S(1)}, u32[]{:S(2)}, u32[]{:S(2)}) collective-permute-start(f32[208,128]{1,0:T(8,128)S(1)} %get-tuple-element.36), channel_id=1, source_target_pairs={{0,1},{1,0},{2,3},{3,2},{4,5},{5,4},{6,7},{7,6},{8,9},{9,8},{10,11... | collective-permute-start | bytes 319496 | tf_op jit(solution)/shard_map/ppermute | solution.py:17
  6.1 8.7 %collective-permute-start.1 = (f32[64,128]{1,0:T(8,128)S(1)}, f32[64,128]{1,0:T(8,128)S(1)}, u32[]{:S(2)}, u32[]{:S(2)}) collective-permute-start(f32[64,128]{1,0:T(8,128)S(1)} %get-tuple-element.42.own_forward), channel_id=1, source_target_pairs={{0,4},{4,8},{8,12},{12,28},{28,24},{24,20},{20,16},{16,0},{1,5},{5... | collective-permute-start | bytes 98312 | tf_op jit(solution)/shard_map/ppermute | solution.py:37
  6.1 9.9 %collective-permute-start.2 = (f32[64,128]{1,0:T(8,128)S(1)}, f32[64,128]{1,0:T(8,128)S(1)}, u32[]{:S(2)}, u32[]{:S(2)}) collective-permute-start(f32[64,128]{1,0:T(8,128)S(1)} %get-tuple-element.43.own_back), channel_id=1, source_target_pairs={{0,16},{4,0},{8,4},{12,8},{28,12},{24,28},{20,24},{16,20},{1,17},{... | collective-permute-start | bytes 98312 | tf_op jit(solution)/shard_map/ppermute | solution.py:38
  8.1 3.9 %collective-permute-start.3 = (f32[64,128]{1,0:T(8,128)S(1)}, f32[64,128]{1,0:T(8,128)S(1)}, u32[]{:S(2)}, u32[]{:S(2)}) collective-permute-start(f32[64,128]{1,0:T(8,128)S(1)} %get-tuple-element.44.after), channel_id=1, source_target_pairs={{0,16},{16,0},{1,17},{17,1},{2,18},{18,2},{3,19},{19,3},{4,20},{20... | collective-permute-start | bytes 98312 | tf_op jit(solution)/shard_map/ppermute | solution.py:17
  9.2 8.7 %collective-permute-start.9 = (f32[272,128]{1,0:T(8,128)S(1)}, f32[272,128]{1,0:T(8,128)S(1)}, u32[]{:S(2)}, u32[]{:S(2)}) collective-permute-start(f32[272,128]{1,0:T(8,128)S(1)} %get-tuple-element.55), channel_id=1, source_target_pairs={{0,1},{1,0},{2,3},{3,2},{4,5},{5,4},{6,7},{7,6},{8,9},{9,8},{10,11... | collective-permute-start | bytes 417800 | tf_op jit(solution)/shard_map/ppermute | solution.py:17
  12.1 8.8 %collective-permute-start.4 = (f32[208,128]{1,0:T(8,128)S(1)}, f32[208,128]{1,0:T(8,128)S(1)}, u32[]{:S(2)}, u32[]{:S(2)}) collective-permute-start(f32[208,128]{1,0:T(8,128)S(1)} %shard_map.101.first.refs_0_.a), channel_id=1, source_target_pairs={{0,2},{1,3},{2,0},{3,1},{4,6},{5,7},{6,4},{7,5},{8,10},{9,11},{10,... | collective-permute-start | bytes 319496 | tf_op jit(solution)/shard_map/ppermute | solution.py:17
  14.7 4.1 %collective-permute-start.7 = (f32[2,32,128]{2,1,0:T(8,128)S(1)}, f32[2,32,128]{2,1,0:T(8,128)S(1)}, u32[]{:S(2)}, u32[]{:S(2)}) collective-permute-start(f32[2,32,128]{2,1,0:T(8,128)S(1)} %shard_map.104), channel_id=1, source_target_pairs={{0,12},{4,8},{8,4},{12,0},{1,13},{5,9},{9,5},{13,1},{2,14},{6,10},... | collective-permute-start | bytes 98312 | tf_op jit(solution)/shard_map/ppermute | solution.py:17
  14.7 4.1 %collective-permute-start.6 = (f32[2,32,128]{2,1,0:T(8,128)S(1)}, f32[2,32,128]{2,1,0:T(8,128)S(1)}, u32[]{:S(2)}, u32[]{:S(2)}) collective-permute-start(f32[2,32,128]{2,1,0:T(8,128)S(1)} %shard_map.104), channel_id=1, source_target_pairs={{0,8},{4,12},{8,0},{12,4},{1,9},{5,13},{9,1},{13,5},{2,10},{6,14},... | collective-permute-start | bytes 98312 | tf_op jit(solution)/shard_map/ppermute | solution.py:17
  16.0 2.8 %collective-permute-start.5 = (f32[2,32,128]{2,1,0:T(8,128)S(1)}, f32[2,32,128]{2,1,0:T(8,128)S(1)}, u32[]{:S(2)}, u32[]{:S(2)}) collective-permute-start(f32[2,32,128]{2,1,0:T(8,128)S(1)} %shard_map.104), channel_id=1, source_target_pairs={{0,4},{4,0},{8,12},{12,8},{1,5},{5,1},{9,13},{13,9},{2,6},{6,2},{1... | collective-permute-start | bytes 98312 | tf_op jit(solution)/shard_map/ppermute | solution.py:17
  17.9 9.2 %collective-permute-start.10 = (f32[344,128]{1,0:T(8,128)S(1)}, f32[344,128]{1,0:T(8,128)S(1)}, u32[]{:S(2)}, u32[]{:S(2)}) collective-permute-start(f32[344,128]{1,0:T(8,128)S(1)} %pad_maximum_fusion.a), channel_id=1, source_target_pairs={{0,3},{1,2},{2,1},{3,0},{4,7},{5,6},{6,5},{7,4},{8,11},{9,10},{10,... | collective-permute-start | bytes 528392 | tf_op jit(solution)/shard_map/ppermute | solution.py:17
  20.9 9.0 %collective-permute-start.8 = (f32[208,128]{1,0:T(8,128)S(1)}, f32[208,128]{1,0:T(8,128)S(1)}, u32[]{:S(2)}, u32[]{:S(2)}) collective-permute-start(f32[208,128]{1,0:T(8,128)S(1)} %shard_map.106.mine.refs_0_), channel_id=1, source_target_pairs={{0,1},{1,0},{2,3},{3,2},{4,5},{5,4},{6,7},{7,6},{8,9},{9,8},{10,11... | collective-permute-start | bytes 319496 | tf_op jit(solution)/shard_map/ppermute | solution.py:17
  21.3 9.7 %collective-permute-start.14 = (f32[72,128]{1,0:T(8,128)S(1)}, f32[72,128]{1,0:T(8,128)S(1)}, u32[]{:S(2)}, u32[]{:S(2)}) collective-permute-start(f32[72,128]{1,0:T(8,128)S(1)} %get-tuple-element.48.refs_0_.forced_1), channel_id=1, source_target_pairs={{0,1},{1,0},{2,3},{3,2},{4,5},{5,4},{6,7},{7,6},{8,9},{9,8},{10,11... | collective-permute-start | bytes 110600 | tf_op jit(solution)/shard_map/ppermute | solution.py:17
  23.0 8.1 %collective-permute-start.13 = (f32[72,128]{1,0:T(8,128)S(1)}, f32[72,128]{1,0:T(8,128)S(1)}, u32[]{:S(2)}, u32[]{:S(2)}) collective-permute-start(f32[72,128]{1,0:T(8,128)S(1)} %get-tuple-element.48.refs_0_.forced_1), channel_id=1, source_target_pairs={{0,2},{1,3},{2,0},{3,1},{4,6},{5,7},{6,4},{7,5},{8,10},{9,11},{10,... | collective-permute-start | bytes 110600 | tf_op jit(solution)/shard_map/ppermute | solution.py:17
  24.6 6.5 %collective-permute-start.12 = (f32[72,128]{1,0:T(8,128)S(1)}, f32[72,128]{1,0:T(8,128)S(1)}, u32[]{:S(2)}, u32[]{:S(2)}) collective-permute-start(f32[72,128]{1,0:T(8,128)S(1)} %get-tuple-element.48.refs_0_.forced_1), channel_id=1, source_target_pairs={{0,3},{1,2},{2,1},{3,0},{4,7},{5,6},{6,5},{7,4},{8,11},{9,10},{10,... | collective-permute-start | bytes 110600 | tf_op jit(solution)/shard_map/ppermute | solution.py:17
  27.2 7.1 %collective-permute-start.11 = (f32[344,128]{1,0:T(8,128)S(1)}, f32[344,128]{1,0:T(8,128)S(1)}, u32[]{:S(2)}, u32[]{:S(2)}) collective-permute-start(f32[344,128]{1,0:T(8,128)S(1)} %shard_map.110.mine), channel_id=1, source_target_pairs={{0,1},{1,0},{2,3},{3,2},{4,5},{5,4},{6,7},{7,6},{8,9},{9,8},{10,11... | collective-permute-start | bytes 528392 | tf_op jit(solution)/shard_map/ppermute | solution.py:17
  35.8 5.8 %collective-permute-start.15 = (f32[40,128]{1,0:T(8,128)S(1)}, f32[40,128]{1,0:T(8,128)S(1)}, u32[]{:S(2)}, u32[]{:S(2)}) collective-permute-start(f32[40,128]{1,0:T(8,128)S(1)} %get-tuple-element.58), channel_id=1, source_target_pairs={{0,4},{4,8},{8,12},{12,28},{28,24},{24,20},{20,16},{16,0},{1,5},{5... | collective-permute-start | bytes 61448 | tf_op jit(solution)/shard_map/ppermute | solution.py:37
  35.8 5.7 %collective-permute-start.16 = (f32[40,128]{1,0:T(8,128)S(1)}, f32[40,128]{1,0:T(8,128)S(1)}, u32[]{:S(2)}, u32[]{:S(2)}) collective-permute-start(f32[40,128]{1,0:T(8,128)S(1)} %get-tuple-element.59), channel_id=1, source_target_pairs={{0,16},{4,0},{8,4},{12,8},{28,12},{24,28},{20,24},{16,20},{1,17},{... | collective-permute-start | bytes 61448 | tf_op jit(solution)/shard_map/ppermute | solution.py:38
  37.8 3.7 %collective-permute-start.17 = (f32[24,128]{1,0:T(8,128)S(1)}, f32[24,128]{1,0:T(8,128)S(1)}, u32[]{:S(2)}, u32[]{:S(2)}) collective-permute-start(f32[24,128]{1,0:T(8,128)S(1)} %get-tuple-element.60), channel_id=1, source_target_pairs={{0,16},{16,0},{1,17},{17,1},{2,18},{18,2},{3,19},{19,3},{4,20},{20... | collective-permute-start | bytes 36872 | tf_op jit(solution)/shard_map/ppermute | solution.py:17
